TPU v7x, 32 devices: a whole 2x2x4 slice. The times are simulated.
32 devices in a mesh: row: 8 (over z, x), col: 4 (over y, core).
Axes of the slice: x: 2, y: 2, z: 4, core: 2. Of those that a mesh axis runs over, the one named last changes fastest.
Arguments:
- residual: bfloat16 [1024, 7168], P('col', 'row'), may hold values from -30 to 30
- attn_gain: float32 [7168], P('row'), may hold values from 0.25 to 1.75
- w_query: bfloat16 [7168, 7168], P('row', 'col'), may hold values from -1 to 1
- w_key: bfloat16 [7168, 1024], P('row', 'col'), may hold values from -11 to 11
- value_weight: bfloat16 [7168, 1024], P('row', 'col'), may hold values from -0.0625 to 0.0625
- w_out: bfloat16 [7168, 7168], P('col', 'row'), may hold values from -0.0625 to 0.0625
- mlp_gain: float32 [7168], P('col'), may hold values from 0.25 to 1.75
- w_gate: bfloat16 [7168, 20480], P('col', 'row'), may hold values from -0.0625 to 0.0625
- w_up: bfloat16 [7168, 20480], P('col', 'row'), may hold values from -0.0625 to 0.0625
- w_down: bfloat16 [20480, 7168], P('row', 'col'), may hold values from -0.0390625 to 0.0390625
- segment_ids: int32 [1024], replicated, may hold values from 0 to 7, never falling along the last dimension, each value on 1 to 512 neighbouring positions
- page_table: int32 [64], replicated, may hold values from 0 to 63, each once
Outputs:
- output: bfloat16 [1024, 7168], P('row', 'col')
- key_cache_pages: bfloat16 [64, 16, 1024], P('row', None, 'col')
- value_cache_pages: bfloat16 [64, 16, 1024], P('row', None, 'col')
Inputs may be any that keep to these rules, and one draw needn't show every extreme that they name: `segment_ids`: document numbers never fall along the stream; each of the 8 documents holds 1 to 512 tokens and one holds exactly 512. A permutation: the tokens b * 16 to b * 16 + 15 go to cache slot page_table[b].
All inputs are finite; a program needn't handle non-finite values.
Results may differ from a plain program's by a relative error of at most 0.035.
Values may be sent and summed in bfloat16 or wider, within the bound.
No kernel may reach another device: no remote copies, remote signals or barrier semaphores. Data moves between devices by JAX's collectives and lax.ppermute only.
A program may use at most 128 MiB of HBM per device.

v0:
```python
import jax
import jax.numpy as jnp
from jax import lax
from jax.sharding import PartitionSpec as P

HEAD_SIZE = 128
ROPE_BASE = 5000000.0
EPSILON = 1e-05
NEGATIVE = -1e30
PARTS = 2


def quotient(value, size):
    if size & (size - 1):
        return lax.div(value, jnp.int32(size))
    return lax.shift_right_logical(value, jnp.int32(size.bit_length() - 1)) if size > 1 else value


def remainder(value, size):
    if size & (size - 1):
        return lax.rem(value, jnp.int32(size))
    return jnp.bitwise_and(value, jnp.int32(size - 1))


def cut_from(block, start, sizes):
    return lax.dynamic_slice(block, start, sizes, allow_negative_indices=False)


class RowWalk:
    def __init__(self, rows):
        self.depth = 4 if rows % 4 == 0 else 1
        self.width = rows // self.depth
        self.rows = rows

    def turned(self, x, z):
        if self.depth & (self.depth - 1) == 0 and self.width == 2:
            return jnp.bitwise_xor(z, x * (self.depth - 1))
        return jnp.where(remainder(x, 2) == 1, self.depth - 1 - z, z)

    def row_at(self, spot):
        x = quotient(spot, self.depth)
        return self.turned(x, remainder(spot, self.depth)) * self.width + x

    def spot_of(self, row):
        x = remainder(row, self.width)
        return x * self.depth + self.turned(x, quotient(row, self.width))

    def listed(self):
        walk = []
        for x in range(self.width):
            zs = range(self.depth) if x % 2 == 0 else reversed(range(self.depth))
            walk += [z * self.width + x for z in zs]
        return walk


class Ring:
    def __init__(self, axis, walks, spot):
        self.axis = axis
        self.size = n = len(walks[0])
        self.right = [(w[i], w[(i + 1) % n]) for w in walks for i in range(n)]
        self.left = [(w[(i + 1) % n], w[i]) for w in walks for i in range(n)]
        self.spot = spot

    def send(self, block, pairs):
        return lax.ppermute(block, self.axis, pairs)

    def at(self, offset):
        return remainder(self.spot + offset % self.size, self.size) if offset % self.size else self.spot

    def reduce_scatter(self, take):
        n, half = self.size, self.size // 2
        if n == 1:
            return take(0).astype(jnp.float32)
        if n == 2:
            got = self.send(take(1).astype(jnp.bfloat16), self.right)
            return take(0).astype(jnp.float32) + got.astype(jnp.float32)
        far = take(half).astype(jnp.bfloat16)
        cut = far.shape[0] // 2
        going_right = self.send(far[:cut], self.right).astype(jnp.float32)
        going_left = self.send(far[cut:], self.left).astype(jnp.float32)
        for step in range(half - 1, 0, -1):
            one = take(step).astype(jnp.float32)
            two = take(-step).astype(jnp.float32)
            if step == half - 1:
                one = jnp.concatenate([one[:cut] + going_right, one[cut:]], axis=0)
                two = jnp.concatenate([two[:cut], two[cut:] + going_left], axis=0)
            else:
                one = one + going_right
                two = two + going_left
            going_right = self.send(one.astype(jnp.bfloat16), self.right).astype(jnp.float32)
            going_left = self.send(two.astype(jnp.bfloat16), self.left).astype(jnp.float32)
        return take(0).astype(jnp.float32) + going_right + going_left

    def all_gather(self, block):
        n, half = self.size, self.size // 2
        if n == 1:
            return [(0, block)]
        if n == 2:
            return [(0, block), (1, self.send(block, self.right))]
        found = [(0, block)]
        from_left = from_right = block
        for step in range(1, half):
            from_left = self.send(from_left, self.right)
            from_right = self.send(from_right, self.left)
            found += [(-step, from_left), (step, from_right)]
        cut = block.shape[0] // 2
        far = jnp.concatenate(
            [self.send(from_left[:cut], self.right), self.send(from_right[cut:], self.left)], axis=0
        )
        return found + [(half, far)]


def place_blocks(shape, dtype, placed):
    buffer = jnp.zeros(shape, dtype)
    for start, block in placed:
        buffer = lax.dynamic_update_slice(buffer, block, start, allow_negative_indices=False)
    return buffer


def tie(block, *earlier):
    return lax.optimization_barrier((block, *earlier))[0]


def rotary_tables(token_positions):
    half_width = HEAD_SIZE // 2
    frequency = ROPE_BASE ** (-2.0 * jnp.arange(half_width, dtype=jnp.float32) / HEAD_SIZE)
    angles = token_positions.astype(jnp.float32)[:, None] * frequency[None, :]
    return jnp.cos(angles)[:, None, :], jnp.sin(angles)[:, None, :]


def rotary_apply(block, tables):
    cosine, sine_part = tables
    half_width = block.shape[-1] // 2
    first_half = block[..., :half_width]
    second = block[..., half_width:]
    return jnp.concatenate(
        [first_half * cosine - second * sine_part, second * cosine + first_half * sine_part],
        axis=-1,
    )


def dot32(a, b):
    return jnp.dot(a, b, preferred_element_type=jnp.float32)


def per_device(
    residual,
    attn_gain,
    w_query,
    w_key,
    value_weight,
    w_out,
    mlp_gain,
    w_gate,
    w_up,
    w_down,
    segment_ids,
    page_table,
):
    rows, cols = lax.axis_size("row"), lax.axis_size("col")
    row_place, col_place = lax.axis_index("row"), lax.axis_index("col")
    lanes = cols // 2
    lane, core = quotient(col_place, 2), remainder(col_place, 2)
    walk = RowWalk(rows)
    row_ring = Ring("row", [walk.listed()], walk.spot_of(row_place))
    lane_ring = Ring("col", [[i * 2 + c for i in range(lanes)] for c in range(2)], lane)
    row_at = [row_place] + [walk.row_at(row_ring.at(i)) for i in range(1, rows)]
    swap = [(i, i ^ 1) for i in range(cols)]

    def other_core(block):
        return lax.ppermute(block, "col", swap)

    tokens = segment_ids.shape[0]
    row_tokens, col_tokens = tokens // rows, tokens // cols
    part_tokens = tokens // PARTS
    row_part, col_part = row_tokens // PARTS, col_tokens // PARTS
    per_col = rows // cols
    row_width = residual.shape[1]
    model_width = row_width * rows
    query_cols, kv_cols = w_query.shape[1], w_key.shape[1]
    kv_local = kv_cols // HEAD_SIZE
    heads = query_cols // HEAD_SIZE
    group = heads // kv_local
    first_row = row_place * row_tokens

    def slot_of_row(who, m):
        if lanes <= 2 and per_col & (per_col - 1) == 0:
            return jnp.bitwise_xor(who, col_place * per_col) * m
        at_col = quotient(who, per_col)
        step = remainder(quotient(at_col, 2) - lane + lanes, lanes)
        side = jnp.bitwise_xor(remainder(at_col, 2), core)
        return ((step * 2 + side) * per_col + remainder(who, per_col)) * m

    def gather_cols(block, send_after=()):
        near = other_core(block)
        found = sorted(lane_ring.all_gather(tie(block, *send_after) if send_after else block), key=lambda f: f[0] % lanes)
        pieces = [block, near]
        for _, b in found[1:]:
            pieces += [b, other_core(b)]
        return jnp.concatenate(pieces, axis=0), found[-1][1]

    def core_sum(block):
        m, w = block.shape[0] // cols, block.shape[1]
        split = block.reshape(lanes, 2, m, w)
        got = other_core(split[:, 1])
        return (split[:, 0].astype(jnp.float32) + got.astype(jnp.float32)).astype(jnp.bfloat16)

    def lane_sum(summed):
        return lane_ring.reduce_scatter(lambda i: summed[i % lanes])

    def row_blocks(block, m):
        def take(i):
            start = slot_of_row(row_at[i], m)
            return cut_from(block, (start, 0), (m, block.shape[1]))

        return take

    def gather_rows(block, along, start_of, first_after=()):
        m, w = block.shape
        shape = (rows * m, w) if along == 0 else (m, rows * w)
        placed = []
        found = row_ring.all_gather(tie(block, *first_after) if first_after else block)
        for i, b in found:
            begin = start_of(row_at[i])
            placed.append(((begin, 0) if along == 0 else (0, begin), b))
        late = tuple(b for _, b in found[-3:-1])
        return place_blocks(shape, block.dtype, placed), late

    gathered, _ = gather_cols(residual)
    widened = gathered.astype(jnp.float32)
    scaled = (widened * attn_gain[None, :]).astype(jnp.bfloat16)
    sums = jnp.sum(widened * widened, axis=1)

    kv_terms = jnp.concatenate([dot32(scaled, w_key), dot32(scaled, value_weight)], axis=1)
    kv_terms = kv_terms.astype(jnp.bfloat16)

    late_ids, late_pages, sums = lax.optimization_barrier((segment_ids, page_table, sums, kv_terms))[:3]
    query_index = first_row + jnp.arange(row_tokens, dtype=jnp.int32)
    own_segment = cut_from(late_ids, (first_row,), (row_tokens,))
    seg_starts = jnp.sum((late_ids[None, :] < own_segment[:, None]).astype(jnp.int32), axis=1)
    tables = rotary_tables(query_index - seg_starts)
    key_rows = walk.row_at(remainder(row_ring.spot + jnp.arange(rows, dtype=jnp.int32), rows))
    key_index = key_rows[:, None] * row_tokens + jnp.arange(row_tokens, dtype=jnp.int32)[None, :]
    key_index = key_index.reshape(tokens)
    key_segment = jnp.sum(
        jnp.where(
            key_rows[:, None, None] == jnp.arange(rows, dtype=jnp.int32)[None, :, None],
            late_ids.reshape(1, rows, row_tokens),
            0,
        ),
        axis=1,
    ).reshape(tokens)
    bit = 1
    while bit < rows:
        sums = sums + lax.ppermute(sums, "row", [(i, i ^ bit) for i in range(rows)])
        bit *= 2
    attn_scale = lax.rsqrt(
        cut_from(sums, (slot_of_row(row_place, row_tokens),), (row_tokens,)) / model_width
        + EPSILON
    )[:, None]

    query_terms = dot32(scaled, w_query).astype(jnp.bfloat16)
    kv_own = row_ring.reduce_scatter(row_blocks(kv_terms, row_tokens)) * attn_scale
    key_own = rotary_apply(kv_own[:, :kv_cols].reshape(row_tokens, kv_local, HEAD_SIZE), tables)
    key_value = jnp.concatenate([key_own.reshape(row_tokens, kv_cols), kv_own[:, kv_cols:]], axis=1)
    found = row_ring.all_gather(key_value.astype(jnp.bfloat16))
    key_value = jnp.concatenate([b for _, b in sorted(found, key=lambda f: f[0] % rows)], axis=0)
    key_all, value_all = key_value[:, :kv_cols], key_value[:, kv_cols:]
    key_heads = key_all.reshape(tokens, kv_local, HEAD_SIZE)
    value_heads = value_all.reshape(tokens, kv_local, HEAD_SIZE)

    queries = row_ring.reduce_scatter(row_blocks(query_terms, row_tokens)) * attn_scale
    queries = rotary_apply(queries.reshape(row_tokens, heads, HEAD_SIZE), tables)
    queries = queries.astype(jnp.bfloat16)

    def attend(part):
        own = slice(part * row_part, (part + 1) * row_part)
        key_mask = (
            (key_segment[None, :] == own_segment[own][:, None])
            & (key_index[None, :] <= query_index[own][:, None])
        )[None, None]
        scores = jnp.where(
            key_mask,
            jnp.einsum(
                "tjgd,sjd->jgts",
                queries[own].reshape(row_part, kv_local, group, HEAD_SIZE),
                key_heads,
                preferred_element_type=jnp.float32,
            )
            * HEAD_SIZE ** (-0.5),
            NEGATIVE,
        )
        peak_score = jnp.max(scores, axis=3, keepdims=True)
        weights = jnp.where(key_mask, jnp.exp(scores - peak_score), 0.0).astype(jnp.bfloat16)
        weight_sum = jnp.sum(weights.astype(jnp.float32), axis=3)
        mixture = jnp.einsum(
            "jgts,sjd->jgtd", weights, value_heads, preferred_element_type=jnp.float32
        )
        return (
            jnp.transpose(mixture / weight_sum[..., None], (2, 0, 1, 3))
            .reshape(row_part, query_cols)
            .astype(jnp.bfloat16)
        )

    def project(part, attended):
        attn_out = lane_sum(core_sum(dot32(attended, w_out).astype(jnp.bfloat16)))
        own = residual.reshape(per_col, PARTS, row_part, row_width)[:, part]
        own = own.reshape(col_part, row_width)
        return (own.astype(jnp.float32) + attn_out).astype(jnp.bfloat16)

    def spread(full_rows, before_core=()):
        w = model_width // cols
        span = 2 * w
        mine = [(0, cut_from(full_rows, (0, lane * span), (col_part, span)))]
        for hop in range(1, lanes):
            pairs = [
                (i * 2 + c, ((i + hop) % lanes) * 2 + c) for i in range(lanes) for c in range(2)
            ]
            sent = cut_from(full_rows, (0, lane_ring.at(hop) * span), (col_part, span))
            mine.append((-hop % lanes, lax.ppermute(sent, "col", pairs)))
        pieces = []
        for hop, b in sorted(mine, key=lambda f: f[0]):
            sent = cut_from(b, (0, (1 - core) * w), (col_part, w))
            if hop and before_core:
                sent = tie(sent, *before_core)
            pieces += [cut_from(b, (0, core * w), (col_part, w)), other_core(sent)]
        return jnp.concatenate(pieces, axis=0)

    def mlp_scale(full_rows):
        full32 = full_rows.astype(jnp.float32)
        return lax.rsqrt(jnp.sum(full32 * full32, axis=1) / model_width + EPSILON)[:, None]

    def widen(stream):
        mid = (stream.astype(jnp.float32) * mlp_gain[None, :]).astype(jnp.bfloat16)
        return (
            core_sum(dot32(mid, w_gate).astype(jnp.bfloat16)),
            core_sum(dot32(mid, w_up).astype(jnp.bfloat16)),
        )

    def finish(hidden_all, stream):
        down = dot32(hidden_all, w_down).astype(jnp.bfloat16)
        mlp_out = row_ring.reduce_scatter(row_blocks(down, row_part))
        own = cut_from(stream, (slot_of_row(row_place, row_part), 0), (row_part, stream.shape[1]))
        return (own.astype(jnp.float32) + mlp_out).astype(jnp.bfloat16)

    def part_slot(who):
        return slot_of_row(who, row_part)

    parts = range(PARTS)
    attended, late = [], ()
    for part in parts:
        got, late = gather_rows(attend(part), 0, part_slot, late)
        attended.append(got)
    full, late = [], ()
    for part in parts:
        got, late = gather_rows(project(part, attended[part]), 1, lambda who: who * row_width, late)
        full.append(got)
    streams, gates, ups, after = [], [], [], ()
    for part in parts:
        stream = spread(full[part], after)
        gate, up = widen(tie(stream, *after) if after else stream)
        streams.append(stream)
        gates.append(gate)
        ups.append(up)
        after = (gate, up)
    hidden, outs, after = [], [], ()
    for part in parts:
        scale = mlp_scale(full[part])
        gate = lane_sum(gates[part]) * scale
        up = lane_sum(tie(ups[part], *after) if after else ups[part]) * scale
        own = (jax.nn.silu(gate) * up).astype(jnp.bfloat16)
        everyone, far = gather_cols(own)
        after = (far,)
        outs.append(finish(everyone, streams[part]))
    output = jnp.concatenate(outs, axis=0)

    block_count = page_table.shape[0]
    page_size = tokens // block_count
    slots_local = block_count // rows
    slot_ids = row_place * slots_local + jnp.arange(slots_local, dtype=jnp.int32)
    block_ids = jnp.arange(block_count, dtype=jnp.int32)
    owned_blocks = jnp.sum(
        jnp.where(late_pages[None, :] == slot_ids[:, None], block_ids[None, :], 0), axis=1
    )
    row_blocks_count = block_count // rows
    at_row = quotient(owned_blocks, row_blocks_count)
    away = remainder(walk.spot_of(at_row) - row_ring.spot + rows, rows)
    owned_blocks = away * row_blocks_count + remainder(owned_blocks, row_blocks_count)
    page_rows = owned_blocks[:, None] * page_size + jnp.arange(page_size, dtype=jnp.int32)[None, :]
    key_cache_pages = jnp.take(key_all, page_rows, axis=0)
    value_cache_pages = jnp.take(value_all, page_rows, axis=0)
    return (output, key_cache_pages, value_cache_pages)


def solution(mesh):
    return jax.shard_map(
        per_device,
        mesh=mesh,
        in_specs=(
            P("col", "row"),
            P("row"),
            P("row", "col"),
            P("row", "col"),
            P("row", "col"),
            P("col", "row"),
            P("col"),
            P("col", "row"),
            P("col", "row"),
            P("row", "col"),
            P(),
            P(),
        ),
        out_specs=(P("row", "col"), P("row", None, "col"), P("row", None, "col")),
        check_vma=False,
    )
```

profile of v0, /device:TPU:0, one launch (start us, length us, event | category | flops | bytes accessed | tf_op | source)
XLA Modules:
  0.0 392.4 jit_solution(10587082676950000724)
XLA Ops:
  0.7 3.0 collective-permute-start.1
  3.7 10.8 %collective-permute-done.1 = bf16[256,896]{1,0:T(8,128)(2,1)} collective-permute-done((bf16[256,896]{1,0:T(8,128)(2,1)}, bf16[256,896]{1,0:T(8,128)(2,1)}, u32[]{:S(2)}, u32[]{:S(2)}) %collective-permute-start.1) | collective-permute-done | bytes 458784 | tf_op jit(solution)/shard_map/ppermute | solution.py:65
  14.6 1.9 fusion.78
  16.6 1.7 fusion.2
  18.7 5.1 %convolution_convert_fusion.4 = bf16[1024,1792]{1,0:T(8,128)(2,1)S(1)} fusion(bf16[896,1792]{1,0:T(8,128)(2,1)S(1)} %copy-done, f32[896]{0:T(1024)S(1)} %copy-done.12, bf16[256,896]{1,0:T(8,128)(2,1)S(1)} %collective-permute-done.2, bf16[256,896]{1,0:T(8,128)(2,1)} %collective-permute-done.1, bf16[256,896]{1,0:T(8,128)(2,1)} %collective-permute-done, ...), kind=kOutput, calls=%fused_computation.10 | convolution fusion | flops 3299344384 | bytes 8719872 | tf_op jit(solution)/shard_map/dot_general | solution.py:143
  23.9 1.8 collective-permute-start.22
  26.0 1.7 collective-permute-start.11
  27.7 2.0 fusion.43
  29.7 1.9 fusion.46
  32.3 1.7 collective-permute-start.3
  36.1 1.9 collective-permute-done.12
  38.0 2.6 collective-permute-start.13
  43.3 2.6 collective-permute-done.8
  45.9 1.7 collective-permute-done.4
  52.1 2.1 collective-permute-done.5
  57.7 6.2 %collective-permute-done.23 = bf16[128,1792]{1,0:T(8,128)(2,1)S(1)} collective-permute-done((bf16[128,1792]{1,0:T(8,128)(2,1)S(1)}, bf16[128,1792]{1,0:T(8,128)(2,1)S(1)}, u32[]{:S(2)}, u32[]{:S(2)}) %collective-permute-start.23) | collective-permute-done | bytes 458784 | tf_op jit(solution)/shard_map/ppermute | solution.py:65
  69.0 5.8 %collective-permute-done.24 = bf16[128,1792]{1,0:T(8,128)(2,1)S(1)} collective-permute-done((bf16[128,1792]{1,0:T(8,128)(2,1)S(1)}, bf16[128,1792]{1,0:T(8,128)(2,1)S(1)}, u32[]{:S(2)}, u32[]{:S(2)}) %collective-permute-start.24) | collective-permute-done | bytes 458784 | tf_op jit(solution)/shard_map/ppermute | solution.py:65
  76.6 2.0 collective-permute-start.18
  78.8 10.6 %collective-permute-done.15 = bf16[128,512]{0,1:T(8,128)(2,1)S(1)} collective-permute-done((bf16[128,512]{0,1:T(8,128)(2,1)S(1)}, bf16[128,512]{0,1:T(8,128)(2,1)S(1)}, u32[]{:S(2)}, u32[]{:S(2)}) %collective-permute-start.15) | collective-permute-done | bytes 131104 | tf_op jit(solution)/shard_map/ppermute | solution.py:65
  96.9 6.1 %collective-permute-done.21 = bf16[64,512]{0,1:T(8,128)(2,1)S(1)} collective-permute-done((bf16[64,512]{0,1:T(8,128)(2,1)S(1)}, bf16[64,512]{0,1:T(8,128)(2,1)S(1)}, u32[]{:S(2)}, u32[]{:S(2)}) %collective-permute-start.21) | collective-permute-done | bytes 65568 | tf_op jit(solution)/shard_map/ppermute | solution.py:65
  103.0 2.1 concatenate.87
  107.3 2.9 convert_reduce_fusion.1
  110.2 2.1 fusion.52
  114.9 2.9 convert_reduce_fusion
  117.7 2.1 fusion.51
  123.2 6.0 %collective-permute-done.32 = bf16[64,1792]{1,0:T(8,128)(2,1)S(1)} collective-permute-done((bf16[64,1792]{1,0:T(8,128)(2,1)S(1)}, bf16[64,1792]{1,0:T(8,128)(2,1)S(1)}, u32[]{:S(2)}, u32[]{:S(2)}) %collective-permute-start.32) | collective-permute-done | bytes 229408 | tf_op jit(solution)/shard_map/ppermute | solution.py:65
  131.6 3.6 collective-permute-done.34
  136.1 2.0 collective-permute-start.67
  138.2 2.0 collective-permute-start.37
  140.4 2.8 collective-permute-done.36
  143.4 2.1 convolution_convert_fusion.8
  147.8 6.0 %collective-permute-done.68 = bf16[64,1792]{1,0:T(8,128)(2,1)S(1)} collective-permute-done((bf16[64,1792]{1,0:T(8,128)(2,1)S(1)}, bf16[64,1792]{1,0:T(8,128)(2,1)S(1)}, u32[]{:S(2)}, u32[]{:S(2)}) %collective-permute-start.68) | collective-permute-done | bytes 229408 | tf_op jit(solution)/shard_map/ppermute | solution.py:65
  157.6 3.5 collective-permute-done.70
  165.1 12.1 %collective-permute-start.41 = (bf16[128,896]{1,0:T(8,128)(2,1)}, bf16[128,896]{1,0:T(8,128)(2,1)}, u32[]{:S(2)}, u32[]{:S(2)}) collective-permute-start(bf16[128,896]{1,0:T(8,128)(2,1)} %get-tuple-element.86), channel_id=1, source_target_pairs={{8,0},{16,8},{24,16},{28,24},{20,28},{12,20},{4,12},{0,4},{9,1},{1... | collective-permute-start | bytes 688136 | tf_op jit(solution)/shard_map/ppermute | solution.py:65
  177.2 2.1 convolution_convert_fusion.7
  192.7 2.5 collective-permute-done.75
  195.3 2.2 collective-permute-done.44
  202.5 3.8 collective-permute-done.46
  210.2 1.8 collective-permute-start.78
  212.4 5.8 %collective-permute-done.78 = bf16[128,896]{1,0:T(8,128)(2,1)S(1)} collective-permute-done((bf16[128,896]{1,0:T(8,128)(2,1)S(1)}, bf16[128,896]{1,0:T(8,128)(2,1)S(1)}, u32[]{:S(2)}, u32[]{:S(2)}) %collective-permute-start.78) | collective-permute-done | bytes 229408 | tf_op jit(solution)/shard_map/ppermute | solution.py:65
  218.2 1.7 collective-permute-start.80
  220.3 5.0 %collective-permute-done.80 = bf16[128,896]{1,0:T(8,128)(2,1)S(1)} collective-permute-done((bf16[128,896]{1,0:T(8,128)(2,1)S(1)}, bf16[128,896]{1,0:T(8,128)(2,1)S(1)}, u32[]{:S(2)}, u32[]{:S(2)}) %collective-permute-start.80) | collective-permute-done | bytes 229408 | tf_op jit(solution)/shard_map/ppermute | solution.py:65
  225.4 1.8 collective-permute-start.82
  227.6 2.6 collective-permute-done.82
  230.2 1.8 collective-permute-done.83
  234.1 10.0 %convolution_convert_fusion.2 = bf16[512,2560]{1,0:T(8,128)(2,1)S(1)} fusion(bf16[1792,2560]{1,0:T(8,128)(2,1)} %param.22, f32[1792]{0:T(1024)S(1)} %copy-done.11, bf16[128,1792]{1,0:T(8,128)(2,1)S(1)} %collective-permute-done.50, bf16[128,1792]{1,0:T(8,128)(2,1)S(1)} %get-tuple-element.61, bf16[128,1792]{1,0:T(8,128)(2,1)S(1)} %collective-permute-done.48, ...), kind=kOutput, calls=%fused_computation.8 | convolution fusion | flops 4708106240 | bytes 13638656 | tf_op jit(solution)/shard_map/dot_general | solution.py:143
  244.4 5.2 %convolution_convert_fusion.3 = bf16[512,2560]{1,0:T(8,128)(2,1)S(1)} fusion(bf16[1792,2560]{1,0:T(8,128)(2,1)S(1)} %bitcast.238, f32[1792]{0:T(1024)S(1)} %copy-done.11, bf16[128,1792]{1,0:T(8,128)(2,1)S(1)} %collective-permute-done.50, bf16[128,1792]{1,0:T(8,128)(2,1)S(1)} %get-tuple-element.61, bf16[128,1792]{1,0:T(8,128)(2,1)S(1)} %collective-permute-done.48, ...), kind=kOutput, calls=%fused_computation.9 | convolution fusion | flops 4708106240 | bytes 13638656 | tf_op jit(solution)/shard_map/dot_general | solution.py:143
  250.1 5.1 %collective-permute-done.85 = bf16[128,3584]{1,0:T(8,128)(2,1)S(1)} collective-permute-done((bf16[128,3584]{1,0:T(8,128)(2,1)S(1)}, bf16[128,3584]{1,0:T(8,128)(2,1)S(1)}, u32[]{:S(2)}, u32[]{:S(2)}) %collective-permute-start.85) | collective-permute-done | bytes 917536 | tf_op jit(solution)/shard_map/ppermute | solution.py:320
  258.5 5.2 %convolution_convert_fusion.1 = bf16[512,2560]{1,0:T(8,128)(2,1)S(1)} fusion(bf16[1792,2560]{1,0:T(8,128)(2,1)S(1)} %bitcast.238, bf16[512,1792]{1,0:T(8,128)(2,1)S(1)} %pad_maximum_fusion.3, f32[1792]{0:T(1024)S(1)} %copy-done.11), kind=kOutput, calls=%fused_computation.7 | convolution fusion | flops 4701683712 | bytes 13638656 | tf_op jit(solution)/shard_map/dot_general | solution.py:143
  263.7 9.0 %convolution_convert_fusion = bf16[512,2560]{1,0:T(8,128)(2,1)S(1)} fusion(bf16[1792,2560]{1,0:T(8,128)(2,1)} %param.22, bf16[512,1792]{1,0:T(8,128)(2,1)S(1)} %pad_maximum_fusion.3, f32[1792]{0:T(1024)S(1)} %copy-done.11), kind=kOutput, calls=%fused_computation.6 | convolution fusion | flops 4701683712 | bytes 13638656 | tf_op jit(solution)/shard_map/dot_general | solution.py:143
  273.5 12.5 %collective-permute-done.52 = bf16[128,2560]{1,0:T(8,128)(2,1)S(1)} collective-permute-done((bf16[128,2560]{1,0:T(8,128)(2,1)S(1)}, bf16[128,2560]{1,0:T(8,128)(2,1)S(1)}, u32[]{:S(2)}, u32[]{:S(2)}) %collective-permute-start.52) | collective-permute-done | bytes 655392 | tf_op jit(solution)/shard_map/ppermute | solution.py:65
  289.6 14.9 %collective-permute-done.56 = bf16[128,2560]{1,0:T(8,128)(2,1)S(1)} collective-permute-done((bf16[128,2560]{1,0:T(8,128)(2,1)S(1)}, bf16[128,2560]{1,0:T(8,128)(2,1)S(1)}, u32[]{:S(2)}, u32[]{:S(2)}) %collective-permute-start.56) | collective-permute-done | bytes 655392 | tf_op jit(solution)/shard_map/ppermute | solution.py:65
  306.8 11.6 %collective-permute-done.88 = bf16[128,2560]{1,0:T(8,128)(2,1)S(1)} collective-permute-done((bf16[128,2560]{1,0:T(8,128)(2,1)S(1)}, bf16[128,2560]{1,0:T(8,128)(2,1)S(1)}, u32[]{:S(2)}, u32[]{:S(2)}) %collective-permute-start.88) | collective-permute-done | bytes 655392 | tf_op jit(solution)/shard_map/ppermute | solution.py:65
  318.5 11.8 %collective-permute-done.90 = bf16[128,2560]{1,0:T(8,128)(2,1)S(1)} collective-permute-done((bf16[128,2560]{1,0:T(8,128)(2,1)S(1)}, bf16[128,2560]{1,0:T(8,128)(2,1)S(1)}, u32[]{:S(2)}, u32[]{:S(2)}) %collective-permute-start.90) | collective-permute-done | bytes 655392 | tf_op jit(solution)/shard_map/ppermute | solution.py:65
  331.6 4.9 %convolution_convert_fusion.6 = bf16[512,1792]{1,0:T(8,128)(2,1)S(1)} fusion(bf16[2560,1792]{1,0:T(8,128)(2,1)S(1)} %bitcast.240, bf16[128,2560]{1,0:T(8,128)(2,1)S(1)} %collective-permute-done.57, bf16[128,2560]{1,0:T(8,128)(2,1)S(1)} %collective-permute-done.56, bf16[128,2560]{1,0:T(8,128)(2,1)S(1)} %collective-permute-done.55, ...), kind=kOutput, calls=%fused_computation.24 | convolution fusion | flops 4709023744 | bytes 13631488 | tf_op jit(solution)/shard_map/dot_general | solution.py:143
  338.8 6.7 %collective-permute-done.92 = bf16[128,2560]{1,0:T(8,128)(2,1)S(1)} collective-permute-done((bf16[128,2560]{1,0:T(8,128)(2,1)S(1)}, bf16[128,2560]{1,0:T(8,128)(2,1)S(1)}, u32[]{:S(2)}, u32[]{:S(2)}) %collective-permute-start.92) | collective-permute-done | bytes 655392 | tf_op jit(solution)/shard_map/ppermute | solution.py:65
  346.0 1.8 collective-permute-start.59
  347.8 4.9 %convolution_convert_fusion.5 = bf16[512,1792]{1,0:T(8,128)(2,1)S(1)} fusion(bf16[2560,1792]{1,0:T(8,128)(2,1)S(1)} %bitcast.240, bf16[128,2560]{1,0:T(8,128)(2,1)S(1)} %collective-permute-done.93, bf16[128,2560]{1,0:T(8,128)(2,1)S(1)} %collective-permute-done.92, bf16[128,2560]{1,0:T(8,128)(2,1)S(1)} %collective-permute-done.91, ...), kind=kOutput, calls=%fused_computation.23 | convolution fusion | flops 4709023744 | bytes 13631488 | tf_op jit(solution)/shard_map/dot_general | solution.py:143
  356.4 2.3 collective-permute-done.94
  361.3 6.3 %collective-permute-done.95 = bf16[64,1792]{1,0:T(8,128)(2,1)S(1)} collective-permute-done((bf16[64,1792]{1,0:T(8,128)(2,1)S(1)}, bf16[64,1792]{1,0:T(8,128)(2,1)S(1)}, u32[]{:S(2)}, u32[]{:S(2)}) %collective-permute-start.95) | collective-permute-done | bytes 229408 | tf_op jit(solution)/shard_map/ppermute | solution.py:65
  371.5 4.8 %collective-permute-done.96 = bf16[64,1792]{1,0:T(8,128)(2,1)S(1)} collective-permute-done((bf16[64,1792]{1,0:T(8,128)(2,1)S(1)}, bf16[64,1792]{1,0:T(8,128)(2,1)S(1)}, u32[]{:S(2)}, u32[]{:S(2)}) %collective-permute-start.96) | collective-permute-done | bytes 229408 | tf_op jit(solution)/shard_map/ppermute | solution.py:65
  378.9 6.1 %collective-permute-done.100 = bf16[64,1792]{1,0:T(8,128)(2,1)S(1)} collective-permute-done((bf16[64,1792]{1,0:T(8,128)(2,1)S(1)}, bf16[64,1792]{1,0:T(8,128)(2,1)S(1)}, u32[]{:S(2)}, u32[]{:S(2)}) %collective-permute-start.100) | collective-permute-done | bytes 229408 | tf_op jit(solution)/shard_map/ppermute | solution.py:65
  385.4 2.7 collective-permute-done.65
  388.3 2.9 collective-permute-done.101
  (354 shorter events, 104.8 us)
Async XLA Ops:
  0.7 13.9 %collective-permute-start.1 = (bf16[256,896]{1,0:T(8,128)(2,1)}, bf16[256,896]{1,0:T(8,128)(2,1)}, u32[]{:S(2)}, u32[]{:S(2)}) collective-permute-start(bf16[256,896]{1,0:T(8,128)(2,1)} %param.14), channel_id=1, source_target_pairs={{0,2},{2,0},{1,3},{3,1},{4,6},{6,4},{5,7},{7,5},{8,10},{10,8},{9,1... | collective-permute-start | bytes 1376264 | tf_op jit(solution)/shard_map/ppermute | solution.py:65
  3.7 12.8 %collective-permute-start = (bf16[256,896]{1,0:T(8,128)(2,1)}, bf16[256,896]{1,0:T(8,128)(2,1)}, u32[]{:S(2)}, u32[]{:S(2)}) collective-permute-start(bf16[256,896]{1,0:T(8,128)(2,1)} %param.14), channel_id=1, source_target_pairs={{0,1},{1,0},{2,3},{3,2},{4,5},{5,4},{6,7},{7,6},{8,9},{9,8},{10,11... | collective-permute-start | bytes 1376264 | tf_op jit(solution)/shard_map/ppermute | solution.py:171
  23.9 25.9 %collective-permute-start.22 = (bf16[64,1792]{1,0:T(8,128)(2,1)S(1)}, bf16[64,1792]{1,0:T(8,128)(2,1)S(1)}, u32[]{:S(2)}, u32[]{:S(2)}) collective-permute-start(bf16[64,1792]{1,0:T(8,128)(2,1)S(1)} %get-tuple-element.24), channel_id=1, source_target_pairs={{0,8},{8,16},{16,24},{24,28},{28,20},{20,12},{12,4},{4,0},{1,9},{9... | collective-permute-start | bytes 688136 | tf_op jit(solution)/shard_map/ppermute | solution.py:65
  25.8 24.0 %collective-permute-start.26 = (bf16[64,1792]{1,0:T(8,128)(2,1)S(1)}, bf16[64,1792]{1,0:T(8,128)(2,1)S(1)}, u32[]{:S(2)}, u32[]{:S(2)}) collective-permute-start(bf16[64,1792]{1,0:T(8,128)(2,1)S(1)} %get-tuple-element.26), channel_id=1, source_target_pairs={{8,0},{16,8},{24,16},{28,24},{20,28},{12,20},{4,12},{0,4},{9,1},{1... | collective-permute-start | bytes 688136 | tf_op jit(solution)/shard_map/ppermute | solution.py:65
  26.0 8.4 %collective-permute-start.11 = (f32[1024]{0:T(1024)S(1)}, f32[1024]{0:T(1024)S(1)}, u32[]{:S(2)}, u32[]{:S(2)}) collective-permute-start(f32[1024]{0:T(1024)S(1)} %fusion.2), channel_id=1, source_target_pairs={{0,4},{4,0},{8,12},{12,8},{16,20},{20,16},{24,28},{28,24},{1,5},{5... | collective-permute-start | bytes 12296 | tf_op jit(solution)/shard_map/ppermute | solution.py:255
  31.9 8.8 %collective-permute-start.7 = (bf16[64,512]{0,1:T(8,128)(2,1)S(1)}, bf16[64,512]{0,1:T(8,128)(2,1)S(1)}, u32[]{:S(2)}, u32[]{:S(2)}) collective-permute-start(bf16[64,512]{0,1:T(8,128)(2,1)S(1)} %get-tuple-element.70), channel_id=1, source_target_pairs={{8,0},{16,8},{24,16},{28,24},{20,28},{12,20},{4,12},{0,4},{9,1},{1... | collective-permute-start | bytes 196616 | tf_op jit(solution)/shard_map/ppermute | solution.py:65
  32.3 9.7 %collective-permute-start.3 = (bf16[64,512]{0,1:T(8,128)(2,1)S(1)}, bf16[64,512]{0,1:T(8,128)(2,1)S(1)}, u32[]{:S(2)}, u32[]{:S(2)}) collective-permute-start(bf16[64,512]{0,1:T(8,128)(2,1)S(1)} %get-tuple-element.69), channel_id=1, source_target_pairs={{0,8},{8,16},{16,24},{24,28},{28,20},{20,12},{12,4},{4,0},{1,9},{9... | collective-permute-start | bytes 196616 | tf_op jit(solution)/shard_map/ppermute | solution.py:65
  50.0 13.9 %collective-permute-start.23 = (bf16[128,1792]{1,0:T(8,128)(2,1)S(1)}, bf16[128,1792]{1,0:T(8,128)(2,1)S(1)}, u32[]{:S(2)}, u32[]{:S(2)}) collective-permute-start(bf16[128,1792]{1,0:T(8,128)(2,1)S(1)} %pad_maximum_fusion.5), channel_id=1, source_target_pairs={{0,8},{8,16},{16,24},{24,28},{28,20},{20,12},{12,4},{4,0},{1,9},{9... | collective-permute-start | bytes 1376264 | tf_op jit(solution)/shard_map/ppermute | solution.py:65
  51.3 17.6 %collective-permute-start.27 = (bf16[128,1792]{1,0:T(8,128)(2,1)S(1)}, bf16[128,1792]{1,0:T(8,128)(2,1)S(1)}, u32[]{:S(2)}, u32[]{:S(2)}) collective-permute-start(bf16[128,1792]{1,0:T(8,128)(2,1)S(1)} %pad_maximum_fusion.6), channel_id=1, source_target_pairs={{8,0},{16,8},{24,16},{28,24},{20,28},{12,20},{4,12},{0,4},{9,1},{1... | collective-permute-start | bytes 1376264 | tf_op jit(solution)/shard_map/ppermute | solution.py:65
  55.6 9.8 %collective-permute-start.10 = (bf16[128,512]{0,1:T(8,128)(2,1)S(1)}, bf16[128,512]{0,1:T(8,128)(2,1)S(1)}, u32[]{:S(2)}, u32[]{:S(2)}) collective-permute-start(bf16[128,512]{0,1:T(8,128)(2,1)S(1)} %get-tuple-element.51), channel_id=1, source_target_pairs={{8,0},{16,8},{24,16},{28,24},{20,28},{12,20},{4,12},{0,4},{9,1},{1... | collective-permute-start | bytes 393224 | tf_op jit(solution)/shard_map/ppermute | solution.py:65
  56.4 10.3 %collective-permute-start.6 = (bf16[128,512]{0,1:T(8,128)(2,1)S(1)}, bf16[128,512]{0,1:T(8,128)(2,1)S(1)}, u32[]{:S(2)}, u32[]{:S(2)}) collective-permute-start(bf16[128,512]{0,1:T(8,128)(2,1)S(1)} %get-tuple-element.50), channel_id=1, source_target_pairs={{0,8},{8,16},{16,24},{24,28},{28,20},{20,12},{12,4},{4,0},{1,9},{9... | collective-permute-start | bytes 393224 | tf_op jit(solution)/shard_map/ppermute | solution.py:65
  64.0 10.7 %collective-permute-start.24 = (bf16[128,1792]{1,0:T(8,128)(2,1)S(1)}, bf16[128,1792]{1,0:T(8,128)(2,1)S(1)}, u32[]{:S(2)}, u32[]{:S(2)}) collective-permute-start(bf16[128,1792]{1,0:T(8,128)(2,1)S(1)} %add_convert_fusion.3), channel_id=1, source_target_pairs={{0,8},{8,16},{16,24},{24,28},{28,20},{20,12},{12,4},{4,0},{1,9},{9... | collective-permute-start | bytes 1376264 | tf_op jit(solution)/shard_map/ppermute | solution.py:65
  66.9 9.7 %collective-permute-start.14 = (bf16[128,512]{0,1:T(8,128)(2,1)S(1)}, bf16[128,512]{0,1:T(8,128)(2,1)S(1)}, u32[]{:S(2)}, u32[]{:S(2)}) collective-permute-start(bf16[128,512]{0,1:T(8,128)(2,1)S(1)} %pad_maximum_fusion.14), channel_id=1, source_target_pairs={{8,0},{16,8},{24,16},{28,24},{20,28},{12,20},{4,12},{0,4},{9,1},{1... | collective-permute-start | bytes 393224 | tf_op jit(solution)/shard_map/ppermute | solution.py:65
  68.3 8.3 %collective-permute-start.17 = (bf16[128,512]{0,1:T(8,128)(2,1)S(1)}, bf16[128,512]{0,1:T(8,128)(2,1)S(1)}, u32[]{:S(2)}, u32[]{:S(2)}) collective-permute-start(bf16[128,512]{0,1:T(8,128)(2,1)S(1)} %pad_maximum_fusion.14), channel_id=1, source_target_pairs={{0,8},{8,16},{16,24},{24,28},{28,20},{20,12},{12,4},{4,0},{1,9},{9... | collective-permute-start | bytes 393224 | tf_op jit(solution)/shard_map/ppermute | solution.py:65
  75.0 18.0 %collective-permute-start.28 = (bf16[128,1792]{1,0:T(8,128)(2,1)S(1)}, bf16[128,1792]{1,0:T(8,128)(2,1)S(1)}, u32[]{:S(2)}, u32[]{:S(2)}) collective-permute-start(bf16[128,1792]{1,0:T(8,128)(2,1)S(1)} %get-tuple-element.21), channel_id=1, source_target_pairs={{8,0},{16,8},{24,16},{28,24},{20,28},{12,20},{4,12},{0,4},{9,1},{1... | collective-permute-start | bytes 1376264 | tf_op jit(solution)/shard_map/ppermute | solution.py:65
  76.6 12.9 %collective-permute-start.15 = (bf16[128,512]{0,1:T(8,128)(2,1)S(1)}, bf16[128,512]{0,1:T(8,128)(2,1)S(1)}, u32[]{:S(2)}, u32[]{:S(2)}) collective-permute-start(bf16[128,512]{0,1:T(8,128)(2,1)S(1)} %collective-permute-done.14), channel_id=1, source_target_pairs={{8,0},{16,8},{24,16},{28,24},{20,28},{12,20},{4,12},{0,4},{9,1},{1... | collective-permute-start | bytes 393224 | tf_op jit(solution)/shard_map/ppermute | solution.py:65
  76.6 14.4 %collective-permute-start.18 = (bf16[128,512]{0,1:T(8,128)(2,1)S(1)}, bf16[128,512]{0,1:T(8,128)(2,1)S(1)}, u32[]{:S(2)}, u32[]{:S(2)}) collective-permute-start(bf16[128,512]{0,1:T(8,128)(2,1)S(1)} %collective-permute-done.17), channel_id=1, source_target_pairs={{0,8},{8,16},{16,24},{24,28},{28,20},{20,12},{12,4},{4,0},{1,9},{9... | collective-permute-start | bytes 393224 | tf_op jit(solution)/shard_map/ppermute | solution.py:65
  91.5 13.7 %collective-permute-start.25 = (bf16[128,1792]{1,0:T(8,128)(2,1)S(1)}, bf16[128,1792]{1,0:T(8,128)(2,1)}, u32[]{:S(2)}, u32[]{:S(2)}) collective-permute-start(bf16[128,1792]{1,0:T(8,128)(2,1)S(1)} %get-tuple-element.20), channel_id=1, source_target_pairs={{0,8},{8,16},{16,24},{24,28},{28,20},{20,12},{12,4},{4,0},{1,9},{9... | collective-permute-start | bytes 1376264 | tf_op jit(solution)/shard_map/ppermute | solution.py:65
  93.1 12.1 %collective-permute-start.29 = (bf16[128,1792]{1,0:T(8,128)(2,1)S(1)}, bf16[128,1792]{1,0:T(8,128)(2,1)}, u32[]{:S(2)}, u32[]{:S(2)}) collective-permute-start(bf16[128,1792]{1,0:T(8,128)(2,1)S(1)} %add_convert_fusion), channel_id=1, source_target_pairs={{8,0},{16,8},{24,16},{28,24},{20,28},{12,20},{4,12},{0,4},{9,1},{1... | collective-permute-start | bytes 1376264 | tf_op jit(solution)/shard_map/ppermute | solution.py:65
  94.5 8.5 %collective-permute-start.21 = (bf16[64,512]{0,1:T(8,128)(2,1)S(1)}, bf16[64,512]{0,1:T(8,128)(2,1)S(1)}, u32[]{:S(2)}, u32[]{:S(2)}) collective-permute-start(bf16[64,512]{0,1:T(8,128)(2,1)S(1)} %slice.353), channel_id=1, source_target_pairs={{8,0},{16,8},{24,16},{28,24},{20,28},{12,20},{4,12},{0,4},{9,1},{1... | collective-permute-start | bytes 196616 | tf_op jit(solution)/shard_map/ppermute | solution.py:65
  112.8 8.1 %collective-permute-start.30 = (bf16[64,1792]{1,0:T(8,128)(2,1)S(1)}, bf16[64,1792]{1,0:T(8,128)(2,1)S(1)}, u32[]{:S(2)}, u32[]{:S(2)}) collective-permute-start(bf16[64,1792]{1,0:T(8,128)(2,1)S(1)} %convert_element_type.514), channel_id=1, source_target_pairs={{0,8},{8,16},{16,24},{24,28},{28,20},{20,12},{12,4},{4,0},{1,9},{9... | collective-permute-start | bytes 688136 | tf_op jit(solution)/shard_map/ppermute | solution.py:65
  120.9 8.3 %collective-permute-start.32 = (bf16[64,1792]{1,0:T(8,128)(2,1)S(1)}, bf16[64,1792]{1,0:T(8,128)(2,1)S(1)}, u32[]{:S(2)}, u32[]{:S(2)}) collective-permute-start(bf16[64,1792]{1,0:T(8,128)(2,1)S(1)} %collective-permute-done.30), channel_id=1, source_target_pairs={{0,8},{8,16},{16,24},{24,28},{28,20},{20,12},{12,4},{4,0},{1,9},{9... | collective-permute-start | bytes 688136 | tf_op jit(solution)/shard_map/ppermute | solution.py:65
  121.6 8.4 %collective-permute-start.33 = (bf16[64,1792]{1,0:T(8,128)(2,1)S(1)}, bf16[64,1792]{1,0:T(8,128)(2,1)S(1)}, u32[]{:S(2)}, u32[]{:S(2)}) collective-permute-start(bf16[64,1792]{1,0:T(8,128)(2,1)S(1)} %collective-permute-done.31), channel_id=1, source_target_pairs={{8,0},{16,8},{24,16},{28,24},{20,28},{12,20},{4,12},{0,4},{9,1},{1... | collective-permute-start | bytes 688136 | tf_op jit(solution)/shard_map/ppermute | solution.py:65
  136.0 9.5 %collective-permute-start.66 = (bf16[64,1792]{1,0:T(8,128)(2,1)S(1)}, bf16[64,1792]{1,0:T(8,128)(2,1)S(1)}, u32[]{:S(2)}, u32[]{:S(2)}) collective-permute-start(bf16[64,1792]{1,0:T(8,128)(2,1)S(1)} %convert_element_type.569), channel_id=1, source_target_pairs={{0,8},{8,16},{16,24},{24,28},{28,20},{20,12},{12,4},{4,0},{1,9},{9... | collective-permute-start | bytes 688136 | tf_op jit(solution)/shard_map/ppermute | solution.py:65
  136.1 10.6 %collective-permute-start.67 = (bf16[64,1792]{1,0:T(8,128)(2,1)S(1)}, bf16[64,1792]{1,0:T(8,128)(2,1)S(1)}, u32[]{:S(2)}, u32[]{:S(2)}) collective-permute-start(bf16[64,1792]{1,0:T(8,128)(2,1)S(1)} %convert_element_type.569), channel_id=1, source_target_pairs={{8,0},{16,8},{24,16},{28,24},{20,28},{12,20},{4,12},{0,4},{9,1},{1... | collective-permute-start | bytes 688136 | tf_op jit(solution)/shard_map/ppermute | solution.py:65
  145.5 10.4 %collective-permute-start.38 = (bf16[2,128,896]{2,1,0:T(8,128)(2,1)S(1)}, bf16[2,128,896]{2,1,0:T(8,128)(2,1)S(1)}, u32[]{:S(2)}, u32[]{:S(2)}) collective-permute-start(bf16[2,128,896]{2,1,0:T(8,128)(2,1)S(1)} %slice_bitcast_fusion.17), channel_id=1, source_target_pairs={{0,1},{1,0},{2,3},{3,2},{4,5},{5,4},{6,7},{7,6},{8,9},{9,8},{10,11... | collective-permute-start | bytes 1376264 | tf_op jit(solution)/shard_map/ppermute | solution.py:171
  145.6 8.2 %collective-permute-start.68 = (bf16[64,1792]{1,0:T(8,128)(2,1)S(1)}, bf16[64,1792]{1,0:T(8,128)(2,1)S(1)}, u32[]{:S(2)}, u32[]{:S(2)}) collective-permute-start(bf16[64,1792]{1,0:T(8,128)(2,1)S(1)} %collective-permute-done.66), channel_id=1, source_target_pairs={{0,8},{8,16},{16,24},{24,28},{28,20},{20,12},{12,4},{4,0},{1,9},{9... | collective-permute-start | bytes 688136 | tf_op jit(solution)/shard_map/ppermute | solution.py:65
  161.1 16.1 %collective-permute-start.72 = (bf16[32,1792]{1,0:T(8,128)(2,1)S(1)}, bf16[32,1792]{1,0:T(8,128)(2,1)S(1)}, u32[]{:S(2)}, u32[]{:S(2)}) collective-permute-start(bf16[32,1792]{1,0:T(8,128)(2,1)S(1)} %slice.377), channel_id=1, source_target_pairs={{0,8},{8,16},{16,24},{24,28},{28,20},{20,12},{12,4},{4,0},{1,9},{9... | collective-permute-start | bytes 344072 | tf_op jit(solution)/shard_map/ppermute | solution.py:65
  161.9 15.3 %collective-permute-start.73 = (bf16[32,1792]{1,0:T(8,128)(2,1)S(1)}, bf16[32,1792]{1,0:T(8,128)(2,1)S(1)}, u32[]{:S(2)}, u32[]{:S(2)}) collective-permute-start(bf16[32,1792]{1,0:T(8,128)(2,1)S(1)} %slice.378), channel_id=1, source_target_pairs={{8,0},{16,8},{24,16},{28,24},{20,28},{12,20},{4,12},{0,4},{9,1},{1... | collective-permute-start | bytes 344072 | tf_op jit(solution)/shard_map/ppermute | solution.py:65
  164.3 18.2 %collective-permute-start.40 = (bf16[128,896]{1,0:T(8,128)(2,1)}, bf16[128,896]{1,0:T(8,128)(2,1)}, u32[]{:S(2)}, u32[]{:S(2)}) collective-permute-start(bf16[128,896]{1,0:T(8,128)(2,1)} %get-tuple-element.86), channel_id=1, source_target_pairs={{0,8},{8,16},{16,24},{24,28},{28,20},{20,12},{12,4},{4,0},{1,9},{9... | collective-permute-start | bytes 688136 | tf_op jit(solution)/shard_map/ppermute | solution.py:65
  165.1 18.3 %collective-permute-start.41 = (bf16[128,896]{1,0:T(8,128)(2,1)}, bf16[128,896]{1,0:T(8,128)(2,1)}, u32[]{:S(2)}, u32[]{:S(2)}) collective-permute-start(bf16[128,896]{1,0:T(8,128)(2,1)} %get-tuple-element.86), channel_id=1, source_target_pairs={{8,0},{16,8},{24,16},{28,24},{20,28},{12,20},{4,12},{0,4},{9,1},{1... | collective-permute-start | bytes 688136 | tf_op jit(solution)/shard_map/ppermute | solution.py:65
  182.5 8.1 %collective-permute-start.42 = (bf16[128,896]{1,0:T(8,128)(2,1)}, bf16[128,896]{1,0:T(8,128)(2,1)S(1)}, u32[]{:S(2)}, u32[]{:S(2)}) collective-permute-start(bf16[128,896]{1,0:T(8,128)(2,1)} %collective-permute-done.40), channel_id=1, source_target_pairs={{0,8},{8,16},{16,24},{24,28},{28,20},{20,12},{12,4},{4,0},{1,9},{9... | collective-permute-start | bytes 688136 | tf_op jit(solution)/shard_map/ppermute | solution.py:65
  183.3 8.0 %collective-permute-start.43 = (bf16[128,896]{1,0:T(8,128)(2,1)}, bf16[128,896]{1,0:T(8,128)(2,1)S(1)}, u32[]{:S(2)}, u32[]{:S(2)}) collective-permute-start(bf16[128,896]{1,0:T(8,128)(2,1)} %collective-permute-done.41), channel_id=1, source_target_pairs={{8,0},{16,8},{24,16},{28,24},{20,28},{12,20},{4,12},{0,4},{9,1},{1... | collective-permute-start | bytes 688136 | tf_op jit(solution)/shard_map/ppermute | solution.py:65
  198.0 12.2 %collective-permute-start.76 = (bf16[128,896]{1,0:T(8,128)(2,1)S(1)}, bf16[128,896]{1,0:T(8,128)(2,1)S(1)}, u32[]{:S(2)}, u32[]{:S(2)}) collective-permute-start(bf16[128,896]{1,0:T(8,128)(2,1)S(1)} %fusion.56), channel_id=1, source_target_pairs={{0,8},{8,16},{16,24},{24,28},{28,20},{20,12},{12,4},{4,0},{1,9},{9... | collective-permute-start | bytes 688136 | tf_op jit(solution)/shard_map/ppermute | solution.py:65
  199.4 12.6 %collective-permute-start.77 = (bf16[128,896]{1,0:T(8,128)(2,1)S(1)}, bf16[128,896]{1,0:T(8,128)(2,1)S(1)}, u32[]{:S(2)}, u32[]{:S(2)}) collective-permute-start(bf16[128,896]{1,0:T(8,128)(2,1)S(1)} %fusion.56), channel_id=1, source_target_pairs={{8,0},{16,8},{24,16},{28,24},{20,28},{12,20},{4,12},{0,4},{9,1},{1... | collective-permute-start | bytes 688136 | tf_op jit(solution)/shard_map/ppermute | solution.py:65
  208.2 23.9 %collective-permute-start.49 = (bf16[128,3584]{1,0:T(8,128)(2,1)S(1)}, bf16[128,3584]{1,0:T(8,128)(2,1)S(1)}, u32[]{:S(2)}, u32[]{:S(2)}) collective-permute-start(bf16[128,3584]{1,0:T(8,128)(2,1)S(1)} %constant_dynamic-slice_fusion.13), channel_id=1, source_target_pairs={{0,2},{1,3},{2,0},{3,1},{4,6},{5,7},{6,4},{7,5},{8,10},{9,11},{10,... | collective-permute-start | bytes 2752520 | tf_op jit(solution)/shard_map/ppermute | solution.py:320
  210.1 23.4 %collective-permute-start.48 = (bf16[128,1792]{1,0:T(8,128)(2,1)S(1)}, bf16[128,1792]{1,0:T(8,128)(2,1)S(1)}, u32[]{:S(2)}, u32[]{:S(2)}) collective-permute-start(bf16[128,1792]{1,0:T(8,128)(2,1)S(1)} %get-tuple-element.47), channel_id=1, source_target_pairs={{0,1},{1,0},{2,3},{3,2},{4,5},{5,4},{6,7},{7,6},{8,9},{9,8},{10,11... | collective-permute-start | bytes 1376264 | tf_op jit(solution)/shard_map/ppermute | solution.py:171
  210.2 8.0 %collective-permute-start.78 = (bf16[128,896]{1,0:T(8,128)(2,1)S(1)}, bf16[128,896]{1,0:T(8,128)(2,1)S(1)}, u32[]{:S(2)}, u32[]{:S(2)}) collective-permute-start(bf16[128,896]{1,0:T(8,128)(2,1)S(1)} %collective-permute-done.76), channel_id=1, source_target_pairs={{0,8},{8,16},{16,24},{24,28},{28,20},{20,12},{12,4},{4,0},{1,9},{9... | collective-permute-start | bytes 688136 | tf_op jit(solution)/shard_map/ppermute | solution.py:65
  212.0 7.9 %collective-permute-start.79 = (bf16[128,896]{1,0:T(8,128)(2,1)S(1)}, bf16[128,896]{1,0:T(8,128)(2,1)S(1)}, u32[]{:S(2)}, u32[]{:S(2)}) collective-permute-start(bf16[128,896]{1,0:T(8,128)(2,1)S(1)} %collective-permute-done.77), channel_id=1, source_target_pairs={{8,0},{16,8},{24,16},{28,24},{20,28},{12,20},{4,12},{0,4},{9,1},{1... | collective-permute-start | bytes 688136 | tf_op jit(solution)/shard_map/ppermute | solution.py:65
  232.4 22.8 %collective-permute-start.85 = (bf16[128,3584]{1,0:T(8,128)(2,1)S(1)}, bf16[128,3584]{1,0:T(8,128)(2,1)S(1)}, u32[]{:S(2)}, u32[]{:S(2)}) collective-permute-start(bf16[128,3584]{1,0:T(8,128)(2,1)S(1)} %constant_dynamic-slice_fusion.5), channel_id=1, source_target_pairs={{0,2},{1,3},{2,0},{3,1},{4,6},{5,7},{6,4},{7,5},{8,10},{9,11},{10,... | collective-permute-start | bytes 2752520 | tf_op jit(solution)/shard_map/ppermute | solution.py:320
  233.3 24.9 %collective-permute-start.84 = (bf16[128,1792]{1,0:T(8,128)(2,1)S(1)}, bf16[128,1792]{1,0:T(8,128)(2,1)S(1)}, u32[]{:S(2)}, u32[]{:S(2)}) collective-permute-start(bf16[128,1792]{1,0:T(8,128)(2,1)S(1)} %get-tuple-element.45), channel_id=1, source_target_pairs={{0,1},{1,0},{2,3},{3,2},{4,5},{5,4},{6,7},{7,6},{8,9},{9,8},{10,11... | collective-permute-start | bytes 1376264 | tf_op jit(solution)/shard_map/ppermute | solution.py:171
  244.2 11.1 %collective-permute-start.53 = (bf16[2,128,2560]{2,1,0:T(8,128)(2,1)S(1)}, bf16[2,128,2560]{2,1,0:T(8,128)(2,1)S(1)}, u32[]{:S(2)}, u32[]{:S(2)}) collective-permute-start(bf16[2,128,2560]{2,1,0:T(8,128)(2,1)S(1)} %slice_bitcast_fusion.4), channel_id=1, source_target_pairs={{0,1},{1,0},{2,3},{3,2},{4,5},{5,4},{6,7},{7,6},{8,9},{9,8},{10,11... | collective-permute-start | bytes 3932168 | tf_op jit(solution)/shard_map/ppermute | solution.py:171
  255.6 17.9 %collective-permute-start.54 = (bf16[128,2560]{1,0:T(8,128)(2,1)S(1)}, bf16[128,2560]{1,0:T(8,128)(2,1)S(1)}, u32[]{:S(2)}, u32[]{:S(2)}) collective-permute-start(bf16[128,2560]{1,0:T(8,128)(2,1)S(1)} %slice_bitcast_fusion.10), channel_id=1, source_target_pairs={{0,2},{2,0},{1,3},{3,1},{4,6},{6,4},{5,7},{7,5},{8,10},{10,8},{9,1... | collective-permute-start | bytes 1966088 | tf_op jit(solution)/shard_map/ppermute | solution.py:65
  256.7 29.4 %collective-permute-start.52 = (bf16[128,2560]{1,0:T(8,128)(2,1)S(1)}, bf16[128,2560]{1,0:T(8,128)(2,1)S(1)}, u32[]{:S(2)}, u32[]{:S(2)}) collective-permute-start(bf16[128,2560]{1,0:T(8,128)(2,1)S(1)} %slice_bitcast_fusion.12), channel_id=1, source_target_pairs={{0,2},{2,0},{1,3},{3,1},{4,6},{6,4},{5,7},{7,5},{8,10},{10,8},{9,1... | collective-permute-start | bytes 1966088 | tf_op jit(solution)/shard_map/ppermute | solution.py:65
  272.8 14.6 %collective-permute-start.87 = (bf16[2,128,2560]{2,1,0:T(8,128)(2,1)S(1)}, bf16[2,128,2560]{2,1,0:T(8,128)(2,1)S(1)}, u32[]{:S(2)}, u32[]{:S(2)}) collective-permute-start(bf16[2,128,2560]{2,1,0:T(8,128)(2,1)S(1)} %slice_bitcast_fusion.2), channel_id=1, source_target_pairs={{0,1},{1,0},{2,3},{3,2},{4,5},{5,4},{6,7},{7,6},{8,9},{9,8},{10,11... | collective-permute-start | bytes 3932168 | tf_op jit(solution)/shard_map/ppermute | solution.py:171
  273.0 16.2 %collective-permute-start.89 = (bf16[2,128,2560]{2,1,0:T(8,128)(2,1)S(1)}, bf16[2,128,2560]{2,1,0:T(8,128)(2,1)S(1)}, u32[]{:S(2)}, u32[]{:S(2)}) collective-permute-start(bf16[2,128,2560]{2,1,0:T(8,128)(2,1)S(1)} %slice_bitcast_fusion), channel_id=1, source_target_pairs={{0,1},{1,0},{2,3},{3,2},{4,5},{5,4},{6,7},{7,6},{8,9},{9,8},{10,11... | collective-permute-start | bytes 3932168 | tf_op jit(solution)/shard_map/ppermute | solution.py:171
  286.7 17.7 %collective-permute-start.56 = (bf16[128,2560]{1,0:T(8,128)(2,1)S(1)}, bf16[128,2560]{1,0:T(8,128)(2,1)S(1)}, u32[]{:S(2)}, u32[]{:S(2)}) collective-permute-start(bf16[128,2560]{1,0:T(8,128)(2,1)S(1)} %fusion.41), channel_id=1, source_target_pairs={{0,2},{2,0},{1,3},{3,1},{4,6},{6,4},{5,7},{7,5},{8,10},{10,8},{9,1... | collective-permute-start | bytes 1966088 | tf_op jit(solution)/shard_map/ppermute | solution.py:65
  287.7 30.8 %collective-permute-start.88 = (bf16[128,2560]{1,0:T(8,128)(2,1)S(1)}, bf16[128,2560]{1,0:T(8,128)(2,1)S(1)}, u32[]{:S(2)}, u32[]{:S(2)}) collective-permute-start(bf16[128,2560]{1,0:T(8,128)(2,1)S(1)} %slice_bitcast_fusion.8), channel_id=1, source_target_pairs={{0,2},{2,0},{1,3},{3,1},{4,6},{6,4},{5,7},{7,5},{8,10},{10,8},{9,1... | collective-permute-start | bytes 1966088 | tf_op jit(solution)/shard_map/ppermute | solution.py:65
  304.5 25.8 %collective-permute-start.90 = (bf16[128,2560]{1,0:T(8,128)(2,1)S(1)}, bf16[128,2560]{1,0:T(8,128)(2,1)S(1)}, u32[]{:S(2)}, u32[]{:S(2)}) collective-permute-start(bf16[128,2560]{1,0:T(8,128)(2,1)S(1)} %slice_bitcast_fusion.14), channel_id=1, source_target_pairs={{0,2},{2,0},{1,3},{3,1},{4,6},{6,4},{5,7},{7,5},{8,10},{10,8},{9,1... | collective-permute-start | bytes 1966088 | tf_op jit(solution)/shard_map/ppermute | solution.py:65
  306.3 25.3 %collective-permute-start.55 = (bf16[128,2560]{1,0:T(8,128)(2,1)S(1)}, bf16[128,2560]{1,0:T(8,128)(2,1)S(1)}, u32[]{:S(2)}, u32[]{:S(2)}) collective-permute-start(bf16[128,2560]{1,0:T(8,128)(2,1)S(1)} %fusion.41), channel_id=1, source_target_pairs={{0,1},{1,0},{2,3},{3,2},{4,5},{5,4},{6,7},{7,6},{8,9},{9,8},{10,11... | collective-permute-start | bytes 1966088 | tf_op jit(solution)/shard_map/ppermute | solution.py:171
  306.4 25.2 %collective-permute-start.57 = (bf16[128,2560]{1,0:T(8,128)(2,1)S(1)}, bf16[128,2560]{1,0:T(8,128)(2,1)S(1)}, u32[]{:S(2)}, u32[]{:S(2)}) collective-permute-start(bf16[128,2560]{1,0:T(8,128)(2,1)S(1)} %collective-permute-done.56), channel_id=1, source_target_pairs={{0,1},{1,0},{2,3},{3,2},{4,5},{5,4},{6,7},{7,6},{8,9},{9,8},{10,11... | collective-permute-start | bytes 1966088 | tf_op jit(solution)/shard_map/ppermute | solution.py:171
  331.0 14.6 %collective-permute-start.92 = (bf16[128,2560]{1,0:T(8,128)(2,1)S(1)}, bf16[128,2560]{1,0:T(8,128)(2,1)S(1)}, u32[]{:S(2)}, u32[]{:S(2)}) collective-permute-start(bf16[128,2560]{1,0:T(8,128)(2,1)S(1)} %fusion.37), channel_id=1, source_target_pairs={{0,2},{2,0},{1,3},{3,1},{4,6},{6,4},{5,7},{7,5},{8,10},{10,8},{9,1... | collective-permute-start | bytes 1966088 | tf_op jit(solution)/shard_map/ppermute | solution.py:65
  336.5 9.0 %collective-permute-start.58 = (bf16[32,1792]{1,0:T(8,128)(2,1)S(1)}, bf16[32,1792]{1,0:T(8,128)(2,1)S(1)}, u32[]{:S(2)}, u32[]{:S(2)}) collective-permute-start(bf16[32,1792]{1,0:T(8,128)(2,1)S(1)} %get-tuple-element.32), channel_id=1, source_target_pairs={{0,8},{8,16},{16,24},{24,28},{28,20},{20,12},{12,4},{4,0},{1,9},{9... | collective-permute-start | bytes 344072 | tf_op jit(solution)/shard_map/ppermute | solution.py:65
  338.7 9.0 %collective-permute-start.91 = (bf16[128,2560]{1,0:T(8,128)(2,1)S(1)}, bf16[128,2560]{1,0:T(8,128)(2,1)S(1)}, u32[]{:S(2)}, u32[]{:S(2)}) collective-permute-start(bf16[128,2560]{1,0:T(8,128)(2,1)S(1)} %fusion.37), channel_id=1, source_target_pairs={{0,1},{1,0},{2,3},{3,2},{4,5},{5,4},{6,7},{7,6},{8,9},{9,8},{10,11... | collective-permute-start | bytes 1966088 | tf_op jit(solution)/shard_map/ppermute | solution.py:171
  345.6 23.6 %collective-permute-start.63 = (bf16[64,1792]{1,0:T(8,128)(2,1)S(1)}, bf16[64,1792]{1,0:T(8,128)(2,1)S(1)}, u32[]{:S(2)}, u32[]{:S(2)}) collective-permute-start(bf16[64,1792]{1,0:T(8,128)(2,1)S(1)} %pad_maximum_fusion.9), channel_id=1, source_target_pairs={{8,0},{16,8},{24,16},{28,24},{20,28},{12,20},{4,12},{0,4},{9,1},{1... | collective-permute-start | bytes 688136 | tf_op jit(solution)/shard_map/ppermute | solution.py:65
  346.0 8.8 %collective-permute-start.59 = (bf16[64,1792]{1,0:T(8,128)(2,1)S(1)}, bf16[64,1792]{1,0:T(8,128)(2,1)S(1)}, u32[]{:S(2)}, u32[]{:S(2)}) collective-permute-start(bf16[64,1792]{1,0:T(8,128)(2,1)S(1)} %pad_maximum_fusion.8), channel_id=1, source_target_pairs={{0,8},{8,16},{16,24},{24,28},{28,20},{20,12},{12,4},{4,0},{1,9},{9... | collective-permute-start | bytes 688136 | tf_op jit(solution)/shard_map/ppermute | solution.py:65
  354.9 14.4 %collective-permute-start.60 = (bf16[64,1792]{1,0:T(8,128)(2,1)S(1)}, bf16[64,1792]{1,0:T(8,128)(2,1)S(1)}, u32[]{:S(2)}, u32[]{:S(2)}) collective-permute-start(bf16[64,1792]{1,0:T(8,128)(2,1)S(1)} %add_convert_fusion.13), channel_id=1, source_target_pairs={{0,8},{8,16},{16,24},{24,28},{28,20},{20,12},{12,4},{4,0},{1,9},{9... | collective-permute-start | bytes 688136 | tf_op jit(solution)/shard_map/ppermute | solution.py:65
  359.2 8.5 %collective-permute-start.95 = (bf16[64,1792]{1,0:T(8,128)(2,1)S(1)}, bf16[64,1792]{1,0:T(8,128)(2,1)S(1)}, u32[]{:S(2)}, u32[]{:S(2)}) collective-permute-start(bf16[64,1792]{1,0:T(8,128)(2,1)S(1)} %pad_maximum_fusion.10), channel_id=1, source_target_pairs={{0,8},{8,16},{16,24},{24,28},{28,20},{20,12},{12,4},{4,0},{1,9},{9... | collective-permute-start | bytes 688136 | tf_op jit(solution)/shard_map/ppermute | solution.py:65
  360.4 11.1 %collective-permute-start.99 = (bf16[64,1792]{1,0:T(8,128)(2,1)S(1)}, bf16[64,1792]{1,0:T(8,128)(2,1)S(1)}, u32[]{:S(2)}, u32[]{:S(2)}) collective-permute-start(bf16[64,1792]{1,0:T(8,128)(2,1)S(1)} %pad_maximum_fusion.11), channel_id=1, source_target_pairs={{8,0},{16,8},{24,16},{28,24},{20,28},{12,20},{4,12},{0,4},{9,1},{1... | collective-permute-start | bytes 688136 | tf_op jit(solution)/shard_map/ppermute | solution.py:65
  367.7 8.6 %collective-permute-start.96 = (bf16[64,1792]{1,0:T(8,128)(2,1)S(1)}, bf16[64,1792]{1,0:T(8,128)(2,1)S(1)}, u32[]{:S(2)}, u32[]{:S(2)}) collective-permute-start(bf16[64,1792]{1,0:T(8,128)(2,1)S(1)} %add_convert_fusion.8), channel_id=1, source_target_pairs={{0,8},{8,16},{16,24},{24,28},{28,20},{20,12},{12,4},{4,0},{1,9},{9... | collective-permute-start | bytes 688136 | tf_op jit(solution)/shard_map/ppermute | solution.py:65
  370.0 15.4 %collective-permute-start.61 = (bf16[64,1792]{1,0:T(8,128)(2,1)S(1)}, bf16[64,1792]{1,0:T(8,128)(2,1)S(1)}, u32[]{:S(2)}, u32[]{:S(2)}) collective-permute-start(bf16[64,1792]{1,0:T(8,128)(2,1)S(1)} %get-tuple-element.28), channel_id=1, source_target_pairs={{0,8},{8,16},{16,24},{24,28},{28,20},{20,12},{12,4},{4,0},{1,9},{9... | collective-permute-start | bytes 688136 | tf_op jit(solution)/shard_map/ppermute | solution.py:65
  376.4 8.6 %collective-permute-start.100 = (bf16[64,1792]{1,0:T(8,128)(2,1)S(1)}, bf16[64,1792]{1,0:T(8,128)(2,1)S(1)}, u32[]{:S(2)}, u32[]{:S(2)}) collective-permute-start(bf16[64,1792]{1,0:T(8,128)(2,1)S(1)} %get-tuple-element.37), channel_id=1, source_target_pairs={{8,0},{16,8},{24,16},{28,24},{20,28},{12,20},{4,12},{0,4},{9,1},{1... | collective-permute-start | bytes 688136 | tf_op jit(solution)/shard_map/ppermute | solution.py:65
  376.8 11.3 %collective-permute-start.65 = (bf16[64,1792]{1,0:T(8,128)(2,1)S(1)}, bf16[64,1792]{1,0:T(8,128)(2,1)S(1)}, u32[]{:S(2)}, u32[]{:S(2)}) collective-permute-start(bf16[64,1792]{1,0:T(8,128)(2,1)S(1)} %add_convert_fusion.10), channel_id=1, source_target_pairs={{8,0},{16,8},{24,16},{28,24},{20,28},{12,20},{4,12},{0,4},{9,1},{1... | collective-permute-start | bytes 688136 | tf_op jit(solution)/shard_map/ppermute | solution.py:65
  377.3 11.0 %collective-permute-start.97 = (bf16[64,1792]{1,0:T(8,128)(2,1)S(1)}, bf16[64,1792]{1,0:T(8,128)(2,1)S(1)}, u32[]{:S(2)}, u32[]{:S(2)}) collective-permute-start(bf16[64,1792]{1,0:T(8,128)(2,1)S(1)} %get-tuple-element.36), channel_id=1, source_target_pairs={{0,8},{8,16},{16,24},{24,28},{28,20},{20,12},{12,4},{4,0},{1,9},{9... | collective-permute-start | bytes 688136 | tf_op jit(solution)/shard_map/ppermute | solution.py:65
  (58 other events, 586.6 us)
where the time goes:
time: 400 us; the launch traced here: 392 us
  waiting for transfers between devices  190 us (48%)
  starting transfers between devices  109 us (27%)
  matrix products  62.2 us (16%)
  other arithmetic  14.8 us (4%)
  local copies, waits for them, and re-layouts  14.1 us (4%)
    ppermute x81, waiting for transfers between devices, send(): return lax.ppermute(block, self.axis, pairs)  182 us
    ppermute x81, starting transfers between devices, send(): return lax.ppermute(block, self.axis, pairs)  98.2 us
    dot_general x11, matrix products, dot32(): return jnp.dot(a, b, preferred_element_type=jnp.float32)  52.2 us
  transfers between devices with their start and end apart: 102, of which 48 were waited for; matrix products, arithmetic and copies ran while one was open for 19% of the time, Pallas kernels for 0%

commit v1 on v0

--- a/solution.py
+++ b/solution.py
@@ -8,6 +8,8 @@
 EPSILON = 1e-05
 NEGATIVE = -1e30
 PARTS = 2
+LAST = 3
+LAG = 2
 
 
 def quotient(value, size):
@@ -68,46 +70,96 @@
         return remainder(self.spot + offset % self.size, self.size) if offset % self.size else self.spot
 
     def reduce_scatter(self, take):
-        n, half = self.size, self.size // 2
-        if n == 1:
-            return take(0).astype(jnp.float32)
-        if n == 2:
-            got = self.send(take(1).astype(jnp.bfloat16), self.right)
-            return take(0).astype(jnp.float32) + got.astype(jnp.float32)
-        far = take(half).astype(jnp.bfloat16)
-        cut = far.shape[0] // 2
-        going_right = self.send(far[:cut], self.right).astype(jnp.float32)
-        going_left = self.send(far[cut:], self.left).astype(jnp.float32)
-        for step in range(half - 1, 0, -1):
-            one = take(step).astype(jnp.float32)
-            two = take(-step).astype(jnp.float32)
-            if step == half - 1:
-                one = jnp.concatenate([one[:cut] + going_right, one[cut:]], axis=0)
-                two = jnp.concatenate([two[:cut], two[cut:] + going_left], axis=0)
+        return SumWalk(self, take).run()
+
+    def all_gather(self, block):
+        return GatherWalk(self, block).run()
+
+
+class SumWalk:
+    def __init__(self, ring, take):
+        self.ring, self.take, self.done = ring, take, 0
+        self.steps = ring.size // 2
+        self.sent = self.got = ()
+
+    def step(self, after=()):
+        ring, take, half = self.ring, self.take, self.steps
+        self.done += 1
+        if ring.size == 2:
+            right, left = take(1).astype(jnp.bfloat16), None
+        elif self.done == 1:
+            far = take(half).astype(jnp.bfloat16)
+            self.cut = far.shape[0] // 2
+            right, left = far[: self.cut], far[self.cut :]
+        else:
+            place = half - self.done + 1
+            right = take(place).astype(jnp.float32)
+            left = take(-place).astype(jnp.float32)
+            going_right, going_left = (g.astype(jnp.float32) for g in self.got)
+            if self.done == 2:
+                cut = self.cut
+                right = jnp.concatenate([right[:cut] + going_right, right[cut:]], axis=0)
+                left = jnp.concatenate([left[:cut], left[cut:] + going_left], axis=0)
             else:
-                one = one + going_right
-                two = two + going_left
-            going_right = self.send(one.astype(jnp.bfloat16), self.right).astype(jnp.float32)
-            going_left = self.send(two.astype(jnp.bfloat16), self.left).astype(jnp.float32)
-        return take(0).astype(jnp.float32) + going_right + going_left
-
-    def all_gather(self, block):
-        n, half = self.size, self.size // 2
-        if n == 1:
-            return [(0, block)]
-        if n == 2:
-            return [(0, block), (1, self.send(block, self.right))]
-        found = [(0, block)]
-        from_left = from_right = block
-        for step in range(1, half):
-            from_left = self.send(from_left, self.right)
-            from_right = self.send(from_right, self.left)
-            found += [(-step, from_left), (step, from_right)]
-        cut = block.shape[0] // 2
-        far = jnp.concatenate(
-            [self.send(from_left[:cut], self.right), self.send(from_right[cut:], self.left)], axis=0
-        )
-        return found + [(half, far)]
+                right, left = right + going_right, left + going_left
+            right, left = right.astype(jnp.bfloat16), left.astype(jnp.bfloat16)
+        if left is None:
+            self.sent = (tie(right, *after),)
+            self.got = (ring.send(self.sent[0], ring.right),)
+        else:
+            self.sent = tie_all((right, left), after)
+            self.got = (ring.send(self.sent[0], ring.right), ring.send(self.sent[1], ring.left))
+
+    def result(self):
+        total = self.take(0).astype(jnp.float32)
+        for block in self.got:
+            total = total + block.astype(jnp.float32)
+        return total
+
+    def run(self):
+        while self.done < self.steps:
+            self.step()
+        return self.result()
+
+
+class GatherWalk:
+    def __init__(self, ring, block):
+        self.ring, self.done = ring, 0
+        self.steps = ring.size // 2
+        self.found = [(0, block)]
+        self.got = (block, block)
+
+    def step(self, after=()):
+        ring = self.ring
+        self.done += 1
+        if ring.size == 2:
+            self.got = (ring.send(tie(self.got[0], *after), ring.right),)
+            self.found.append((1, self.got[0]))
+            return
+        right, left = tie_all(self.got, after)
+        if self.done == self.steps:
+            cut = right.shape[0] // 2
+            right, left = right[:cut], left[cut:]
+        self.got = (ring.send(right, ring.right), ring.send(left, ring.left))
+        if self.done == self.steps:
+            self.found.append((self.done, jnp.concatenate(self.got, axis=0)))
+        else:
+            self.found += [(-self.done, self.got[0]), (self.done, self.got[1])]
+
+    def run(self):
+        while self.done < self.steps:
+            self.step()
+        return self.found
+
+
+def tie_all(blocks, earlier):
+    if len(blocks) + len(earlier) < 2:
+        return tuple(blocks)
+    return tuple(lax.optimization_barrier((*blocks, *earlier))[: len(blocks)])
+
+
+def tie(block, *earlier):
+    return tie_all((block,), earlier)[0]
 
 
 def place_blocks(shape, dtype, placed):
@@ -115,10 +167,6 @@
     for start, block in placed:
         buffer = lax.dynamic_update_slice(buffer, block, start, allow_negative_indices=False)
     return buffer
-
-
-def tie(block, *earlier):
-    return lax.optimization_barrier((block, *earlier))[0]
 
 
 def rotary_tables(token_positions):
@@ -191,11 +239,12 @@
         side = jnp.bitwise_xor(remainder(at_col, 2), core)
         return ((step * 2 + side) * per_col + remainder(who, per_col)) * m
 
-    def gather_cols(block, send_after=()):
+    def gather_cols(block, after=()):
         near = other_core(block)
-        found = sorted(lane_ring.all_gather(tie(block, *send_after) if send_after else block), key=lambda f: f[0] % lanes)
+        found = sorted(lane_ring.all_gather(block), key=lambda f: f[0] % lanes)
         pieces = [block, near]
         for _, b in found[1:]:
+            b = tie(b, *after)
             pieces += [b, other_core(b)]
         return jnp.concatenate(pieces, axis=0), found[-1][1]
 
@@ -205,8 +254,11 @@
         got = other_core(split[:, 1])
         return (split[:, 0].astype(jnp.float32) + got.astype(jnp.float32)).astype(jnp.bfloat16)
 
-    def lane_sum(summed):
-        return lane_ring.reduce_scatter(lambda i: summed[i % lanes])
+    def lane_walk(summed):
+        walk_on = SumWalk(lane_ring, lambda i: summed[i % lanes])
+        while walk_on.done < walk_on.steps:
+            walk_on.step()
+        return walk_on
 
     def row_blocks(block, m):
         def take(i):
@@ -215,16 +267,14 @@
 
         return take
 
-    def gather_rows(block, along, start_of, first_after=()):
-        m, w = block.shape
+    def lay_out(found, along, start_of):
+        m, w = found[0][1].shape
         shape = (rows * m, w) if along == 0 else (m, rows * w)
         placed = []
-        found = row_ring.all_gather(tie(block, *first_after) if first_after else block)
         for i, b in found:
             begin = start_of(row_at[i])
             placed.append(((begin, 0) if along == 0 else (0, begin), b))
-        late = tuple(b for _, b in found[-3:-1])
-        return place_blocks(shape, block.dtype, placed), late
+        return place_blocks(shape, found[0][1].dtype, placed)
 
     gathered, _ = gather_cols(residual)
     widened = gathered.astype(jnp.float32)
@@ -250,30 +300,44 @@
         ),
         axis=1,
     ).reshape(tokens)
-    bit = 1
-    while bit < rows:
-        sums = sums + lax.ppermute(sums, "row", [(i, i ^ bit) for i in range(rows)])
-        bit *= 2
-    attn_scale = lax.rsqrt(
-        cut_from(sums, (slot_of_row(row_place, row_tokens),), (row_tokens,)) / model_width
-        + EPSILON
-    )[:, None]
-
-    query_terms = dot32(scaled, w_query).astype(jnp.bfloat16)
-    kv_own = row_ring.reduce_scatter(row_blocks(kv_terms, row_tokens)) * attn_scale
-    key_own = rotary_apply(kv_own[:, :kv_cols].reshape(row_tokens, kv_local, HEAD_SIZE), tables)
-    key_value = jnp.concatenate([key_own.reshape(row_tokens, kv_cols), kv_own[:, kv_cols:]], axis=1)
-    found = row_ring.all_gather(key_value.astype(jnp.bfloat16))
-    key_value = jnp.concatenate([b for _, b in sorted(found, key=lambda f: f[0] % rows)], axis=0)
+    query_terms = dot32(tie(scaled, kv_terms), w_query).astype(jnp.bfloat16)
+    query_walk = SumWalk(row_ring, row_blocks(query_terms, row_tokens))
+    kv_walk = SumWalk(row_ring, row_blocks(kv_terms, row_tokens))
+    kv_spread, bit = None, 1
+    for step in range(query_walk.steps):
+        query_walk.step()
+        for turn in range(2):
+            after = query_walk.sent if step and not turn else ()
+            if kv_walk.done < kv_walk.steps:
+                kv_walk.step(after)
+                if bit < rows:
+                    got = lax.ppermute(sums, "row", [(i, i ^ bit) for i in range(rows)])
+                    sums = sums + tie(got, *kv_walk.got)
+                    bit *= 2
+                continue
+            if kv_spread is None:
+                attn_scale = lax.rsqrt(
+                    cut_from(sums, (slot_of_row(row_place, row_tokens),), (row_tokens,)) / model_width
+                    + EPSILON
+                )[:, None]
+                kv_own = kv_walk.result() * attn_scale
+                key_own = rotary_apply(
+                    kv_own[:, :kv_cols].reshape(row_tokens, kv_local, HEAD_SIZE), tables
+                ).reshape(row_tokens, kv_cols)
+                key_value = jnp.concatenate([key_own, kv_own[:, kv_cols:]], axis=1)
+                kv_spread = GatherWalk(row_ring, key_value.astype(jnp.bfloat16))
+            kv_spread.step(after)
+    found = sorted(kv_spread.run(), key=lambda f: f[0] % rows)
+    key_value = jnp.concatenate([b for _, b in found], axis=0)
     key_all, value_all = key_value[:, :kv_cols], key_value[:, kv_cols:]
     key_heads = key_all.reshape(tokens, kv_local, HEAD_SIZE)
     value_heads = value_all.reshape(tokens, kv_local, HEAD_SIZE)
 
-    queries = row_ring.reduce_scatter(row_blocks(query_terms, row_tokens)) * attn_scale
+    queries = query_walk.result() * attn_scale
     queries = rotary_apply(queries.reshape(row_tokens, heads, HEAD_SIZE), tables)
     queries = queries.astype(jnp.bfloat16)
 
-    def attend(part):
+    def attend(part, after=()):
         own = slice(part * row_part, (part + 1) * row_part)
         key_mask = (
             (key_segment[None, :] == own_segment[own][:, None])
@@ -283,7 +347,7 @@
             key_mask,
             jnp.einsum(
                 "tjgd,sjd->jgts",
-                queries[own].reshape(row_part, kv_local, group, HEAD_SIZE),
+                tie(queries[own], *after).reshape(row_part, kv_local, group, HEAD_SIZE),
                 key_heads,
                 preferred_element_type=jnp.float32,
             )
@@ -302,13 +366,16 @@
             .astype(jnp.bfloat16)
         )
 
-    def project(part, attended):
-        attn_out = lane_sum(core_sum(dot32(attended, w_out).astype(jnp.bfloat16)))
+    def head_sums(walk_on):
+        attended = lay_out(walk_on.found, 0, lambda who: slot_of_row(who, row_part))
+        return core_sum(dot32(attended, w_out).astype(jnp.bfloat16))
+
+    def add_stream(part, summed):
         own = residual.reshape(per_col, PARTS, row_part, row_width)[:, part]
-        own = own.reshape(col_part, row_width)
-        return (own.astype(jnp.float32) + attn_out).astype(jnp.bfloat16)
-
-    def spread(full_rows, before_core=()):
+        own = own.reshape(col_part, row_width).astype(jnp.float32)
+        return GatherWalk(row_ring, (own + lane_walk(summed).result()).astype(jnp.bfloat16))
+
+    def spread(full_rows):
         w = model_width // cols
         span = 2 * w
         mine = [(0, cut_from(full_rows, (0, lane * span), (col_part, span)))]
@@ -318,61 +385,128 @@
             ]
             sent = cut_from(full_rows, (0, lane_ring.at(hop) * span), (col_part, span))
             mine.append((-hop % lanes, lax.ppermute(sent, "col", pairs)))
+        return [b for _, b in sorted(mine, key=lambda f: f[0])]
+
+    def scale_of(blocks):
+        total = 0.0
+        for block in blocks:
+            block = block.astype(jnp.float32)
+            total = total + jnp.sum(block * block, axis=1)
+        return lax.rsqrt(total / model_width + EPSILON)[:, None]
+
+    def along_z(block, last_after):
+        up = [(z * 2 + x, (z + 1) % 4 * 2 + x) for z in range(4) for x in range(2)]
+        blocks = [block]
+        while len(blocks) < 4:
+            after = last_after if len(blocks) == LAST else ()
+            blocks.append(lax.ppermute(tie(blocks[-1], *after), "row", up))
+        return blocks
+
+    def to_takers(blocks):
+        z = quotient(row_place, 2)
+        here = [quotient(remainder(z - i + 4, 4), 2) == lane for i in range(2)]
+        given = [jnp.where(here[i], blocks[i + 2], blocks[i]) for i in range(2)]
+        kept = [jnp.where(here[i], blocks[i], blocks[i + 2]) for i in range(2)]
+        over = lax.ppermute(jnp.concatenate(given, axis=0), "col", [(i, i ^ 2) for i in range(cols)])
+        came = [over[:col_part], over[col_part:]]
+        first = remainder(jnp.bitwise_xor(z, core), 2) == 0
+        mine = [jnp.where(first, b[0], b[1]) for b in (kept, came)]
+        theirs = [jnp.where(first, b[1], b[0]) for b in (kept, came)]
+        near = other_core(jnp.concatenate(theirs, axis=0))
+        return jnp.concatenate([mine[0], near[:col_part], mine[1], near[col_part:]], axis=0)
+
+    def join_x(own, other):
+        x = remainder(row_place, 2)
+        return jnp.concatenate(
+            [jnp.where(x == 0, own, other), jnp.where(x == 0, other, own)], axis=1
+        )
+
+    def join_cores(mine, before_core):
+        w = model_width // cols
         pieces = []
-        for hop, b in sorted(mine, key=lambda f: f[0]):
+        for hop, b in enumerate(mine):
+            if hop:
+                b = tie(b, *before_core)
             sent = cut_from(b, (0, (1 - core) * w), (col_part, w))
-            if hop and before_core:
-                sent = tie(sent, *before_core)
             pieces += [cut_from(b, (0, core * w), (col_part, w)), other_core(sent)]
         return jnp.concatenate(pieces, axis=0)
 
-    def mlp_scale(full_rows):
-        full32 = full_rows.astype(jnp.float32)
-        return lax.rsqrt(jnp.sum(full32 * full32, axis=1) / model_width + EPSILON)[:, None]
-
     def widen(stream):
         mid = (stream.astype(jnp.float32) * mlp_gain[None, :]).astype(jnp.bfloat16)
-        return (
-            core_sum(dot32(mid, w_gate).astype(jnp.bfloat16)),
-            core_sum(dot32(mid, w_up).astype(jnp.bfloat16)),
-        )
-
-    def finish(hidden_all, stream):
-        down = dot32(hidden_all, w_down).astype(jnp.bfloat16)
-        mlp_out = row_ring.reduce_scatter(row_blocks(down, row_part))
+        mid = lax.optimization_barrier(mid)
+        gate = dot32(mid, w_gate).astype(jnp.bfloat16)
+        up = dot32(mid, w_up).astype(jnp.bfloat16)
+        return core_sum(gate), core_sum(up), (gate, up)
+
+    block_0 = attend(0)
+    heads_0 = GatherWalk(row_ring, block_0)
+    heads_0.step()
+    block_1 = attend(1, (block_0,))
+    heads_1 = GatherWalk(row_ring, block_1)
+    heads_0.step((block_1,))
+    steps = heads_0.steps
+    for step in range(2, steps):
+        heads_0.step()
+        heads_1.step(heads_0.found[-4][1:] if step == 2 else ())
+    summed_0 = head_sums(heads_0)
+    stream_0 = add_stream(0, summed_0)
+    while heads_1.done < steps:
+        heads_1.step((summed_0,) if heads_1.done == steps - 1 else ())
+    stream_0.step()
+    stream_0.step()
+    second = stream_0.got
+    full = lay_out(stream_0.run(), 1, lambda who: who * row_width)
+    scales = [scale_of([full])]
+    halves = spread(full)
+    stream_1 = add_stream(1, head_sums(heads_1))
+    if rows == 8 and cols == 4:
+        swap_x = [(i, i ^ 1) for i in range(rows)]
+        blocks = along_z(tie(stream_1.found[0][1], *second), halves[1:])
+        total = 0.0
+        for block in blocks:
+            block = block.astype(jnp.float32)
+            total = total + jnp.sum(block * block, axis=1)
+        total = total + lax.ppermute(total, "row", swap_x)
+        scales.append(lax.rsqrt(total / model_width + EPSILON)[:, None])
+        own = to_takers(blocks)
+        other = lax.ppermute(own, "row", swap_x)
+        stream_0 = join_cores(halves, ())
+        gate_0, up_0, terms_0 = widen(stream_0)
+        stream_1 = join_x(own, tie(other, *terms_0))
+    else:
+        stream_1.step(second)
+        full = lay_out(stream_1.run(), 1, lambda who: who * row_width)
+        scales.append(scale_of([full]))
+        stream_0 = join_cores(halves, ())
+        gate_0, up_0, terms_0 = widen(stream_0)
+        stream_1 = join_cores(spread(full), terms_0)
+
+    def gated(gate, up, scale):
+        return (jax.nn.silu(gate * scale) * (up * scale)).astype(jnp.bfloat16)
+
+    def down_walk(everyone):
+        down = dot32(everyone, w_down).astype(jnp.bfloat16)
+        return SumWalk(row_ring, row_blocks(down, row_part))
+
+    def finish(stream, walk_on):
         own = cut_from(stream, (slot_of_row(row_place, row_part), 0), (row_part, stream.shape[1]))
-        return (own.astype(jnp.float32) + mlp_out).astype(jnp.bfloat16)
-
-    def part_slot(who):
-        return slot_of_row(who, row_part)
-
-    parts = range(PARTS)
-    attended, late = [], ()
-    for part in parts:
-        got, late = gather_rows(attend(part), 0, part_slot, late)
-        attended.append(got)
-    full, late = [], ()
-    for part in parts:
-        got, late = gather_rows(project(part, attended[part]), 1, lambda who: who * row_width, late)
-        full.append(got)
-    streams, gates, ups, after = [], [], [], ()
-    for part in parts:
-        stream = spread(full[part], after)
-        gate, up = widen(tie(stream, *after) if after else stream)
-        streams.append(stream)
-        gates.append(gate)
-        ups.append(up)
-        after = (gate, up)
-    hidden, outs, after = [], [], ()
-    for part in parts:
-        scale = mlp_scale(full[part])
-        gate = lane_sum(gates[part]) * scale
-        up = lane_sum(tie(ups[part], *after) if after else ups[part]) * scale
-        own = (jax.nn.silu(gate) * up).astype(jnp.bfloat16)
-        everyone, far = gather_cols(own)
-        after = (far,)
-        outs.append(finish(everyone, streams[part]))
-    output = jnp.concatenate(outs, axis=0)
+        return (own.astype(jnp.float32) + walk_on.result()).astype(jnp.bfloat16)
+
+    gate_0, up_0 = lane_walk(gate_0), lane_walk(up_0)
+    gate_1, up_1, terms_1 = widen(tie(stream_1, *gate_0.got))
+    hidden_0 = gated(gate_0.result(), up_0.result(), scales[0])
+    everyone, far = gather_cols(tie(hidden_0, *terms_1))
+    gate_1, up_1 = lane_walk(tie(gate_1, far)), lane_walk(tie(up_1, far))
+    down_0 = down_walk(everyone)
+    while down_0.done < down_0.steps - 1:
+        down_0.step()
+    gate_1.got, up_1.got = tie_all(gate_1.got, down_0.got), tie_all(up_1.got, down_0.got)
+    gate_1, up_1 = gate_1.result(), up_1.result()
+    down_0.step()
+    everyone, far = gather_cols(gated(gate_1, up_1, scales[1]), down_0.got)
+    down_1 = down_walk(everyone)
+    down_1.run()
+    output = jnp.concatenate([finish(stream_0, down_0), finish(stream_1, down_1)], axis=0)
 
     block_count = page_table.shape[0]
     page_size = tokens // block_count

time: 400 us -> 386 us (0.965)
  starting transfers between devices: 109 us -> 92.2 us
  other arithmetic: 14.8 us -> 22.1 us
  local copies, waits for them, and re-layouts: 14.1 us -> 18.2 us
  waiting for transfers between devices: 190 us -> 186 us
    ppermute x81 -> x73, waiting for transfers between devices: 182 us -> 134 us  [send(): return lax.ppermute(block, self.axis, pairs)]
    ppermute x3 -> x9, waiting for transfers between devices: 1.91 us -> 37.5 us  [the longest x1 18.6 us: per_device(): other = lax.ppermute(own, 'row', swap_x)]
    ppermute x81 -> x73, starting transfers between devices: 98.2 us -> 77.9 us  [send(): return lax.ppermute(block, self.axis, pairs)]
    convert_element_type x16, other arithmetic: 2.73 us -> 9.39 us  [the longest x8 3.17 us: step(): right, left = (right.astype(jnp.bfloat16), left.astype(jnp.bfloat16))]
    ppermute x16 -> x15, waiting for transfers between devices: 0.8 us -> 6.15 us  [other_core(): return lax.ppermute(block, 'col', swap)]
    ppermute x3 -> x9, starting transfers between devices: 5.94 us -> 11.1 us  [the longest x3 5.08 us: per_device(): got = lax.ppermute(sums, 'row', [(i, i ^ bit) for i in range(rows)])]
    ppermute x2 -> x1, waiting for transfers between devices: 5.06 us -> 8.12 us  [spread(): mine.append((-hop % lanes, lax.ppermute(sent, 'col', pairs)))]
  transfers between devices with their start and end apart: 102 -> 98, of which waited for: 48 -> 57; matrix products, arithmetic and copies ran while one was open for 19% -> 19% of each run, Pallas kernels for 0% -> 0%
where the time goes in v1:
time: 386 us; the launch traced here: 379 us
  waiting for transfers between devices  186 us (48%)
  starting transfers between devices  92.2 us (24%)
  matrix products  58.7 us (15%)
  other arithmetic  22.1 us (6%)
  local copies, waits for them, and re-layouts  18.2 us (5%)
    ppermute x73, waiting for transfers between devices, send(): return lax.ppermute(block, self.axis, pairs)  134 us
    ppermute x73, starting transfers between devices, send(): return lax.ppermute(block, self.axis, pairs)  77.9 us
    dot_general x11, matrix products, dot32(): return jnp.dot(a, b, preferred_element_type=jnp.float32)  48.7 us
    ppermute x1, waiting for transfers between devices, per_device(): other = lax.ppermute(own, 'row', swap_x)  18.6 us
    ppermute x3, waiting for transfers between devices, along_z(): blocks.append(lax.ppermute(tie(blocks[-1], *after), 'row', up))  13.5 us
    ppermute x1, waiting for transfers between devices, spread(): mine.append((-hop % lanes, lax.ppermute(sent, 'col', pairs)))  8.12 us
  transfers between devices with their start and end apart: 98, of which 57 were waited for; matrix products, arithmetic and copies ran while one was open for 19% of the time, Pallas kernels for 0%

profile of v1, /device:TPU:0, one launch (start us, length us, event | category | flops | bytes accessed | tf_op | source)
XLA Modules:
  0.0 379.1 jit_solution(10296837596908416177)
XLA Ops:
  0.6 3.0 collective-permute-start.1
  3.7 10.8 %collective-permute-done.1 = bf16[256,896]{1,0:T(8,128)(2,1)} collective-permute-done((bf16[256,896]{1,0:T(8,128)(2,1)}, bf16[256,896]{1,0:T(8,128)(2,1)}, u32[]{:S(2)}, u32[]{:S(2)}) %collective-permute-start.1) | collective-permute-done | bytes 458784 | tf_op jit(solution)/shard_map/ppermute | solution.py:67
  14.6 1.8 fusion.69
  16.5 1.9 fusion.3
  20.6 1.9 collective-permute-start.3
  23.0 1.8 collective-permute-start.13
  24.8 4.1 %convolution_convert_fusion.4 = bf16[1024,1792]{1,0:T(8,128)(2,1)S(1)} fusion(bf16[1024,896]{1,0:T(8,128)(2,1)S(1)} %get-tuple-element.91, bf16[896,1792]{1,0:T(8,128)(2,1)S(1)} %copy-done), kind=kOutput, calls=%fused_computation.10 | convolution fusion | flops 3290169344 | bytes 8716288 | tf_op jit(solution)/shard_map/dot_general | solution.py:191
  29.0 1.6 collective-permute-start.7
  31.5 1.6 collective-permute-start.5
  33.8 5.1 %collective-permute-done.5 = bf16[128,512]{0,1:T(8,128)(2,1)S(1)} collective-permute-done((bf16[128,512]{0,1:T(8,128)(2,1)S(1)}, bf16[128,512]{0,1:T(8,128)(2,1)S(1)}, u32[]{:S(2)}, u32[]{:S(2)}) %collective-permute-start.5) | collective-permute-done | bytes 131104 | tf_op jit(solution)/shard_map/ppermute | solution.py:67
  40.5 1.6 collective-permute-start.9
  44.5 2.7 collective-permute-done.14
  47.2 1.7 collective-permute-start.15
  53.7 8.3 %collective-permute-done.11 = bf16[128,512]{0,1:T(8,128)(2,1)S(1)} collective-permute-done((bf16[128,512]{0,1:T(8,128)(2,1)S(1)}, bf16[128,512]{0,1:T(8,128)(2,1)S(1)}, u32[]{:S(2)}, u32[]{:S(2)}) %collective-permute-start.11) | collective-permute-done | bytes 131104 | tf_op jit(solution)/shard_map/ppermute | solution.py:67
  66.6 8.5 %collective-permute-done.18 = bf16[128,512]{0,1:T(8,128)(2,1)S(1)} collective-permute-done((bf16[128,512]{0,1:T(8,128)(2,1)S(1)}, bf16[128,512]{0,1:T(8,128)(2,1)S(1)}, u32[]{:S(2)}, u32[]{:S(2)}) %collective-permute-start.18) | collective-permute-done | bytes 131104 | tf_op jit(solution)/shard_map/ppermute | solution.py:67
  77.4 3.0 collective-permute-done.20
  80.4 2.3 collective-permute-done.21
  91.5 4.3 %collective-permute-done.27 = bf16[64,512]{0,1:T(8,128)(2,1)S(1)} collective-permute-done((bf16[64,512]{0,1:T(8,128)(2,1)S(1)}, bf16[64,512]{0,1:T(8,128)(2,1)S(1)}, u32[]{:S(2)}, u32[]{:S(2)}) %collective-permute-start.27) | collective-permute-done | bytes 65568 | tf_op jit(solution)/shard_map/ppermute | solution.py:67
  95.8 2.9 concatenate.95
  98.8 1.8 add_multiply_fusion
  101.8 2.9 convert_reduce_fusion.1
  104.6 2.1 fusion.41
  109.3 2.9 convert_reduce_fusion
  112.2 2.1 fusion.40
  119.1 3.5 collective-permute-done.32
  122.6 2.4 collective-permute-start.55
  125.1 2.0 collective-permute-start.34
  127.1 1.9 collective-permute-done.55
  129.0 2.0 collective-permute-done.56
  133.6 2.0 collective-permute-start.36
  135.7 3.2 collective-permute-done.37
  138.9 2.1 convolution_convert_fusion.8
  143.3 5.9 %collective-permute-done.59 = bf16[64,1792]{1,0:T(8,128)(2,1)S(1)} collective-permute-done((bf16[64,1792]{1,0:T(8,128)(2,1)S(1)}, bf16[64,1792]{1,0:T(8,128)(2,1)S(1)}, u32[]{:S(2)}, u32[]{:S(2)}) %collective-permute-start.59) | collective-permute-done | bytes 229408 | tf_op jit(solution)/shard_map/ppermute | solution.py:67
  156.0 2.1 convolution_convert_fusion.7
  161.6 3.8 %collective-permute-done.40 = bf16[128,896]{1,0:T(8,128)(2,1)S(1)} collective-permute-done((bf16[128,896]{1,0:T(8,128)(2,1)S(1)}, bf16[128,896]{1,0:T(8,128)(2,1)S(1)}, u32[]{:S(2)}, u32[]{:S(2)}) %collective-permute-start.40) | collective-permute-done | bytes 229408 | tf_op jit(solution)/shard_map/ppermute | solution.py:67
  179.0 3.3 collective-permute-done.44
  182.4 1.7 collective-permute-done.45
  186.2 3.0 collective-permute-done.65
  193.3 3.8 collective-permute-done.66
  197.2 8.1 %collective-permute-done.49 = bf16[128,3584]{1,0:T(8,128)(2,1)S(1)} collective-permute-done((bf16[128,3584]{1,0:T(8,128)(2,1)S(1)}, bf16[128,3584]{1,0:T(8,128)(2,1)S(1)}, u32[]{:S(2)}, u32[]{:S(2)}) %collective-permute-start.49) | collective-permute-done | bytes 917536 | tf_op jit(solution)/shard_map/ppermute | solution.py:387
  206.5 6.7 %collective-permute-done.67 = bf16[128,896]{1,0:T(8,128)(2,1)S(1)} collective-permute-done((bf16[128,896]{1,0:T(8,128)(2,1)S(1)}, bf16[128,896]{1,0:T(8,128)(2,1)S(1)}, u32[]{:S(2)}, u32[]{:S(2)}) %collective-permute-start.67) | collective-permute-done | bytes 229408 | tf_op jit(solution)/shard_map/ppermute | solution.py:402
  215.9 9.4 %convolution_convert_fusion.2 = bf16[512,2560]{1,0:T(8,128)(2,1)S(1)} fusion(bf16[512,1792]{1,0:T(8,128)(2,1)S(1)} %multiply_convert_fusion.1, bf16[1792,2560]{1,0:T(8,128)(2,1)} %param.22), kind=kOutput, calls=%fused_computation.8 | convolution fusion | flops 4698931200 | bytes 13631488 | tf_op jit(solution)/shard_map/dot_general | solution.py:191
  225.4 5.1 %convolution_convert_fusion.3 = bf16[512,2560]{1,0:T(8,128)(2,1)S(1)} fusion(bf16[512,1792]{1,0:T(8,128)(2,1)S(1)} %multiply_convert_fusion.1, bf16[1792,2560]{1,0:T(8,128)(2,1)S(1)} %bitcast.244), kind=kOutput, calls=%fused_computation.9 | convolution fusion | flops 4698931200 | bytes 13631488 | tf_op jit(solution)/shard_map/dot_general | solution.py:191
  231.5 2.8 collective-permute-done.69
  238.3 18.6 %collective-permute-done.70 = bf16[512,896]{1,0:T(8,128)(2,1)S(1)} collective-permute-done((bf16[512,896]{1,0:T(8,128)(2,1)S(1)}, bf16[512,896]{1,0:T(8,128)(2,1)S(1)}, u32[]{:S(2)}, u32[]{:S(2)}) %collective-permute-start.70) | collective-permute-done | bytes 917536 | tf_op jit(solution)/shard_map/ppermute | solution.py:472
  258.9 5.1 %convolution_convert_fusion = bf16[512,2560]{1,0:T(8,128)(2,1)S(1)} fusion(bf16[512,1792]{1,0:T(8,128)(2,1)S(1)} %multiply_convert_fusion, bf16[1792,2560]{1,0:T(8,128)(2,1)S(1)} %bitcast.242), kind=kOutput, calls=%fused_computation.6 | convolution fusion | flops 4698931200 | bytes 13631488 | tf_op jit(solution)/shard_map/dot_general | solution.py:191
  264.0 5.3 %convolution_convert_fusion.1 = bf16[512,2560]{1,0:T(8,128)(2,1)S(1)} fusion(bf16[512,1792]{1,0:T(8,128)(2,1)S(1)} %multiply_convert_fusion, bf16[1792,2560]{1,0:T(8,128)(2,1)S(1)} %bitcast.244), kind=kOutput, calls=%fused_computation.7 | convolution fusion | flops 4698931200 | bytes 13631488 | tf_op jit(solution)/shard_map/dot_general | solution.py:191
  271.4 15.9 %collective-permute-done.72 = bf16[128,2560]{1,0:T(8,128)(2,1)S(1)} collective-permute-done((bf16[128,2560]{1,0:T(8,128)(2,1)S(1)}, bf16[128,2560]{1,0:T(8,128)(2,1)S(1)}, u32[]{:S(2)}, u32[]{:S(2)}) %collective-permute-start.72) | collective-permute-done | bytes 655392 | tf_op jit(solution)/shard_map/ppermute | solution.py:67
  289.5 9.1 %convolution_convert_fusion.6 = bf16[512,1792]{1,0:T(8,128)(2,1)S(1)} fusion(bf16[2560,1792]{1,0:T(8,128)(2,1)} %param.23, bf16[128,2560]{1,0:T(8,128)(2,1)S(1)} %collective-permute-done.73, bf16[128,2560]{1,0:T(8,128)(2,1)S(1)} %collective-permute-done.72, bf16[128,2560]{1,0:T(8,128)(2,1)S(1)} %collective-permute-done.71, bf16[128,2560]{1,0:T(8,128)(2,1)S(1)} %fusion.36), kind=kOutput, calls=%fused_computation.23 | convolution fusion | flops 4709023744 | bytes 13631488 | tf_op jit(solution)/shard_map/dot_general | solution.py:191
  298.7 2.0 collective-permute-start.75
  301.0 3.0 collective-permute-done.74
  304.5 1.8 collective-permute-start.77
  306.9 4.4 %collective-permute-done.76 = bf16[64,1792]{1,0:T(8,128)(2,1)S(1)} collective-permute-done((bf16[64,1792]{1,0:T(8,128)(2,1)S(1)}, bf16[64,1792]{1,0:T(8,128)(2,1)S(1)}, u32[]{:S(2)}, u32[]{:S(2)}) %collective-permute-start.76) | collective-permute-done | bytes 229408 | tf_op jit(solution)/shard_map/ppermute | solution.py:67
  312.1 1.7 collective-permute-start.79
  315.2 2.7 collective-permute-done.84
  318.2 3.8 %collective-permute-done.83 = bf16[128,2560]{1,0:T(8,128)(2,1)S(1)} collective-permute-done((bf16[128,2560]{1,0:T(8,128)(2,1)S(1)}, bf16[128,2560]{1,0:T(8,128)(2,1)S(1)}, u32[]{:S(2)}, u32[]{:S(2)}) %collective-permute-start.83) | collective-permute-done | bytes 655392 | tf_op jit(solution)/shard_map/ppermute | solution.py:67
  325.4 4.0 %collective-permute-done.80 = bf16[64,1792]{1,0:T(8,128)(2,1)S(1)} collective-permute-done((bf16[64,1792]{1,0:T(8,128)(2,1)S(1)}, bf16[64,1792]{1,0:T(8,128)(2,1)S(1)}, u32[]{:S(2)}, u32[]{:S(2)}) %collective-permute-start.80) | collective-permute-done | bytes 229408 | tf_op jit(solution)/shard_map/ppermute | solution.py:67
  330.0 7.4 %collective-permute-done.88 = bf16[128,2560]{1,0:T(8,128)(2,1)S(1)} collective-permute-done((bf16[128,2560]{1,0:T(8,128)(2,1)S(1)}, bf16[128,2560]{1,0:T(8,128)(2,1)S(1)}, u32[]{:S(2)}, u32[]{:S(2)}) %collective-permute-start.88) | collective-permute-done | bytes 655392 | tf_op jit(solution)/shard_map/ppermute | solution.py:67
  337.4 2.0 collective-permute-done.89
  339.5 4.9 %convolution_convert_fusion.5 = bf16[512,1792]{1,0:T(8,128)(2,1)S(1)} fusion(bf16[2560,1792]{1,0:T(8,128)(2,1)S(1)} %bitcast.246, bf16[128,2560]{1,0:T(8,128)(2,1)S(1)} %collective-permute-done.89, bf16[128,2560]{1,0:T(8,128)(2,1)S(1)} %collective-permute-done.88, bf16[128,2560]{1,0:T(8,128)(2,1)S(1)} %collective-permute-done.87, ...), kind=kOutput, calls=%fused_computation.22 | convolution fusion | flops 4709023744 | bytes 13631488 | tf_op jit(solution)/shard_map/dot_general | solution.py:191
  354.1 1.7 collective-permute-start.93
  356.6 3.7 collective-permute-done.92
  363.9 3.8 %collective-permute-done.94 = bf16[64,1792]{1,0:T(8,128)(2,1)S(1)} collective-permute-done((bf16[64,1792]{1,0:T(8,128)(2,1)S(1)}, bf16[64,1792]{1,0:T(8,128)(2,1)S(1)}, u32[]{:S(2)}, u32[]{:S(2)}) %collective-permute-start.94) | collective-permute-done | bytes 229408 | tf_op jit(solution)/shard_map/ppermute | solution.py:67
  372.8 2.8 collective-permute-done.96
  (384 shorter events, 117.4 us)
Async XLA Ops:
  0.6 13.9 %collective-permute-start.1 = (bf16[256,896]{1,0:T(8,128)(2,1)}, bf16[256,896]{1,0:T(8,128)(2,1)}, u32[]{:S(2)}, u32[]{:S(2)}) collective-permute-start(bf16[256,896]{1,0:T(8,128)(2,1)} %param.14), channel_id=1, source_target_pairs={{0,2},{2,0},{1,3},{3,1},{4,6},{6,4},{5,7},{7,5},{8,10},{10,8},{9,1... | collective-permute-start | bytes 1376264 | tf_op jit(solution)/shard_map/ppermute | solution.py:67
  3.7 12.7 %collective-permute-start = (bf16[256,896]{1,0:T(8,128)(2,1)}, bf16[256,896]{1,0:T(8,128)(2,1)}, u32[]{:S(2)}, u32[]{:S(2)}) collective-permute-start(bf16[256,896]{1,0:T(8,128)(2,1)} %param.14), channel_id=1, source_target_pairs={{0,1},{1,0},{2,3},{3,2},{4,5},{5,4},{6,7},{7,6},{8,9},{9,8},{10,11... | collective-permute-start | bytes 1376264 | tf_op jit(solution)/shard_map/ppermute | solution.py:219
  20.6 10.5 %collective-permute-start.3 = (bf16[64,512]{0,1:T(8,128)(2,1)S(1)}, bf16[64,512]{0,1:T(8,128)(2,1)S(1)}, u32[]{:S(2)}, u32[]{:S(2)}) collective-permute-start(bf16[64,512]{0,1:T(8,128)(2,1)S(1)} %get-tuple-element.87), channel_id=1, source_target_pairs={{0,8},{8,16},{16,24},{24,28},{28,20},{20,12},{12,4},{4,0},{1,9},{9... | collective-permute-start | bytes 196616 | tf_op jit(solution)/shard_map/ppermute | solution.py:67
  22.5 8.8 %collective-permute-start.4 = (bf16[64,512]{0,1:T(8,128)(2,1)S(1)}, bf16[64,512]{0,1:T(8,128)(2,1)S(1)}, u32[]{:S(2)}, u32[]{:S(2)}) collective-permute-start(bf16[64,512]{0,1:T(8,128)(2,1)S(1)} %get-tuple-element.88), channel_id=1, source_target_pairs={{8,0},{16,8},{24,16},{28,24},{20,28},{12,20},{4,12},{0,4},{9,1},{1... | collective-permute-start | bytes 196616 | tf_op jit(solution)/shard_map/ppermute | solution.py:67
  23.0 19.7 %collective-permute-start.13 = (f32[1024]{0:T(1024)S(1)}, f32[1024]{0:T(1024)S(1)}, u32[]{:S(2)}, u32[]{:S(2)}) collective-permute-start(f32[1024]{0:T(1024)S(1)} %get-tuple-element.100), channel_id=1, source_target_pairs={{0,4},{4,0},{8,12},{12,8},{16,20},{20,16},{24,28},{28,24},{1,5},{5... | collective-permute-start | bytes 12296 | tf_op jit(solution)/shard_map/ppermute | solution.py:314
  29.0 11.3 %collective-permute-start.7 = (bf16[64,1792]{1,0:T(8,128)(2,1)S(1)}, bf16[64,1792]{1,0:T(8,128)(2,1)S(1)}, u32[]{:S(2)}, u32[]{:S(2)}) collective-permute-start(bf16[64,1792]{1,0:T(8,128)(2,1)S(1)} %get-tuple-element.92), channel_id=1, source_target_pairs={{0,8},{8,16},{16,24},{24,28},{28,20},{20,12},{12,4},{4,0},{1,9},{9... | collective-permute-start | bytes 688136 | tf_op jit(solution)/shard_map/ppermute | solution.py:67
  30.7 9.7 %collective-permute-start.8 = (bf16[64,1792]{1,0:T(8,128)(2,1)S(1)}, bf16[64,1792]{1,0:T(8,128)(2,1)S(1)}, u32[]{:S(2)}, u32[]{:S(2)}) collective-permute-start(bf16[64,1792]{1,0:T(8,128)(2,1)S(1)} %get-tuple-element.93), channel_id=1, source_target_pairs={{8,0},{16,8},{24,16},{28,24},{20,28},{12,20},{4,12},{0,4},{9,1},{1... | collective-permute-start | bytes 688136 | tf_op jit(solution)/shard_map/ppermute | solution.py:67
  31.5 7.4 %collective-permute-start.5 = (bf16[128,512]{0,1:T(8,128)(2,1)S(1)}, bf16[128,512]{0,1:T(8,128)(2,1)S(1)}, u32[]{:S(2)}, u32[]{:S(2)}) collective-permute-start(bf16[128,512]{0,1:T(8,128)(2,1)S(1)} %pad_maximum_fusion.15), channel_id=1, source_target_pairs={{0,8},{8,16},{16,24},{24,28},{28,20},{20,12},{12,4},{4,0},{1,9},{9... | collective-permute-start | bytes 393224 | tf_op jit(solution)/shard_map/ppermute | solution.py:67
  33.1 7.1 %collective-permute-start.6 = (bf16[128,512]{0,1:T(8,128)(2,1)S(1)}, bf16[128,512]{0,1:T(8,128)(2,1)S(1)}, u32[]{:S(2)}, u32[]{:S(2)}) collective-permute-start(bf16[128,512]{0,1:T(8,128)(2,1)S(1)} %pad_maximum_fusion.16), channel_id=1, source_target_pairs={{8,0},{16,8},{24,16},{28,24},{20,28},{12,20},{4,12},{0,4},{9,1},{1... | collective-permute-start | bytes 393224 | tf_op jit(solution)/shard_map/ppermute | solution.py:67
  40.5 10.4 %collective-permute-start.9 = (bf16[128,512]{0,1:T(8,128)(2,1)S(1)}, bf16[128,512]{0,1:T(8,128)(2,1)S(1)}, u32[]{:S(2)}, u32[]{:S(2)}) collective-permute-start(bf16[128,512]{0,1:T(8,128)(2,1)S(1)} %get-tuple-element.96), channel_id=1, source_target_pairs={{0,8},{8,16},{16,24},{24,28},{28,20},{20,12},{12,4},{4,0},{1,9},{9... | collective-permute-start | bytes 393224 | tf_op jit(solution)/shard_map/ppermute | solution.py:67
  42.2 8.8 %collective-permute-start.10 = (bf16[128,512]{0,1:T(8,128)(2,1)S(1)}, bf16[128,512]{0,1:T(8,128)(2,1)S(1)}, u32[]{:S(2)}, u32[]{:S(2)}) collective-permute-start(bf16[128,512]{0,1:T(8,128)(2,1)S(1)} %get-tuple-element.97), channel_id=1, source_target_pairs={{8,0},{16,8},{24,16},{28,24},{20,28},{12,20},{4,12},{0,4},{9,1},{1... | collective-permute-start | bytes 393224 | tf_op jit(solution)/shard_map/ppermute | solution.py:67
  47.2 6.5 %collective-permute-start.15 = (f32[1024]{0:T(1024)S(1)}, f32[1024]{0:T(1024)S(1)}, u32[]{:S(2)}, u32[]{:S(2)}) collective-permute-start(f32[1024]{0:T(1024)S(1)} %add.392), channel_id=1, source_target_pairs={{0,16},{4,20},{8,24},{12,28},{16,0},{20,4},{24,8},{28,12},{1,17},{... | collective-permute-start | bytes 12296 | tf_op jit(solution)/shard_map/ppermute | solution.py:314
  48.9 13.2 %collective-permute-start.16 = (bf16[128,1792]{1,0:T(8,128)(2,1)S(1)}, bf16[128,1792]{1,0:T(8,128)(2,1)S(1)}, u32[]{:S(2)}, u32[]{:S(2)}) collective-permute-start(bf16[128,1792]{1,0:T(8,128)(2,1)S(1)} %get-tuple-element.94), channel_id=1, source_target_pairs={{0,8},{8,16},{16,24},{24,28},{28,20},{20,12},{12,4},{4,0},{1,9},{9... | collective-permute-start | bytes 1376264 | tf_op jit(solution)/shard_map/ppermute | solution.py:67
  49.4 12.7 %collective-permute-start.17 = (bf16[128,1792]{1,0:T(8,128)(2,1)S(1)}, bf16[128,1792]{1,0:T(8,128)(2,1)S(1)}, u32[]{:S(2)}, u32[]{:S(2)}) collective-permute-start(bf16[128,1792]{1,0:T(8,128)(2,1)S(1)} %get-tuple-element.95), channel_id=1, source_target_pairs={{8,0},{16,8},{24,16},{28,24},{20,28},{12,20},{4,12},{0,4},{9,1},{1... | collective-permute-start | bytes 1376264 | tf_op jit(solution)/shard_map/ppermute | solution.py:67
  51.0 11.0 %collective-permute-start.11 = (bf16[128,512]{0,1:T(8,128)(2,1)S(1)}, bf16[128,512]{0,1:T(8,128)(2,1)S(1)}, u32[]{:S(2)}, u32[]{:S(2)}) collective-permute-start(bf16[128,512]{0,1:T(8,128)(2,1)S(1)} %get-tuple-element.98), channel_id=1, source_target_pairs={{0,8},{8,16},{16,24},{24,28},{28,20},{20,12},{12,4},{4,0},{1,9},{9... | collective-permute-start | bytes 393224 | tf_op jit(solution)/shard_map/ppermute | solution.py:67
  51.6 10.4 %collective-permute-start.12 = (bf16[128,512]{0,1:T(8,128)(2,1)S(1)}, bf16[128,512]{0,1:T(8,128)(2,1)S(1)}, u32[]{:S(2)}, u32[]{:S(2)}) collective-permute-start(bf16[128,512]{0,1:T(8,128)(2,1)S(1)} %get-tuple-element.99), channel_id=1, source_target_pairs={{8,0},{16,8},{24,16},{28,24},{20,28},{12,20},{4,12},{0,4},{9,1},{1... | collective-permute-start | bytes 393224 | tf_op jit(solution)/shard_map/ppermute | solution.py:67
  62.3 14.9 %collective-permute-start.22 = (bf16[128,1792]{1,0:T(8,128)(2,1)S(1)}, bf16[128,1792]{1,0:T(8,128)(2,1)S(1)}, u32[]{:S(2)}, u32[]{:S(2)}) collective-permute-start(bf16[128,1792]{1,0:T(8,128)(2,1)S(1)} %get-tuple-element.104), channel_id=1, source_target_pairs={{0,8},{8,16},{16,24},{24,28},{28,20},{20,12},{12,4},{4,0},{1,9},{9... | collective-permute-start | bytes 1376264 | tf_op jit(solution)/shard_map/ppermute | solution.py:67
  63.9 13.3 %collective-permute-start.23 = (bf16[128,1792]{1,0:T(8,128)(2,1)S(1)}, bf16[128,1792]{1,0:T(8,128)(2,1)S(1)}, u32[]{:S(2)}, u32[]{:S(2)}) collective-permute-start(bf16[128,1792]{1,0:T(8,128)(2,1)S(1)} %get-tuple-element.105), channel_id=1, source_target_pairs={{8,0},{16,8},{24,16},{28,24},{20,28},{12,20},{4,12},{0,4},{9,1},{1... | collective-permute-start | bytes 1376264 | tf_op jit(solution)/shard_map/ppermute | solution.py:67
  64.5 10.7 %collective-permute-start.18 = (bf16[128,512]{0,1:T(8,128)(2,1)S(1)}, bf16[128,512]{0,1:T(8,128)(2,1)S(1)}, u32[]{:S(2)}, u32[]{:S(2)}) collective-permute-start(bf16[128,512]{0,1:T(8,128)(2,1)S(1)} %pad_maximum_fusion.17), channel_id=1, source_target_pairs={{8,0},{16,8},{24,16},{28,24},{20,28},{12,20},{4,12},{0,4},{9,1},{1... | collective-permute-start | bytes 393224 | tf_op jit(solution)/shard_map/ppermute | solution.py:67
  65.8 9.4 %collective-permute-start.19 = (bf16[128,512]{0,1:T(8,128)(2,1)S(1)}, bf16[128,512]{0,1:T(8,128)(2,1)S(1)}, u32[]{:S(2)}, u32[]{:S(2)}) collective-permute-start(bf16[128,512]{0,1:T(8,128)(2,1)S(1)} %pad_maximum_fusion.17), channel_id=1, source_target_pairs={{0,8},{8,16},{16,24},{24,28},{28,20},{20,12},{12,4},{4,0},{1,9},{9... | collective-permute-start | bytes 393224 | tf_op jit(solution)/shard_map/ppermute | solution.py:67
  76.4 6.4 %collective-permute-start.21 = (bf16[128,512]{0,1:T(8,128)(2,1)S(1)}, bf16[128,512]{0,1:T(8,128)(2,1)S(1)}, u32[]{:S(2)}, u32[]{:S(2)}) collective-permute-start(bf16[128,512]{0,1:T(8,128)(2,1)S(1)} %collective-permute-done.19), channel_id=1, source_target_pairs={{0,8},{8,16},{16,24},{24,28},{28,20},{20,12},{12,4},{4,0},{1,9},{9... | collective-permute-start | bytes 393224 | tf_op jit(solution)/shard_map/ppermute | solution.py:67
  85.0 13.8 %collective-permute-start.28 = (bf16[128,1792]{1,0:T(8,128)(2,1)S(1)}, bf16[128,1792]{1,0:T(8,128)(2,1)}, u32[]{:S(2)}, u32[]{:S(2)}) collective-permute-start(bf16[128,1792]{1,0:T(8,128)(2,1)S(1)} %get-tuple-element.110), channel_id=1, source_target_pairs={{0,8},{8,16},{16,24},{24,28},{28,20},{20,12},{12,4},{4,0},{1,9},{9... | collective-permute-start | bytes 1376264 | tf_op jit(solution)/shard_map/ppermute | solution.py:67
  85.9 12.9 %collective-permute-start.29 = (bf16[128,1792]{1,0:T(8,128)(2,1)S(1)}, bf16[128,1792]{1,0:T(8,128)(2,1)}, u32[]{:S(2)}, u32[]{:S(2)}) collective-permute-start(bf16[128,1792]{1,0:T(8,128)(2,1)S(1)} %get-tuple-element.111), channel_id=1, source_target_pairs={{8,0},{16,8},{24,16},{28,24},{20,28},{12,20},{4,12},{0,4},{9,1},{1... | collective-permute-start | bytes 1376264 | tf_op jit(solution)/shard_map/ppermute | solution.py:67
  88.5 7.3 %collective-permute-start.27 = (bf16[64,512]{0,1:T(8,128)(2,1)S(1)}, bf16[64,512]{0,1:T(8,128)(2,1)S(1)}, u32[]{:S(2)}, u32[]{:S(2)}) collective-permute-start(bf16[64,512]{0,1:T(8,128)(2,1)S(1)} %slice.285), channel_id=1, source_target_pairs={{8,0},{16,8},{24,16},{28,24},{20,28},{12,20},{4,12},{0,4},{9,1},{1... | collective-permute-start | bytes 196616 | tf_op jit(solution)/shard_map/ppermute | solution.py:67
  89.3 6.5 %collective-permute-start.26 = (bf16[64,512]{0,1:T(8,128)(2,1)S(1)}, bf16[64,512]{0,1:T(8,128)(2,1)S(1)}, u32[]{:S(2)}, u32[]{:S(2)}) collective-permute-start(bf16[64,512]{0,1:T(8,128)(2,1)S(1)} %bitcast.238), channel_id=1, source_target_pairs={{0,8},{8,16},{16,24},{24,28},{28,20},{20,12},{12,4},{4,0},{1,9},{9... | collective-permute-start | bytes 196616 | tf_op jit(solution)/shard_map/ppermute | solution.py:67
  107.2 7.9 %collective-permute-start.30 = (bf16[64,1792]{1,0:T(8,128)(2,1)S(1)}, bf16[64,1792]{1,0:T(8,128)(2,1)}, u32[]{:S(2)}, u32[]{:S(2)}) collective-permute-start(bf16[64,1792]{1,0:T(8,128)(2,1)S(1)} %convert_element_type.523), channel_id=1, source_target_pairs={{0,8},{8,16},{16,24},{24,28},{28,20},{20,12},{12,4},{4,0},{1,9},{9... | collective-permute-start | bytes 688136 | tf_op jit(solution)/shard_map/ppermute | solution.py:67
  115.1 7.5 %collective-permute-start.32 = (bf16[64,1792]{1,0:T(8,128)(2,1)}, bf16[64,1792]{1,0:T(8,128)(2,1)S(1)}, u32[]{:S(2)}, u32[]{:S(2)}) collective-permute-start(bf16[64,1792]{1,0:T(8,128)(2,1)} %collective-permute-done.30), channel_id=1, source_target_pairs={{0,8},{8,16},{16,24},{24,28},{28,20},{20,12},{12,4},{4,0},{1,9},{9... | collective-permute-start | bytes 688136 | tf_op jit(solution)/shard_map/ppermute | solution.py:67
  116.6 8.4 %collective-permute-start.33 = (bf16[64,1792]{1,0:T(8,128)(2,1)}, bf16[64,1792]{1,0:T(8,128)(2,1)S(1)}, u32[]{:S(2)}, u32[]{:S(2)}) collective-permute-start(bf16[64,1792]{1,0:T(8,128)(2,1)} %collective-permute-done.31), channel_id=1, source_target_pairs={{8,0},{16,8},{24,16},{28,24},{20,28},{12,20},{4,12},{0,4},{9,1},{1... | collective-permute-start | bytes 688136 | tf_op jit(solution)/shard_map/ppermute | solution.py:67
  122.6 6.4 %collective-permute-start.55 = (bf16[64,1792]{1,0:T(8,128)(2,1)S(1)}, bf16[64,1792]{1,0:T(8,128)(2,1)S(1)}, u32[]{:S(2)}, u32[]{:S(2)}) collective-permute-start(bf16[64,1792]{1,0:T(8,128)(2,1)S(1)} %convert_element_type.527), channel_id=1, source_target_pairs={{0,8},{8,16},{16,24},{24,28},{28,20},{20,12},{12,4},{4,0},{1,9},{9... | collective-permute-start | bytes 688136 | tf_op jit(solution)/shard_map/ppermute | solution.py:67
  125.1 8.0 %collective-permute-start.34 = (bf16[64,1792]{1,0:T(8,128)(2,1)S(1)}, bf16[64,1792]{1,0:T(8,128)(2,1)S(1)}, u32[]{:S(2)}, u32[]{:S(2)}) collective-permute-start(bf16[64,1792]{1,0:T(8,128)(2,1)S(1)} %collective-permute-done.32), channel_id=1, source_target_pairs={{0,8},{8,16},{16,24},{24,28},{28,20},{20,12},{12,4},{4,0},{1,9},{9... | collective-permute-start | bytes 688136 | tf_op jit(solution)/shard_map/ppermute | solution.py:67
  127.0 6.4 %collective-permute-start.35 = (bf16[64,1792]{1,0:T(8,128)(2,1)S(1)}, bf16[64,1792]{1,0:T(8,128)(2,1)S(1)}, u32[]{:S(2)}, u32[]{:S(2)}) collective-permute-start(bf16[64,1792]{1,0:T(8,128)(2,1)S(1)} %collective-permute-done.33), channel_id=1, source_target_pairs={{8,0},{16,8},{24,16},{28,24},{20,28},{12,20},{4,12},{0,4},{9,1},{1... | collective-permute-start | bytes 688136 | tf_op jit(solution)/shard_map/ppermute | solution.py:67
  131.0 10.1 %collective-permute-start.57 = (bf16[64,1792]{1,0:T(8,128)(2,1)S(1)}, bf16[64,1792]{1,0:T(8,128)(2,1)S(1)}, u32[]{:S(2)}, u32[]{:S(2)}) collective-permute-start(bf16[64,1792]{1,0:T(8,128)(2,1)S(1)} %collective-permute-done.55), channel_id=1, source_target_pairs={{0,8},{8,16},{16,24},{24,28},{28,20},{20,12},{12,4},{4,0},{1,9},{9... | collective-permute-start | bytes 688136 | tf_op jit(solution)/shard_map/ppermute | solution.py:67
  131.6 9.5 %collective-permute-start.58 = (bf16[64,1792]{1,0:T(8,128)(2,1)S(1)}, bf16[64,1792]{1,0:T(8,128)(2,1)S(1)}, u32[]{:S(2)}, u32[]{:S(2)}) collective-permute-start(bf16[64,1792]{1,0:T(8,128)(2,1)S(1)} %collective-permute-done.56), channel_id=1, source_target_pairs={{8,0},{16,8},{24,16},{28,24},{20,28},{12,20},{4,12},{0,4},{9,1},{1... | collective-permute-start | bytes 688136 | tf_op jit(solution)/shard_map/ppermute | solution.py:67
  141.0 9.3 %collective-permute-start.38 = (bf16[2,128,896]{2,1,0:T(8,128)(2,1)S(1)}, bf16[2,128,896]{2,1,0:T(8,128)(2,1)S(1)}, u32[]{:S(2)}, u32[]{:S(2)}) collective-permute-start(bf16[2,128,896]{2,1,0:T(8,128)(2,1)S(1)} %slice_bitcast_fusion.16), channel_id=1, source_target_pairs={{0,1},{1,0},{2,3},{3,2},{4,5},{5,4},{6,7},{7,6},{8,9},{9,8},{10,11... | collective-permute-start | bytes 1376264 | tf_op jit(solution)/shard_map/ppermute | solution.py:219
  141.1 8.0 %collective-permute-start.59 = (bf16[64,1792]{1,0:T(8,128)(2,1)S(1)}, bf16[64,1792]{1,0:T(8,128)(2,1)S(1)}, u32[]{:S(2)}, u32[]{:S(2)}) collective-permute-start(bf16[64,1792]{1,0:T(8,128)(2,1)S(1)} %collective-permute-done.57), channel_id=1, source_target_pairs={{0,8},{8,16},{16,24},{24,28},{28,20},{20,12},{12,4},{4,0},{1,9},{9... | collective-permute-start | bytes 688136 | tf_op jit(solution)/shard_map/ppermute | solution.py:67
  142.7 7.7 %collective-permute-start.60 = (bf16[64,1792]{1,0:T(8,128)(2,1)S(1)}, bf16[64,1792]{1,0:T(8,128)(2,1)S(1)}, u32[]{:S(2)}, u32[]{:S(2)}) collective-permute-start(bf16[64,1792]{1,0:T(8,128)(2,1)S(1)} %collective-permute-done.58), channel_id=1, source_target_pairs={{8,0},{16,8},{24,16},{28,24},{20,28},{12,20},{4,12},{0,4},{9,1},{1... | collective-permute-start | bytes 688136 | tf_op jit(solution)/shard_map/ppermute | solution.py:67
  161.5 9.0 %collective-permute-start.63 = (bf16[2,128,896]{2,1,0:T(8,128)(2,1)S(1)}, bf16[2,128,896]{2,1,0:T(8,128)(2,1)S(1)}, u32[]{:S(2)}, u32[]{:S(2)}) collective-permute-start(bf16[2,128,896]{2,1,0:T(8,128)(2,1)S(1)} %slice_bitcast_fusion.14), channel_id=1, source_target_pairs={{0,1},{1,0},{2,3},{3,2},{4,5},{5,4},{6,7},{7,6},{8,9},{9,8},{10,11... | collective-permute-start | bytes 1376264 | tf_op jit(solution)/shard_map/ppermute | solution.py:219
  167.0 7.4 %collective-permute-start.42 = (bf16[128,896]{1,0:T(8,128)(2,1)S(1)}, bf16[128,896]{1,0:T(8,128)(2,1)S(1)}, u32[]{:S(2)}, u32[]{:S(2)}) collective-permute-start(bf16[128,896]{1,0:T(8,128)(2,1)S(1)} %collective-permute-done.40), channel_id=1, source_target_pairs={{0,8},{8,16},{16,24},{24,28},{28,20},{20,12},{12,4},{4,0},{1,9},{9... | collective-permute-start | bytes 688136 | tf_op jit(solution)/shard_map/ppermute | solution.py:67
  168.1 7.4 %collective-permute-start.43 = (bf16[128,896]{1,0:T(8,128)(2,1)}, bf16[128,896]{1,0:T(8,128)(2,1)S(1)}, u32[]{:S(2)}, u32[]{:S(2)}) collective-permute-start(bf16[128,896]{1,0:T(8,128)(2,1)} %collective-permute-done.41), channel_id=1, source_target_pairs={{8,0},{16,8},{24,16},{28,24},{20,28},{12,20},{4,12},{0,4},{9,1},{1... | collective-permute-start | bytes 688136 | tf_op jit(solution)/shard_map/ppermute | solution.py:67
  175.5 6.8 %collective-permute-start.44 = (bf16[128,896]{1,0:T(8,128)(2,1)S(1)}, bf16[128,896]{1,0:T(8,128)(2,1)S(1)}, u32[]{:S(2)}, u32[]{:S(2)}) collective-permute-start(bf16[128,896]{1,0:T(8,128)(2,1)S(1)} %collective-permute-done.42), channel_id=1, source_target_pairs={{0,8},{8,16},{16,24},{24,28},{28,20},{20,12},{12,4},{4,0},{1,9},{9... | collective-permute-start | bytes 688136 | tf_op jit(solution)/shard_map/ppermute | solution.py:67
  176.6 7.4 %collective-permute-start.45 = (bf16[128,896]{1,0:T(8,128)(2,1)S(1)}, bf16[128,896]{1,0:T(8,128)(2,1)S(1)}, u32[]{:S(2)}, u32[]{:S(2)}) collective-permute-start(bf16[128,896]{1,0:T(8,128)(2,1)S(1)} %collective-permute-done.43), channel_id=1, source_target_pairs={{8,0},{16,8},{24,16},{28,24},{20,28},{12,20},{4,12},{0,4},{9,1},{1... | collective-permute-start | bytes 688136 | tf_op jit(solution)/shard_map/ppermute | solution.py:67
  177.9 11.4 %collective-permute-start.65 = (bf16[128,896]{1,0:T(8,128)(2,1)S(1)}, bf16[128,896]{1,0:T(8,128)(2,1)S(1)}, u32[]{:S(2)}, u32[]{:S(2)}) collective-permute-start(bf16[128,896]{1,0:T(8,128)(2,1)S(1)} %fusion.45), channel_id=1, source_target_pairs={{0,8},{4,12},{8,16},{12,20},{16,24},{20,28},{24,0},{28,4},{1,9},{5... | collective-permute-start | bytes 688136 | tf_op jit(solution)/shard_map/ppermute | solution.py:402
  184.1 6.5 %collective-permute-start.47 = (bf16[64,896]{1,0:T(8,128)(2,1)S(1)}, bf16[64,896]{1,0:T(8,128)(2,1)S(1)}, u32[]{:S(2)}, u32[]{:S(2)}) collective-permute-start(bf16[64,896]{1,0:T(8,128)(2,1)S(1)} %slice.301), channel_id=1, source_target_pairs={{8,0},{16,8},{24,16},{28,24},{20,28},{12,20},{4,12},{0,4},{9,1},{1... | collective-permute-start | bytes 344072 | tf_op jit(solution)/shard_map/ppermute | solution.py:67
  189.3 7.8 %collective-permute-start.66 = (bf16[128,896]{1,0:T(8,128)(2,1)S(1)}, bf16[128,896]{1,0:T(8,128)(2,1)S(1)}, u32[]{:S(2)}, u32[]{:S(2)}) collective-permute-start(bf16[128,896]{1,0:T(8,128)(2,1)S(1)} %collective-permute-done.65), channel_id=1, source_target_pairs={{0,8},{4,12},{8,16},{12,20},{16,24},{20,28},{24,0},{28,4},{1,9},{5... | collective-permute-start | bytes 688136 | tf_op jit(solution)/shard_map/ppermute | solution.py:402
  190.7 14.6 %collective-permute-start.49 = (bf16[128,3584]{1,0:T(8,128)(2,1)S(1)}, bf16[128,3584]{1,0:T(8,128)(2,1)S(1)}, u32[]{:S(2)}, u32[]{:S(2)}) collective-permute-start(bf16[128,3584]{1,0:T(8,128)(2,1)S(1)} %constant_dynamic-slice_fusion.8), channel_id=1, source_target_pairs={{0,2},{1,3},{2,0},{3,1},{4,6},{5,7},{6,4},{7,5},{8,10},{9,11},{10,... | collective-permute-start | bytes 2752520 | tf_op jit(solution)/shard_map/ppermute | solution.py:387
  193.2 21.8 %collective-permute-start.48 = (bf16[128,1792]{1,0:T(8,128)(2,1)S(1)}, bf16[128,1792]{1,0:T(8,128)(2,1)S(1)}, u32[]{:S(2)}, u32[]{:S(2)}) collective-permute-start(bf16[128,1792]{1,0:T(8,128)(2,1)S(1)} %get-tuple-element.201), channel_id=1, source_target_pairs={{0,1},{1,0},{2,3},{3,2},{4,5},{5,4},{6,7},{7,6},{8,9},{9,8},{10,11... | collective-permute-start | bytes 1376264 | tf_op jit(solution)/shard_map/ppermute | solution.py:219
  205.3 7.8 %collective-permute-start.67 = (bf16[128,896]{1,0:T(8,128)(2,1)S(1)}, bf16[128,896]{1,0:T(8,128)(2,1)S(1)}, u32[]{:S(2)}, u32[]{:S(2)}) collective-permute-start(bf16[128,896]{1,0:T(8,128)(2,1)S(1)} %collective-permute-done.66), channel_id=1, source_target_pairs={{0,8},{4,12},{8,16},{12,20},{16,24},{20,28},{24,0},{28,4},{1,9},{5... | collective-permute-start | bytes 688136 | tf_op jit(solution)/shard_map/ppermute | solution.py:402
  206.4 8.6 %collective-permute-start.50 = (bf16[128,1792]{1,0:T(8,128)(2,1)S(1)}, bf16[128,1792]{1,0:T(8,128)(2,1)S(1)}, u32[]{:S(2)}, u32[]{:S(2)}) collective-permute-start(bf16[128,1792]{1,0:T(8,128)(2,1)S(1)} %get-tuple-element.216), channel_id=1, source_target_pairs={{0,1},{1,0},{2,3},{3,2},{4,5},{5,4},{6,7},{7,6},{8,9},{9,8},{10,11... | collective-permute-start | bytes 1376264 | tf_op jit(solution)/shard_map/ppermute | solution.py:219
  213.3 17.4 %collective-permute-start.68 = (bf16[256,896]{1,0:T(8,128)(2,1)S(1)}, bf16[256,896]{1,0:T(8,128)(2,1)S(1)}, u32[]{:S(2)}, u32[]{:S(2)}) collective-permute-start(bf16[256,896]{1,0:T(8,128)(2,1)S(1)} %pad_maximum_fusion.8), channel_id=1, source_target_pairs={{0,2},{1,3},{2,0},{3,1},{4,6},{5,7},{6,4},{7,5},{8,10},{9,11},{10,... | collective-permute-start | bytes 1376264 | tf_op jit(solution)/shard_map/ppermute | solution.py:410
  234.5 22.5 %collective-permute-start.70 = (bf16[512,896]{1,0:T(8,128)(2,1)S(1)}, bf16[512,896]{1,0:T(8,128)(2,1)S(1)}, u32[]{:S(2)}, u32[]{:S(2)}) collective-permute-start(bf16[512,896]{1,0:T(8,128)(2,1)S(1)} %pad_maximum_fusion.4), channel_id=1, source_target_pairs={{0,4},{4,0},{8,12},{12,8},{16,20},{20,16},{24,28},{28,24},{1,5},{5... | collective-permute-start | bytes 2752520 | tf_op jit(solution)/shard_map/ppermute | solution.py:472
  235.8 22.8 %collective-permute-start.52 = (bf16[128,2560]{1,0:T(8,128)(2,1)S(1)}, bf16[128,2560]{1,0:T(8,128)(2,1)S(1)}, u32[]{:S(2)}, u32[]{:S(2)}) collective-permute-start(bf16[128,2560]{1,0:T(8,128)(2,1)S(1)} %slice_bitcast_fusion.10), channel_id=1, source_target_pairs={{0,2},{2,0},{1,3},{3,1},{4,6},{6,4},{5,7},{7,5},{8,10},{10,8},{9,1... | collective-permute-start | bytes 1966088 | tf_op jit(solution)/shard_map/ppermute | solution.py:67
  236.8 32.7 %collective-permute-start.54 = (bf16[128,2560]{1,0:T(8,128)(2,1)S(1)}, bf16[128,2560]{1,0:T(8,128)(2,1)S(1)}, u32[]{:S(2)}, u32[]{:S(2)}) collective-permute-start(bf16[128,2560]{1,0:T(8,128)(2,1)S(1)} %slice_bitcast_fusion.8), channel_id=1, source_target_pairs={{0,2},{2,0},{1,3},{3,1},{4,6},{6,4},{5,7},{7,5},{8,10},{10,8},{9,1... | collective-permute-start | bytes 1966088 | tf_op jit(solution)/shard_map/ppermute | solution.py:67
  269.4 18.0 %collective-permute-start.85 = (bf16[2,128,2560]{2,1,0:T(8,128)(2,1)S(1)}, bf16[2,128,2560]{2,1,0:T(8,128)(2,1)S(1)}, u32[]{:S(2)}, u32[]{:S(2)}) collective-permute-start(bf16[2,128,2560]{2,1,0:T(8,128)(2,1)S(1)} %slice_bitcast_fusion), channel_id=1, source_target_pairs={{0,1},{1,0},{2,3},{3,2},{4,5},{5,4},{6,7},{7,6},{8,9},{9,8},{10,11... | collective-permute-start | bytes 3932168 | tf_op jit(solution)/shard_map/ppermute | solution.py:219
  270.2 17.2 %collective-permute-start.72 = (bf16[128,2560]{1,0:T(8,128)(2,1)S(1)}, bf16[128,2560]{1,0:T(8,128)(2,1)S(1)}, u32[]{:S(2)}, u32[]{:S(2)}) collective-permute-start(bf16[128,2560]{1,0:T(8,128)(2,1)S(1)} %fusion.36), channel_id=1, source_target_pairs={{0,2},{2,0},{1,3},{3,1},{4,6},{6,4},{5,7},{7,5},{8,10},{10,8},{9,1... | collective-permute-start | bytes 1966088 | tf_op jit(solution)/shard_map/ppermute | solution.py:67
  270.7 17.6 %collective-permute-start.71 = (bf16[128,2560]{1,0:T(8,128)(2,1)S(1)}, bf16[128,2560]{1,0:T(8,128)(2,1)S(1)}, u32[]{:S(2)}, u32[]{:S(2)}) collective-permute-start(bf16[128,2560]{1,0:T(8,128)(2,1)S(1)} %fusion.36), channel_id=1, source_target_pairs={{0,1},{1,0},{2,3},{3,2},{4,5},{5,4},{6,7},{7,6},{8,9},{9,8},{10,11... | collective-permute-start | bytes 1966088 | tf_op jit(solution)/shard_map/ppermute | solution.py:219
  271.0 29.6 %collective-permute-start.82 = (bf16[2,128,2560]{2,1,0:T(8,128)(2,1)S(1)}, bf16[2,128,2560]{2,1,0:T(8,128)(2,1)S(1)}, u32[]{:S(2)}, u32[]{:S(2)}) collective-permute-start(bf16[2,128,2560]{2,1,0:T(8,128)(2,1)S(1)} %slice_bitcast_fusion.2), channel_id=1, source_target_pairs={{0,1},{1,0},{2,3},{3,2},{4,5},{5,4},{6,7},{7,6},{8,9},{9,8},{10,11... | collective-permute-start | bytes 3932168 | tf_op jit(solution)/shard_map/ppermute | solution.py:219
  287.8 30.4 %collective-permute-start.86 = (bf16[128,2560]{1,0:T(8,128)(2,1)S(1)}, bf16[128,2560]{1,0:T(8,128)(2,1)S(1)}, u32[]{:S(2)}, u32[]{:S(2)}) collective-permute-start(bf16[128,2560]{1,0:T(8,128)(2,1)S(1)} %slice_bitcast_fusion.12), channel_id=1, source_target_pairs={{0,2},{2,0},{1,3},{3,1},{4,6},{6,4},{5,7},{7,5},{8,10},{10,8},{9,1... | collective-permute-start | bytes 1966088 | tf_op jit(solution)/shard_map/ppermute | solution.py:67
  304.2 7.1 %collective-permute-start.76 = (bf16[64,1792]{1,0:T(8,128)(2,1)S(1)}, bf16[64,1792]{1,0:T(8,128)(2,1)S(1)}, u32[]{:S(2)}, u32[]{:S(2)}) collective-permute-start(bf16[64,1792]{1,0:T(8,128)(2,1)S(1)} %pad_maximum_fusion.11), channel_id=1, source_target_pairs={{0,8},{8,16},{16,24},{24,28},{28,20},{20,12},{12,4},{4,0},{1,9},{9... | collective-permute-start | bytes 688136 | tf_op jit(solution)/shard_map/ppermute | solution.py:67
  304.5 7.1 %collective-permute-start.77 = (bf16[64,1792]{1,0:T(8,128)(2,1)S(1)}, bf16[64,1792]{1,0:T(8,128)(2,1)S(1)}, u32[]{:S(2)}, u32[]{:S(2)}) collective-permute-start(bf16[64,1792]{1,0:T(8,128)(2,1)S(1)} %pad_maximum_fusion.12), channel_id=1, source_target_pairs={{8,0},{16,8},{24,16},{28,24},{20,28},{12,20},{4,12},{0,4},{9,1},{1... | collective-permute-start | bytes 688136 | tf_op jit(solution)/shard_map/ppermute | solution.py:67
  306.3 15.6 %collective-permute-start.83 = (bf16[128,2560]{1,0:T(8,128)(2,1)S(1)}, bf16[128,2560]{1,0:T(8,128)(2,1)S(1)}, u32[]{:S(2)}, u32[]{:S(2)}) collective-permute-start(bf16[128,2560]{1,0:T(8,128)(2,1)S(1)} %slice_bitcast_fusion.13), channel_id=1, source_target_pairs={{0,2},{2,0},{1,3},{3,1},{4,6},{6,4},{5,7},{7,5},{8,10},{10,8},{9,1... | collective-permute-start | bytes 1966088 | tf_op jit(solution)/shard_map/ppermute | solution.py:67
  322.6 14.7 %collective-permute-start.88 = (bf16[128,2560]{1,0:T(8,128)(2,1)S(1)}, bf16[128,2560]{1,0:T(8,128)(2,1)S(1)}, u32[]{:S(2)}, u32[]{:S(2)}) collective-permute-start(bf16[128,2560]{1,0:T(8,128)(2,1)S(1)} %fusion.32), channel_id=1, source_target_pairs={{0,2},{2,0},{1,3},{3,1},{4,6},{6,4},{5,7},{7,5},{8,10},{10,8},{9,1... | collective-permute-start | bytes 1966088 | tf_op jit(solution)/shard_map/ppermute | solution.py:67
  325.4 12.0 %collective-permute-start.87 = (bf16[128,2560]{1,0:T(8,128)(2,1)S(1)}, bf16[128,2560]{1,0:T(8,128)(2,1)S(1)}, u32[]{:S(2)}, u32[]{:S(2)}) collective-permute-start(bf16[128,2560]{1,0:T(8,128)(2,1)S(1)} %fusion.32), channel_id=1, source_target_pairs={{0,1},{1,0},{2,3},{3,2},{4,5},{5,4},{6,7},{7,6},{8,9},{9,8},{10,11... | collective-permute-start | bytes 1966088 | tf_op jit(solution)/shard_map/ppermute | solution.py:219
  353.8 6.5 %collective-permute-start.92 = (bf16[64,1792]{1,0:T(8,128)(2,1)S(1)}, bf16[64,1792]{1,0:T(8,128)(2,1)S(1)}, u32[]{:S(2)}, u32[]{:S(2)}) collective-permute-start(bf16[64,1792]{1,0:T(8,128)(2,1)S(1)} %pad_maximum_fusion.13), channel_id=1, source_target_pairs={{0,8},{8,16},{16,24},{24,28},{28,20},{20,12},{12,4},{4,0},{1,9},{9... | collective-permute-start | bytes 688136 | tf_op jit(solution)/shard_map/ppermute | solution.py:67
  354.1 6.4 %collective-permute-start.93 = (bf16[64,1792]{1,0:T(8,128)(2,1)S(1)}, bf16[64,1792]{1,0:T(8,128)(2,1)S(1)}, u32[]{:S(2)}, u32[]{:S(2)}) collective-permute-start(bf16[64,1792]{1,0:T(8,128)(2,1)S(1)} %pad_maximum_fusion.14), channel_id=1, source_target_pairs={{8,0},{16,8},{24,16},{28,24},{20,28},{12,20},{4,12},{0,4},{9,1},{1... | collective-permute-start | bytes 688136 | tf_op jit(solution)/shard_map/ppermute | solution.py:67
  (75 other events, 749.3 us)

commit v2 on v1

--- a/solution.py
+++ b/solution.py
@@ -307,7 +307,7 @@
     for step in range(query_walk.steps):
         query_walk.step()
         for turn in range(2):
-            after = query_walk.sent if step and not turn else ()
+            after = ()
             if kv_walk.done < kv_walk.steps:
                 kv_walk.step(after)
                 if bit < rows:
@@ -495,7 +495,7 @@
     gate_0, up_0 = lane_walk(gate_0), lane_walk(up_0)
     gate_1, up_1, terms_1 = widen(tie(stream_1, *gate_0.got))
     hidden_0 = gated(gate_0.result(), up_0.result(), scales[0])
-    everyone, far = gather_cols(tie(hidden_0, *terms_1))
+    everyone, far = gather_cols(hidden_0, terms_1)
     gate_1, up_1 = lane_walk(tie(gate_1, far)), lane_walk(tie(up_1, far))
     down_0 = down_walk(everyone)
     while down_0.done < down_0.steps - 1:

time: 386 us -> 376 us (0.974)
  waiting for transfers between devices: 186 us -> 172 us
    ppermute x73, waiting for transfers between devices: 134 us -> 128 us  [send(): return lax.ppermute(block, self.axis, pairs)]
  transfers between devices with their start and end apart: 98 -> 98, of which waited for: 57 -> 61; matrix products, arithmetic and copies ran while one was open for 19% -> 19% of each run, Pallas kernels for 0% -> 0%
where the time goes in v2:
time: 376 us; the launch traced here: 369 us
  waiting for transfers between devices  172 us (46%)
  starting transfers between devices  94.1 us (25%)
  matrix products  59.3 us (16%)
  other arithmetic  21.9 us (6%)
  local copies, waits for them, and re-layouts  20.2 us (5%)
    ppermute x73, waiting for transfers between devices, send(): return lax.ppermute(block, self.axis, pairs)  128 us
    ppermute x73, starting transfers between devices, send(): return lax.ppermute(block, self.axis, pairs)  77.3 us
    dot_general x11, matrix products, dot32(): return jnp.dot(a, b, preferred_element_type=jnp.float32)  49.2 us
    ppermute x1, waiting for transfers between devices, per_device(): other = lax.ppermute(own, 'row', swap_x)  17.8 us
    ppermute x3, waiting for transfers between devices, along_z(): blocks.append(lax.ppermute(tie(blocks[-1], *after), 'row', up))  13.1 us
  transfers between devices with their start and end apart: 98, of which 61 were waited for; matrix products, arithmetic and copies ran while one was open for 19% of the time, Pallas kernels for 0%

profile of v2, /device:TPU:0, one launch (start us, length us, event | category | flops | bytes accessed | tf_op | source)
XLA Modules:
  0.0 369.4 jit_solution(10393108482079542600)
XLA Ops:
  0.6 3.0 collective-permute-start.1
  3.7 10.8 %collective-permute-done.1 = bf16[256,896]{1,0:T(8,128)(2,1)} collective-permute-done((bf16[256,896]{1,0:T(8,128)(2,1)}, bf16[256,896]{1,0:T(8,128)(2,1)}, u32[]{:S(2)}, u32[]{:S(2)}) %collective-permute-start.1) | collective-permute-done | bytes 458784 | tf_op jit(solution)/shard_map/ppermute | solution.py:67
  14.6 1.8 fusion.69
  16.5 1.9 fusion.3
  21.0 1.8 collective-permute-start.3
  23.0 1.7 collective-permute-start.11
  24.8 4.1 %convolution_convert_fusion.4 = bf16[1024,1792]{1,0:T(8,128)(2,1)S(1)} fusion(bf16[1024,896]{1,0:T(8,128)(2,1)S(1)} %get-tuple-element.107, bf16[896,1792]{1,0:T(8,128)(2,1)S(1)} %copy-done), kind=kOutput, calls=%fused_computation.10 | convolution fusion | flops 3290169344 | bytes 8716288 | tf_op jit(solution)/shard_map/dot_general | solution.py:191
  34.0 1.6 collective-permute-start.12
  35.6 3.4 collective-permute-done.5
  42.5 2.6 collective-permute-start.13
  47.0 1.7 collective-permute-start.9
  49.2 1.7 collective-permute-start.24
  51.4 2.2 collective-permute-done.9
  55.8 1.6 collective-permute-start.15
  57.9 7.0 %collective-permute-done.14 = bf16[128,512]{0,1:T(8,128)(2,1)S(1)} collective-permute-done((bf16[128,512]{0,1:T(8,128)(2,1)S(1)}, bf16[128,512]{0,1:T(8,128)(2,1)S(1)}, u32[]{:S(2)}, u32[]{:S(2)}) %collective-permute-start.14) | collective-permute-done | bytes 131104 | tf_op jit(solution)/shard_map/ppermute | solution.py:67
  67.5 1.8 collective-permute-start.27
  69.4 2.0 collective-permute-done.16
  74.1 7.1 %collective-permute-done.18 = bf16[128,512]{0,1:T(8,128)(2,1)S(1)} collective-permute-done((bf16[128,512]{0,1:T(8,128)(2,1)S(1)}, bf16[128,512]{0,1:T(8,128)(2,1)S(1)}, u32[]{:S(2)}, u32[]{:S(2)}) %collective-permute-start.18) | collective-permute-done | bytes 131104 | tf_op jit(solution)/shard_map/ppermute | solution.py:67
  84.8 1.7 collective-permute-start.29
  87.7 2.5 concatenate.93
  90.3 2.7 collective-permute-done.28
  96.0 2.9 convert_reduce_fusion.1
  98.9 2.1 fusion.41
  103.5 2.9 convert_reduce_fusion
  106.4 2.1 fusion.40
  113.6 4.8 %collective-permute-done.32 = bf16[64,1792]{1,0:T(8,128)(2,1)S(1)} collective-permute-done((bf16[64,1792]{1,0:T(8,128)(2,1)}, bf16[64,1792]{1,0:T(8,128)(2,1)S(1)}, u32[]{:S(2)}, u32[]{:S(2)}) %collective-permute-start.32) | collective-permute-done | bytes 229408 | tf_op jit(solution)/shard_map/ppermute | solution.py:67
  122.5 3.1 collective-permute-done.57
  130.3 3.2 collective-permute-done.37
  134.5 2.1 convolution_convert_fusion.8
  138.8 5.9 %collective-permute-done.61 = bf16[64,1792]{1,0:T(8,128)(2,1)S(1)} collective-permute-done((bf16[64,1792]{1,0:T(8,128)(2,1)S(1)}, bf16[64,1792]{1,0:T(8,128)(2,1)S(1)}, u32[]{:S(2)}, u32[]{:S(2)}) %collective-permute-start.61) | collective-permute-done | bytes 229408 | tf_op jit(solution)/shard_map/ppermute | solution.py:67
  151.5 2.1 convolution_convert_fusion.7
  157.2 3.8 %collective-permute-done.40 = bf16[128,896]{1,0:T(8,128)(2,1)S(1)} collective-permute-done((bf16[128,896]{1,0:T(8,128)(2,1)S(1)}, bf16[128,896]{1,0:T(8,128)(2,1)S(1)}, u32[]{:S(2)}, u32[]{:S(2)}) %collective-permute-start.40) | collective-permute-done | bytes 229408 | tf_op jit(solution)/shard_map/ppermute | solution.py:67
  169.6 1.7 collective-permute-start.44
  173.6 2.7 collective-permute-done.44
  176.3 2.7 collective-permute-done.45
  181.2 2.8 collective-permute-done.47
  185.1 2.1 collective-permute-start.49
  189.0 6.2 %collective-permute-done.68 = bf16[128,896]{1,0:T(8,128)(2,1)S(1)} collective-permute-done((bf16[128,896]{1,0:T(8,128)(2,1)S(1)}, bf16[128,896]{1,0:T(8,128)(2,1)S(1)}, u32[]{:S(2)}, u32[]{:S(2)}) %collective-permute-start.68) | collective-permute-done | bytes 229408 | tf_op jit(solution)/shard_map/ppermute | solution.py:402
  195.2 5.0 %collective-permute-done.49 = bf16[128,3584]{1,0:T(8,128)(2,1)S(1)} collective-permute-done((bf16[128,3584]{1,0:T(8,128)(2,1)S(1)}, bf16[128,3584]{1,0:T(8,128)(2,1)S(1)}, u32[]{:S(2)}, u32[]{:S(2)}) %collective-permute-start.49) | collective-permute-done | bytes 917536 | tf_op jit(solution)/shard_map/ppermute | solution.py:387
  201.2 6.9 %collective-permute-done.69 = bf16[128,896]{1,0:T(8,128)(2,1)S(1)} collective-permute-done((bf16[128,896]{1,0:T(8,128)(2,1)S(1)}, bf16[128,896]{1,0:T(8,128)(2,1)S(1)}, u32[]{:S(2)}, u32[]{:S(2)}) %collective-permute-start.69) | collective-permute-done | bytes 229408 | tf_op jit(solution)/shard_map/ppermute | solution.py:402
  210.7 9.4 %convolution_convert_fusion.2 = bf16[512,2560]{1,0:T(8,128)(2,1)S(1)} fusion(bf16[512,1792]{1,0:T(8,128)(2,1)S(1)} %multiply_convert_fusion.1, bf16[1792,2560]{1,0:T(8,128)(2,1)} %param.22), kind=kOutput, calls=%fused_computation.8 | convolution fusion | flops 4698931200 | bytes 13631488 | tf_op jit(solution)/shard_map/dot_general | solution.py:191
  220.2 5.1 %convolution_convert_fusion.3 = bf16[512,2560]{1,0:T(8,128)(2,1)S(1)} fusion(bf16[512,1792]{1,0:T(8,128)(2,1)S(1)} %multiply_convert_fusion.1, bf16[1792,2560]{1,0:T(8,128)(2,1)S(1)} %bitcast.244), kind=kOutput, calls=%fused_computation.9 | convolution fusion | flops 4698931200 | bytes 13631488 | tf_op jit(solution)/shard_map/dot_general | solution.py:191
  226.3 2.8 collective-permute-done.71
  233.9 17.8 %collective-permute-done.72 = bf16[512,896]{1,0:T(8,128)(2,1)S(1)} collective-permute-done((bf16[512,896]{1,0:T(8,128)(2,1)S(1)}, bf16[512,896]{1,0:T(8,128)(2,1)S(1)}, u32[]{:S(2)}, u32[]{:S(2)}) %collective-permute-start.72) | collective-permute-done | bytes 917536 | tf_op jit(solution)/shard_map/ppermute | solution.py:472
  253.3 8.5 %collective-permute-done.52 = bf16[128,2560]{1,0:T(8,128)(2,1)S(1)} collective-permute-done((bf16[128,2560]{1,0:T(8,128)(2,1)S(1)}, bf16[128,2560]{1,0:T(8,128)(2,1)S(1)}, u32[]{:S(2)}, u32[]{:S(2)}) %collective-permute-start.52) | collective-permute-done | bytes 655392 | tf_op jit(solution)/shard_map/ppermute | solution.py:67
  263.4 5.1 %convolution_convert_fusion = bf16[512,2560]{1,0:T(8,128)(2,1)S(1)} fusion(bf16[512,1792]{1,0:T(8,128)(2,1)S(1)} %multiply_convert_fusion, bf16[1792,2560]{1,0:T(8,128)(2,1)S(1)} %bitcast.242), kind=kOutput, calls=%fused_computation.6 | convolution fusion | flops 4698931200 | bytes 13631488 | tf_op jit(solution)/shard_map/dot_general | solution.py:191
  269.2 5.3 %convolution_convert_fusion.1 = bf16[512,2560]{1,0:T(8,128)(2,1)S(1)} fusion(bf16[512,1792]{1,0:T(8,128)(2,1)S(1)} %multiply_convert_fusion, bf16[1792,2560]{1,0:T(8,128)(2,1)S(1)} %bitcast.244), kind=kOutput, calls=%fused_computation.7 | convolution fusion | flops 4698931200 | bytes 13631488 | tf_op jit(solution)/shard_map/dot_general | solution.py:191
  274.7 3.5 collective-permute-done.56
  280.3 9.7 %convolution_convert_fusion.6 = bf16[512,1792]{1,0:T(8,128)(2,1)S(1)} fusion(bf16[2560,1792]{1,0:T(8,128)(2,1)} %param.23, bf16[128,2560]{1,0:T(8,128)(2,1)S(1)} %collective-permute-done.73, bf16[128,2560]{1,0:T(8,128)(2,1)} %copy-done.33, bf16[128,2560]{1,0:T(8,128)(2,1)} %collective-permute-done.55, bf16[128,2560]{1,0:T(8,128)(2,1)S(1)} %fusion.36), kind=kOutput, calls=%fused_computation.23 | convolution fusion | flops 4709023744 | bytes 13631488 | tf_op jit(solution)/shard_map/dot_general | solution.py:191
  290.1 2.0 collective-permute-start.75
  292.4 2.8 collective-permute-done.74
  295.7 1.8 collective-permute-start.77
  298.1 4.2 %collective-permute-done.76 = bf16[64,1792]{1,0:T(8,128)(2,1)S(1)} collective-permute-done((bf16[64,1792]{1,0:T(8,128)(2,1)S(1)}, bf16[64,1792]{1,0:T(8,128)(2,1)S(1)}, u32[]{:S(2)}, u32[]{:S(2)}) %collective-permute-start.76) | collective-permute-done | bytes 229408 | tf_op jit(solution)/shard_map/ppermute | solution.py:67
  303.1 1.7 collective-permute-start.79
  306.2 2.6 collective-permute-done.84
  309.1 3.9 %collective-permute-done.83 = bf16[128,2560]{1,0:T(8,128)(2,1)S(1)} collective-permute-done((bf16[128,2560]{1,0:T(8,128)(2,1)S(1)}, bf16[128,2560]{1,0:T(8,128)(2,1)S(1)}, u32[]{:S(2)}, u32[]{:S(2)}) %collective-permute-start.83) | collective-permute-done | bytes 655392 | tf_op jit(solution)/shard_map/ppermute | solution.py:67
  316.4 4.0 %collective-permute-done.80 = bf16[64,1792]{1,0:T(8,128)(2,1)S(1)} collective-permute-done((bf16[64,1792]{1,0:T(8,128)(2,1)S(1)}, bf16[64,1792]{1,0:T(8,128)(2,1)S(1)}, u32[]{:S(2)}, u32[]{:S(2)}) %collective-permute-start.80) | collective-permute-done | bytes 229408 | tf_op jit(solution)/shard_map/ppermute | solution.py:67
  320.9 7.3 %collective-permute-done.88 = bf16[128,2560]{1,0:T(8,128)(2,1)S(1)} collective-permute-done((bf16[128,2560]{1,0:T(8,128)(2,1)S(1)}, bf16[128,2560]{1,0:T(8,128)(2,1)S(1)}, u32[]{:S(2)}, u32[]{:S(2)}) %collective-permute-start.88) | collective-permute-done | bytes 655392 | tf_op jit(solution)/shard_map/ppermute | solution.py:67
  328.3 2.0 collective-permute-done.89
  330.3 4.9 %convolution_convert_fusion.5 = bf16[512,1792]{1,0:T(8,128)(2,1)S(1)} fusion(bf16[2560,1792]{1,0:T(8,128)(2,1)S(1)} %bitcast.246, bf16[128,2560]{1,0:T(8,128)(2,1)S(1)} %collective-permute-done.89, bf16[128,2560]{1,0:T(8,128)(2,1)S(1)} %collective-permute-done.88, bf16[128,2560]{1,0:T(8,128)(2,1)S(1)} %collective-permute-done.87, ...), kind=kOutput, calls=%fused_computation.22 | convolution fusion | flops 4709023744 | bytes 13631488 | tf_op jit(solution)/shard_map/dot_general | solution.py:191
  344.8 1.7 collective-permute-start.93
  347.3 3.7 %collective-permute-done.92 = bf16[64,1792]{1,0:T(8,128)(2,1)S(1)} collective-permute-done((bf16[64,1792]{1,0:T(8,128)(2,1)S(1)}, bf16[64,1792]{1,0:T(8,128)(2,1)S(1)}, u32[]{:S(2)}, u32[]{:S(2)}) %collective-permute-start.92) | collective-permute-done | bytes 229408 | tf_op jit(solution)/shard_map/ppermute | solution.py:67
  354.7 3.8 %collective-permute-done.94 = bf16[64,1792]{1,0:T(8,128)(2,1)S(1)} collective-permute-done((bf16[64,1792]{1,0:T(8,128)(2,1)S(1)}, bf16[64,1792]{1,0:T(8,128)(2,1)S(1)}, u32[]{:S(2)}, u32[]{:S(2)}) %collective-permute-start.94) | collective-permute-done | bytes 229408 | tf_op jit(solution)/shard_map/ppermute | solution.py:67
  363.5 2.8 collective-permute-done.96
  (394 shorter events, 120.6 us)
Async XLA Ops:
  0.6 13.9 %collective-permute-start.1 = (bf16[256,896]{1,0:T(8,128)(2,1)}, bf16[256,896]{1,0:T(8,128)(2,1)}, u32[]{:S(2)}, u32[]{:S(2)}) collective-permute-start(bf16[256,896]{1,0:T(8,128)(2,1)} %param.14), channel_id=1, source_target_pairs={{0,2},{2,0},{1,3},{3,1},{4,6},{6,4},{5,7},{7,5},{8,10},{10,8},{9,1... | collective-permute-start | bytes 1376264 | tf_op jit(solution)/shard_map/ppermute | solution.py:67
  3.7 12.7 %collective-permute-start = (bf16[256,896]{1,0:T(8,128)(2,1)}, bf16[256,896]{1,0:T(8,128)(2,1)}, u32[]{:S(2)}, u32[]{:S(2)}) collective-permute-start(bf16[256,896]{1,0:T(8,128)(2,1)} %param.14), channel_id=1, source_target_pairs={{0,1},{1,0},{2,3},{3,2},{4,5},{5,4},{6,7},{7,6},{8,9},{9,8},{10,11... | collective-permute-start | bytes 1376264 | tf_op jit(solution)/shard_map/ppermute | solution.py:219
  21.0 10.1 %collective-permute-start.3 = (bf16[64,512]{0,1:T(8,128)(2,1)S(1)}, bf16[64,512]{0,1:T(8,128)(2,1)S(1)}, u32[]{:S(2)}, u32[]{:S(2)}) collective-permute-start(bf16[64,512]{0,1:T(8,128)(2,1)S(1)} %get-tuple-element.87), channel_id=1, source_target_pairs={{0,8},{8,16},{16,24},{24,28},{28,20},{20,12},{12,4},{4,0},{1,9},{9... | collective-permute-start | bytes 196616 | tf_op jit(solution)/shard_map/ppermute | solution.py:67
  22.8 8.5 %collective-permute-start.4 = (bf16[64,512]{0,1:T(8,128)(2,1)S(1)}, bf16[64,512]{0,1:T(8,128)(2,1)S(1)}, u32[]{:S(2)}, u32[]{:S(2)}) collective-permute-start(bf16[64,512]{0,1:T(8,128)(2,1)S(1)} %get-tuple-element.88), channel_id=1, source_target_pairs={{8,0},{16,8},{24,16},{28,24},{20,28},{12,20},{4,12},{0,4},{9,1},{1... | collective-permute-start | bytes 196616 | tf_op jit(solution)/shard_map/ppermute | solution.py:67
  23.0 10.9 %collective-permute-start.11 = (f32[1024]{0:T(1024)S(1)}, f32[1024]{0:T(1024)S(1)}, u32[]{:S(2)}, u32[]{:S(2)}) collective-permute-start(f32[1024]{0:T(1024)S(1)} %get-tuple-element.95), channel_id=1, source_target_pairs={{0,4},{4,0},{8,12},{12,8},{16,20},{20,16},{24,28},{28,24},{1,5},{5... | collective-permute-start | bytes 12296 | tf_op jit(solution)/shard_map/ppermute | solution.py:314
  29.0 16.1 %collective-permute-start.22 = (bf16[64,1792]{1,0:T(8,128)(2,1)S(1)}, bf16[64,1792]{1,0:T(8,128)(2,1)S(1)}, u32[]{:S(2)}, u32[]{:S(2)}) collective-permute-start(bf16[64,1792]{1,0:T(8,128)(2,1)S(1)} %get-tuple-element.108), channel_id=1, source_target_pairs={{0,8},{8,16},{16,24},{24,28},{28,20},{20,12},{12,4},{4,0},{1,9},{9... | collective-permute-start | bytes 688136 | tf_op jit(solution)/shard_map/ppermute | solution.py:67
  30.6 14.4 %collective-permute-start.23 = (bf16[64,1792]{1,0:T(8,128)(2,1)S(1)}, bf16[64,1792]{1,0:T(8,128)(2,1)S(1)}, u32[]{:S(2)}, u32[]{:S(2)}) collective-permute-start(bf16[64,1792]{1,0:T(8,128)(2,1)S(1)} %get-tuple-element.109), channel_id=1, source_target_pairs={{8,0},{16,8},{24,16},{28,24},{20,28},{12,20},{4,12},{0,4},{9,1},{1... | collective-permute-start | bytes 688136 | tf_op jit(solution)/shard_map/ppermute | solution.py:67
  31.5 7.5 %collective-permute-start.5 = (bf16[128,512]{0,1:T(8,128)(2,1)S(1)}, bf16[128,512]{0,1:T(8,128)(2,1)S(1)}, u32[]{:S(2)}, u32[]{:S(2)}) collective-permute-start(bf16[128,512]{0,1:T(8,128)(2,1)S(1)} %pad_maximum_fusion.15), channel_id=1, source_target_pairs={{0,8},{8,16},{16,24},{24,28},{28,20},{20,12},{12,4},{4,0},{1,9},{9... | collective-permute-start | bytes 393224 | tf_op jit(solution)/shard_map/ppermute | solution.py:67
  33.1 7.2 %collective-permute-start.6 = (bf16[128,512]{0,1:T(8,128)(2,1)S(1)}, bf16[128,512]{0,1:T(8,128)(2,1)S(1)}, u32[]{:S(2)}, u32[]{:S(2)}) collective-permute-start(bf16[128,512]{0,1:T(8,128)(2,1)S(1)} %pad_maximum_fusion.16), channel_id=1, source_target_pairs={{8,0},{16,8},{24,16},{28,24},{20,28},{12,20},{4,12},{0,4},{9,1},{1... | collective-permute-start | bytes 393224 | tf_op jit(solution)/shard_map/ppermute | solution.py:67
  34.0 8.5 %collective-permute-start.12 = (f32[1024]{0:T(1024)S(1)}, f32[1024]{0:T(1024)S(1)}, u32[]{:S(2)}, u32[]{:S(2)}) collective-permute-start(f32[1024]{0:T(1024)S(1)} %add.389), channel_id=1, source_target_pairs={{0,8},{4,12},{8,0},{12,4},{16,24},{20,28},{24,16},{28,20},{1,9},{5... | collective-permute-start | bytes 12296 | tf_op jit(solution)/shard_map/ppermute | solution.py:314
  42.5 8.8 %collective-permute-start.13 = (f32[1024]{0:T(1024)S(1)}, f32[1024]{0:T(1024)S(1)}, u32[]{:S(2)}, u32[]{:S(2)}) collective-permute-start(f32[1024]{0:T(1024)S(1)} %add.390), channel_id=1, source_target_pairs={{0,16},{4,20},{8,24},{12,28},{16,0},{20,4},{24,8},{28,12},{1,17},{... | collective-permute-start | bytes 12296 | tf_op jit(solution)/shard_map/ppermute | solution.py:314
  47.0 6.5 %collective-permute-start.9 = (bf16[128,512]{0,1:T(8,128)(2,1)S(1)}, bf16[128,512]{0,1:T(8,128)(2,1)S(1)}, u32[]{:S(2)}, u32[]{:S(2)}) collective-permute-start(bf16[128,512]{0,1:T(8,128)(2,1)S(1)} %get-tuple-element.93), channel_id=1, source_target_pairs={{0,8},{8,16},{16,24},{24,28},{28,20},{20,12},{12,4},{4,0},{1,9},{9... | collective-permute-start | bytes 393224 | tf_op jit(solution)/shard_map/ppermute | solution.py:67
  48.7 6.4 %collective-permute-start.10 = (bf16[128,512]{0,1:T(8,128)(2,1)S(1)}, bf16[128,512]{0,1:T(8,128)(2,1)S(1)}, u32[]{:S(2)}, u32[]{:S(2)}) collective-permute-start(bf16[128,512]{0,1:T(8,128)(2,1)S(1)} %get-tuple-element.94), channel_id=1, source_target_pairs={{8,0},{16,8},{24,16},{28,24},{20,28},{12,20},{4,12},{0,4},{9,1},{1... | collective-permute-start | bytes 393224 | tf_op jit(solution)/shard_map/ppermute | solution.py:67
  49.2 17.9 %collective-permute-start.24 = (bf16[128,1792]{1,0:T(8,128)(2,1)S(1)}, bf16[128,1792]{1,0:T(8,128)(2,1)S(1)}, u32[]{:S(2)}, u32[]{:S(2)}) collective-permute-start(bf16[128,1792]{1,0:T(8,128)(2,1)S(1)} %get-tuple-element.110), channel_id=1, source_target_pairs={{0,8},{8,16},{16,24},{24,28},{28,20},{20,12},{12,4},{4,0},{1,9},{9... | collective-permute-start | bytes 1376264 | tf_op jit(solution)/shard_map/ppermute | solution.py:67
  50.9 16.2 %collective-permute-start.25 = (bf16[128,1792]{1,0:T(8,128)(2,1)S(1)}, bf16[128,1792]{1,0:T(8,128)(2,1)S(1)}, u32[]{:S(2)}, u32[]{:S(2)}) collective-permute-start(bf16[128,1792]{1,0:T(8,128)(2,1)S(1)} %get-tuple-element.111), channel_id=1, source_target_pairs={{8,0},{16,8},{24,16},{28,24},{20,28},{12,20},{4,12},{0,4},{9,1},{1... | collective-permute-start | bytes 1376264 | tf_op jit(solution)/shard_map/ppermute | solution.py:67
  55.3 9.7 %collective-permute-start.14 = (bf16[128,512]{0,1:T(8,128)(2,1)S(1)}, bf16[128,512]{0,1:T(8,128)(2,1)S(1)}, u32[]{:S(2)}, u32[]{:S(2)}) collective-permute-start(bf16[128,512]{0,1:T(8,128)(2,1)S(1)} %pad_maximum_fusion.17), channel_id=1, source_target_pairs={{8,0},{16,8},{24,16},{28,24},{20,28},{12,20},{4,12},{0,4},{9,1},{1... | collective-permute-start | bytes 393224 | tf_op jit(solution)/shard_map/ppermute | solution.py:67
  55.8 9.2 %collective-permute-start.15 = (bf16[128,512]{0,1:T(8,128)(2,1)S(1)}, bf16[128,512]{0,1:T(8,128)(2,1)S(1)}, u32[]{:S(2)}, u32[]{:S(2)}) collective-permute-start(bf16[128,512]{0,1:T(8,128)(2,1)S(1)} %pad_maximum_fusion.17), channel_id=1, source_target_pairs={{0,8},{8,16},{16,24},{24,28},{28,20},{20,12},{12,4},{4,0},{1,9},{9... | collective-permute-start | bytes 393224 | tf_op jit(solution)/shard_map/ppermute | solution.py:67
  65.0 6.5 %collective-permute-start.16 = (bf16[128,512]{0,1:T(8,128)(2,1)S(1)}, bf16[128,512]{0,1:T(8,128)(2,1)S(1)}, u32[]{:S(2)}, u32[]{:S(2)}) collective-permute-start(bf16[128,512]{0,1:T(8,128)(2,1)S(1)} %collective-permute-done.14), channel_id=1, source_target_pairs={{8,0},{16,8},{24,16},{28,24},{20,28},{12,20},{4,12},{0,4},{9,1},{1... | collective-permute-start | bytes 393224 | tf_op jit(solution)/shard_map/ppermute | solution.py:67
  67.3 16.1 %collective-permute-start.26 = (bf16[128,1792]{1,0:T(8,128)(2,1)S(1)}, bf16[128,1792]{1,0:T(8,128)(2,1)S(1)}, u32[]{:S(2)}, u32[]{:S(2)}) collective-permute-start(bf16[128,1792]{1,0:T(8,128)(2,1)S(1)} %get-tuple-element.112), channel_id=1, source_target_pairs={{0,8},{8,16},{16,24},{24,28},{28,20},{20,12},{12,4},{4,0},{1,9},{9... | collective-permute-start | bytes 1376264 | tf_op jit(solution)/shard_map/ppermute | solution.py:67
  67.5 15.8 %collective-permute-start.27 = (bf16[128,1792]{1,0:T(8,128)(2,1)S(1)}, bf16[128,1792]{1,0:T(8,128)(2,1)S(1)}, u32[]{:S(2)}, u32[]{:S(2)}) collective-permute-start(bf16[128,1792]{1,0:T(8,128)(2,1)S(1)} %get-tuple-element.113), channel_id=1, source_target_pairs={{8,0},{16,8},{24,16},{28,24},{20,28},{12,20},{4,12},{0,4},{9,1},{1... | collective-permute-start | bytes 1376264 | tf_op jit(solution)/shard_map/ppermute | solution.py:67
  71.9 9.3 %collective-permute-start.18 = (bf16[128,512]{0,1:T(8,128)(2,1)S(1)}, bf16[128,512]{0,1:T(8,128)(2,1)S(1)}, u32[]{:S(2)}, u32[]{:S(2)}) collective-permute-start(bf16[128,512]{0,1:T(8,128)(2,1)S(1)} %collective-permute-done.16), channel_id=1, source_target_pairs={{8,0},{16,8},{24,16},{28,24},{20,28},{12,20},{4,12},{0,4},{9,1},{1... | collective-permute-start | bytes 393224 | tf_op jit(solution)/shard_map/ppermute | solution.py:67
  72.4 8.8 %collective-permute-start.19 = (bf16[128,512]{0,1:T(8,128)(2,1)S(1)}, bf16[128,512]{0,1:T(8,128)(2,1)S(1)}, u32[]{:S(2)}, u32[]{:S(2)}) collective-permute-start(bf16[128,512]{0,1:T(8,128)(2,1)S(1)} %collective-permute-done.17), channel_id=1, source_target_pairs={{0,8},{8,16},{16,24},{24,28},{28,20},{20,12},{12,4},{4,0},{1,9},{9... | collective-permute-start | bytes 393224 | tf_op jit(solution)/shard_map/ppermute | solution.py:67
  84.4 8.7 %collective-permute-start.28 = (bf16[128,1792]{1,0:T(8,128)(2,1)}, bf16[128,1792]{1,0:T(8,128)(2,1)S(1)}, u32[]{:S(2)}, u32[]{:S(2)}) collective-permute-start(bf16[128,1792]{1,0:T(8,128)(2,1)} %get-tuple-element.114), channel_id=1, source_target_pairs={{0,8},{8,16},{16,24},{24,28},{28,20},{20,12},{12,4},{4,0},{1,9},{9... | collective-permute-start | bytes 1376264 | tf_op jit(solution)/shard_map/ppermute | solution.py:67
  84.8 9.0 %collective-permute-start.29 = (bf16[128,1792]{1,0:T(8,128)(2,1)S(1)}, bf16[128,1792]{1,0:T(8,128)(2,1)}, u32[]{:S(2)}, u32[]{:S(2)}) collective-permute-start(bf16[128,1792]{1,0:T(8,128)(2,1)S(1)} %get-tuple-element.115), channel_id=1, source_target_pairs={{8,0},{16,8},{24,16},{28,24},{20,28},{12,20},{4,12},{0,4},{9,1},{1... | collective-permute-start | bytes 1376264 | tf_op jit(solution)/shard_map/ppermute | solution.py:67
  101.4 7.9 %collective-permute-start.30 = (bf16[64,1792]{1,0:T(8,128)(2,1)S(1)}, bf16[64,1792]{1,0:T(8,128)(2,1)}, u32[]{:S(2)}, u32[]{:S(2)}) collective-permute-start(bf16[64,1792]{1,0:T(8,128)(2,1)S(1)} %convert_element_type.523), channel_id=1, source_target_pairs={{0,8},{8,16},{16,24},{24,28},{28,20},{20,12},{12,4},{4,0},{1,9},{9... | collective-permute-start | bytes 688136 | tf_op jit(solution)/shard_map/ppermute | solution.py:67
  102.0 7.7 %collective-permute-start.31 = (bf16[64,1792]{1,0:T(8,128)(2,1)S(1)}, bf16[64,1792]{1,0:T(8,128)(2,1)}, u32[]{:S(2)}, u32[]{:S(2)}) collective-permute-start(bf16[64,1792]{1,0:T(8,128)(2,1)S(1)} %convert_element_type.523), channel_id=1, source_target_pairs={{8,0},{16,8},{24,16},{28,24},{20,28},{12,20},{4,12},{0,4},{9,1},{1... | collective-permute-start | bytes 688136 | tf_op jit(solution)/shard_map/ppermute | solution.py:67
  109.6 8.8 %collective-permute-start.32 = (bf16[64,1792]{1,0:T(8,128)(2,1)}, bf16[64,1792]{1,0:T(8,128)(2,1)S(1)}, u32[]{:S(2)}, u32[]{:S(2)}) collective-permute-start(bf16[64,1792]{1,0:T(8,128)(2,1)} %collective-permute-done.30), channel_id=1, source_target_pairs={{0,8},{8,16},{16,24},{24,28},{28,20},{20,12},{12,4},{4,0},{1,9},{9... | collective-permute-start | bytes 688136 | tf_op jit(solution)/shard_map/ppermute | solution.py:67
  110.2 10.2 %collective-permute-start.33 = (bf16[64,1792]{1,0:T(8,128)(2,1)}, bf16[64,1792]{1,0:T(8,128)(2,1)S(1)}, u32[]{:S(2)}, u32[]{:S(2)}) collective-permute-start(bf16[64,1792]{1,0:T(8,128)(2,1)} %collective-permute-done.31), channel_id=1, source_target_pairs={{8,0},{16,8},{24,16},{28,24},{20,28},{12,20},{4,12},{0,4},{9,1},{1... | collective-permute-start | bytes 688136 | tf_op jit(solution)/shard_map/ppermute | solution.py:67
  118.4 7.2 %collective-permute-start.57 = (bf16[64,1792]{1,0:T(8,128)(2,1)S(1)}, bf16[64,1792]{1,0:T(8,128)(2,1)S(1)}, u32[]{:S(2)}, u32[]{:S(2)}) collective-permute-start(bf16[64,1792]{1,0:T(8,128)(2,1)S(1)} %convert_element_type.527), channel_id=1, source_target_pairs={{0,8},{8,16},{16,24},{24,28},{28,20},{20,12},{12,4},{4,0},{1,9},{9... | collective-permute-start | bytes 688136 | tf_op jit(solution)/shard_map/ppermute | solution.py:67
  119.0 6.6 %collective-permute-start.58 = (bf16[64,1792]{1,0:T(8,128)(2,1)S(1)}, bf16[64,1792]{1,0:T(8,128)(2,1)S(1)}, u32[]{:S(2)}, u32[]{:S(2)}) collective-permute-start(bf16[64,1792]{1,0:T(8,128)(2,1)S(1)} %convert_element_type.527), channel_id=1, source_target_pairs={{8,0},{16,8},{24,16},{28,24},{20,28},{12,20},{4,12},{0,4},{9,1},{1... | collective-permute-start | bytes 688136 | tf_op jit(solution)/shard_map/ppermute | solution.py:67
  120.4 7.7 %collective-permute-start.34 = (bf16[64,1792]{1,0:T(8,128)(2,1)S(1)}, bf16[64,1792]{1,0:T(8,128)(2,1)S(1)}, u32[]{:S(2)}, u32[]{:S(2)}) collective-permute-start(bf16[64,1792]{1,0:T(8,128)(2,1)S(1)} %collective-permute-done.32), channel_id=1, source_target_pairs={{0,8},{8,16},{16,24},{24,28},{28,20},{20,12},{12,4},{4,0},{1,9},{9... | collective-permute-start | bytes 688136 | tf_op jit(solution)/shard_map/ppermute | solution.py:67
  121.0 7.1 %collective-permute-start.35 = (bf16[64,1792]{1,0:T(8,128)(2,1)S(1)}, bf16[64,1792]{1,0:T(8,128)(2,1)S(1)}, u32[]{:S(2)}, u32[]{:S(2)}) collective-permute-start(bf16[64,1792]{1,0:T(8,128)(2,1)S(1)} %collective-permute-done.33), channel_id=1, source_target_pairs={{8,0},{16,8},{24,16},{28,24},{20,28},{12,20},{4,12},{0,4},{9,1},{1... | collective-permute-start | bytes 688136 | tf_op jit(solution)/shard_map/ppermute | solution.py:67
  125.6 11.0 %collective-permute-start.59 = (bf16[64,1792]{1,0:T(8,128)(2,1)S(1)}, bf16[64,1792]{1,0:T(8,128)(2,1)S(1)}, u32[]{:S(2)}, u32[]{:S(2)}) collective-permute-start(bf16[64,1792]{1,0:T(8,128)(2,1)S(1)} %collective-permute-done.57), channel_id=1, source_target_pairs={{0,8},{8,16},{16,24},{24,28},{28,20},{20,12},{12,4},{4,0},{1,9},{9... | collective-permute-start | bytes 688136 | tf_op jit(solution)/shard_map/ppermute | solution.py:67
  126.3 10.4 %collective-permute-start.60 = (bf16[64,1792]{1,0:T(8,128)(2,1)S(1)}, bf16[64,1792]{1,0:T(8,128)(2,1)S(1)}, u32[]{:S(2)}, u32[]{:S(2)}) collective-permute-start(bf16[64,1792]{1,0:T(8,128)(2,1)S(1)} %collective-permute-done.58), channel_id=1, source_target_pairs={{8,0},{16,8},{24,16},{28,24},{20,28},{12,20},{4,12},{0,4},{9,1},{1... | collective-permute-start | bytes 688136 | tf_op jit(solution)/shard_map/ppermute | solution.py:67
  136.6 8.4 %collective-permute-start.38 = (bf16[2,128,896]{2,1,0:T(8,128)(2,1)S(1)}, bf16[2,128,896]{2,1,0:T(8,128)(2,1)S(1)}, u32[]{:S(2)}, u32[]{:S(2)}) collective-permute-start(bf16[2,128,896]{2,1,0:T(8,128)(2,1)S(1)} %slice_bitcast_fusion.16), channel_id=1, source_target_pairs={{0,1},{1,0},{2,3},{3,2},{4,5},{5,4},{6,7},{7,6},{8,9},{9,8},{10,11... | collective-permute-start | bytes 1376264 | tf_op jit(solution)/shard_map/ppermute | solution.py:219
  136.7 8.0 %collective-permute-start.61 = (bf16[64,1792]{1,0:T(8,128)(2,1)S(1)}, bf16[64,1792]{1,0:T(8,128)(2,1)S(1)}, u32[]{:S(2)}, u32[]{:S(2)}) collective-permute-start(bf16[64,1792]{1,0:T(8,128)(2,1)S(1)} %collective-permute-done.59), channel_id=1, source_target_pairs={{0,8},{8,16},{16,24},{24,28},{28,20},{20,12},{12,4},{4,0},{1,9},{9... | collective-permute-start | bytes 688136 | tf_op jit(solution)/shard_map/ppermute | solution.py:67
  137.3 7.7 %collective-permute-start.62 = (bf16[64,1792]{1,0:T(8,128)(2,1)S(1)}, bf16[64,1792]{1,0:T(8,128)(2,1)S(1)}, u32[]{:S(2)}, u32[]{:S(2)}) collective-permute-start(bf16[64,1792]{1,0:T(8,128)(2,1)S(1)} %collective-permute-done.60), channel_id=1, source_target_pairs={{8,0},{16,8},{24,16},{28,24},{20,28},{12,20},{4,12},{0,4},{9,1},{1... | collective-permute-start | bytes 688136 | tf_op jit(solution)/shard_map/ppermute | solution.py:67
  157.0 8.1 %collective-permute-start.65 = (bf16[2,128,896]{2,1,0:T(8,128)(2,1)S(1)}, bf16[2,128,896]{2,1,0:T(8,128)(2,1)S(1)}, u32[]{:S(2)}, u32[]{:S(2)}) collective-permute-start(bf16[2,128,896]{2,1,0:T(8,128)(2,1)S(1)} %slice_bitcast_fusion.14), channel_id=1, source_target_pairs={{0,1},{1,0},{2,3},{3,2},{4,5},{5,4},{6,7},{7,6},{8,9},{9,8},{10,11... | collective-permute-start | bytes 1376264 | tf_op jit(solution)/shard_map/ppermute | solution.py:219
  161.7 7.4 %collective-permute-start.42 = (bf16[128,896]{1,0:T(8,128)(2,1)S(1)}, bf16[128,896]{1,0:T(8,128)(2,1)S(1)}, u32[]{:S(2)}, u32[]{:S(2)}) collective-permute-start(bf16[128,896]{1,0:T(8,128)(2,1)S(1)} %collective-permute-done.40), channel_id=1, source_target_pairs={{0,8},{8,16},{16,24},{24,28},{28,20},{20,12},{12,4},{4,0},{1,9},{9... | collective-permute-start | bytes 688136 | tf_op jit(solution)/shard_map/ppermute | solution.py:67
  162.7 6.9 %collective-permute-start.43 = (bf16[128,896]{1,0:T(8,128)(2,1)}, bf16[128,896]{1,0:T(8,128)(2,1)S(1)}, u32[]{:S(2)}, u32[]{:S(2)}) collective-permute-start(bf16[128,896]{1,0:T(8,128)(2,1)} %collective-permute-done.41), channel_id=1, source_target_pairs={{8,0},{16,8},{24,16},{28,24},{20,28},{12,20},{4,12},{0,4},{9,1},{1... | collective-permute-start | bytes 688136 | tf_op jit(solution)/shard_map/ppermute | solution.py:67
  169.6 6.7 %collective-permute-start.44 = (bf16[128,896]{1,0:T(8,128)(2,1)S(1)}, bf16[128,896]{1,0:T(8,128)(2,1)S(1)}, u32[]{:S(2)}, u32[]{:S(2)}) collective-permute-start(bf16[128,896]{1,0:T(8,128)(2,1)S(1)} %collective-permute-done.42), channel_id=1, source_target_pairs={{0,8},{8,16},{16,24},{24,28},{28,20},{20,12},{12,4},{4,0},{1,9},{9... | collective-permute-start | bytes 688136 | tf_op jit(solution)/shard_map/ppermute | solution.py:67
  171.3 7.7 %collective-permute-start.45 = (bf16[128,896]{1,0:T(8,128)(2,1)S(1)}, bf16[128,896]{1,0:T(8,128)(2,1)S(1)}, u32[]{:S(2)}, u32[]{:S(2)}) collective-permute-start(bf16[128,896]{1,0:T(8,128)(2,1)S(1)} %collective-permute-done.43), channel_id=1, source_target_pairs={{8,0},{16,8},{24,16},{28,24},{20,28},{12,20},{4,12},{0,4},{9,1},{1... | collective-permute-start | bytes 688136 | tf_op jit(solution)/shard_map/ppermute | solution.py:67
  172.5 14.8 %collective-permute-start.67 = (bf16[128,896]{1,0:T(8,128)(2,1)S(1)}, bf16[128,896]{1,0:T(8,128)(2,1)S(1)}, u32[]{:S(2)}, u32[]{:S(2)}) collective-permute-start(bf16[128,896]{1,0:T(8,128)(2,1)S(1)} %fusion.45), channel_id=1, source_target_pairs={{0,8},{4,12},{8,16},{12,20},{16,24},{20,28},{24,0},{28,4},{1,9},{5... | collective-permute-start | bytes 688136 | tf_op jit(solution)/shard_map/ppermute | solution.py:402
  185.1 15.2 %collective-permute-start.49 = (bf16[128,3584]{1,0:T(8,128)(2,1)S(1)}, bf16[128,3584]{1,0:T(8,128)(2,1)S(1)}, u32[]{:S(2)}, u32[]{:S(2)}) collective-permute-start(bf16[128,3584]{1,0:T(8,128)(2,1)S(1)} %constant_dynamic-slice_fusion.8), channel_id=1, source_target_pairs={{0,2},{1,3},{2,0},{3,1},{4,6},{5,7},{6,4},{7,5},{8,10},{9,11},{10,... | collective-permute-start | bytes 2752520 | tf_op jit(solution)/shard_map/ppermute | solution.py:387
  187.3 7.9 %collective-permute-start.68 = (bf16[128,896]{1,0:T(8,128)(2,1)S(1)}, bf16[128,896]{1,0:T(8,128)(2,1)S(1)}, u32[]{:S(2)}, u32[]{:S(2)}) collective-permute-start(bf16[128,896]{1,0:T(8,128)(2,1)S(1)} %collective-permute-done.67), channel_id=1, source_target_pairs={{0,8},{4,12},{8,16},{12,20},{16,24},{20,28},{24,0},{28,4},{1,9},{5... | collective-permute-start | bytes 688136 | tf_op jit(solution)/shard_map/ppermute | solution.py:402
  188.9 20.9 %collective-permute-start.48 = (bf16[128,1792]{1,0:T(8,128)(2,1)S(1)}, bf16[128,1792]{1,0:T(8,128)(2,1)S(1)}, u32[]{:S(2)}, u32[]{:S(2)}) collective-permute-start(bf16[128,1792]{1,0:T(8,128)(2,1)S(1)} %get-tuple-element.201), channel_id=1, source_target_pairs={{0,1},{1,0},{2,3},{3,2},{4,5},{5,4},{6,7},{7,6},{8,9},{9,8},{10,11... | collective-permute-start | bytes 1376264 | tf_op jit(solution)/shard_map/ppermute | solution.py:219
  200.2 7.8 %collective-permute-start.69 = (bf16[128,896]{1,0:T(8,128)(2,1)S(1)}, bf16[128,896]{1,0:T(8,128)(2,1)S(1)}, u32[]{:S(2)}, u32[]{:S(2)}) collective-permute-start(bf16[128,896]{1,0:T(8,128)(2,1)S(1)} %collective-permute-done.68), channel_id=1, source_target_pairs={{0,8},{4,12},{8,16},{12,20},{16,24},{20,28},{24,0},{28,4},{1,9},{5... | collective-permute-start | bytes 688136 | tf_op jit(solution)/shard_map/ppermute | solution.py:402
  201.0 8.8 %collective-permute-start.50 = (bf16[128,1792]{1,0:T(8,128)(2,1)S(1)}, bf16[128,1792]{1,0:T(8,128)(2,1)S(1)}, u32[]{:S(2)}, u32[]{:S(2)}) collective-permute-start(bf16[128,1792]{1,0:T(8,128)(2,1)S(1)} %get-tuple-element.216), channel_id=1, source_target_pairs={{0,1},{1,0},{2,3},{3,2},{4,5},{5,4},{6,7},{7,6},{8,9},{9,8},{10,11... | collective-permute-start | bytes 1376264 | tf_op jit(solution)/shard_map/ppermute | solution.py:219
  208.2 17.2 %collective-permute-start.70 = (bf16[256,896]{1,0:T(8,128)(2,1)S(1)}, bf16[256,896]{1,0:T(8,128)(2,1)S(1)}, u32[]{:S(2)}, u32[]{:S(2)}) collective-permute-start(bf16[256,896]{1,0:T(8,128)(2,1)S(1)} %pad_maximum_fusion.8), channel_id=1, source_target_pairs={{0,2},{1,3},{2,0},{3,1},{4,6},{5,7},{6,4},{7,5},{8,10},{9,11},{10,... | collective-permute-start | bytes 1376264 | tf_op jit(solution)/shard_map/ppermute | solution.py:410
  229.3 22.5 %collective-permute-start.72 = (bf16[512,896]{1,0:T(8,128)(2,1)S(1)}, bf16[512,896]{1,0:T(8,128)(2,1)S(1)}, u32[]{:S(2)}, u32[]{:S(2)}) collective-permute-start(bf16[512,896]{1,0:T(8,128)(2,1)S(1)} %pad_maximum_fusion.4), channel_id=1, source_target_pairs={{0,4},{4,0},{8,12},{12,8},{16,20},{20,16},{24,28},{28,24},{1,5},{5... | collective-permute-start | bytes 2752520 | tf_op jit(solution)/shard_map/ppermute | solution.py:472
  231.2 22.1 %collective-permute-start.54 = (bf16[128,2560]{1,0:T(8,128)(2,1)S(1)}, bf16[128,2560]{1,0:T(8,128)(2,1)S(1)}, u32[]{:S(2)}, u32[]{:S(2)}) collective-permute-start(bf16[128,2560]{1,0:T(8,128)(2,1)S(1)} %slice_bitcast_fusion.8), channel_id=1, source_target_pairs={{0,2},{2,0},{1,3},{3,1},{4,6},{6,4},{5,7},{7,5},{8,10},{10,8},{9,1... | collective-permute-start | bytes 1966088 | tf_op jit(solution)/shard_map/ppermute | solution.py:67
  232.2 29.6 %collective-permute-start.52 = (bf16[128,2560]{1,0:T(8,128)(2,1)S(1)}, bf16[128,2560]{1,0:T(8,128)(2,1)S(1)}, u32[]{:S(2)}, u32[]{:S(2)}) collective-permute-start(bf16[128,2560]{1,0:T(8,128)(2,1)S(1)} %slice_bitcast_fusion.10), channel_id=1, source_target_pairs={{0,2},{2,0},{1,3},{3,1},{4,6},{6,4},{5,7},{7,5},{8,10},{10,8},{9,1... | collective-permute-start | bytes 1966088 | tf_op jit(solution)/shard_map/ppermute | solution.py:67
  262.5 15.7 %collective-permute-start.56 = (bf16[128,2560]{1,0:T(8,128)(2,1)S(1)}, bf16[128,2560]{1,0:T(8,128)(2,1)S(1)}, u32[]{:S(2)}, u32[]{:S(2)}) collective-permute-start(bf16[128,2560]{1,0:T(8,128)(2,1)S(1)} %fusion.36), channel_id=1, source_target_pairs={{0,2},{2,0},{1,3},{3,1},{4,6},{6,4},{5,7},{7,5},{8,10},{10,8},{9,1... | collective-permute-start | bytes 1966088 | tf_op jit(solution)/shard_map/ppermute | solution.py:67
  263.1 16.6 %collective-permute-start.55 = (bf16[128,2560]{1,0:T(8,128)(2,1)S(1)}, bf16[128,2560]{1,0:T(8,128)(2,1)}, u32[]{:S(2)}, u32[]{:S(2)}) collective-permute-start(bf16[128,2560]{1,0:T(8,128)(2,1)S(1)} %fusion.36), channel_id=1, source_target_pairs={{0,1},{1,0},{2,3},{3,2},{4,5},{5,4},{6,7},{7,6},{8,9},{9,8},{10,11... | collective-permute-start | bytes 1966088 | tf_op jit(solution)/shard_map/ppermute | solution.py:219
  268.6 9.5 %collective-permute-start.85 = (bf16[2,128,2560]{2,1,0:T(8,128)(2,1)S(1)}, bf16[2,128,2560]{2,1,0:T(8,128)(2,1)S(1)}, u32[]{:S(2)}, u32[]{:S(2)}) collective-permute-start(bf16[2,128,2560]{2,1,0:T(8,128)(2,1)S(1)} %slice_bitcast_fusion), channel_id=1, source_target_pairs={{0,1},{1,0},{2,3},{3,2},{4,5},{5,4},{6,7},{7,6},{8,9},{9,8},{10,11... | collective-permute-start | bytes 3932168 | tf_op jit(solution)/shard_map/ppermute | solution.py:219
  274.6 17.5 %collective-permute-start.82 = (bf16[2,128,2560]{2,1,0:T(8,128)(2,1)S(1)}, bf16[2,128,2560]{2,1,0:T(8,128)(2,1)S(1)}, u32[]{:S(2)}, u32[]{:S(2)}) collective-permute-start(bf16[2,128,2560]{2,1,0:T(8,128)(2,1)S(1)} %slice_bitcast_fusion.2), channel_id=1, source_target_pairs={{0,1},{1,0},{2,3},{3,2},{4,5},{5,4},{6,7},{7,6},{8,9},{9,8},{10,11... | collective-permute-start | bytes 3932168 | tf_op jit(solution)/shard_map/ppermute | solution.py:219
  279.1 30.0 %collective-permute-start.86 = (bf16[128,2560]{1,0:T(8,128)(2,1)S(1)}, bf16[128,2560]{1,0:T(8,128)(2,1)S(1)}, u32[]{:S(2)}, u32[]{:S(2)}) collective-permute-start(bf16[128,2560]{1,0:T(8,128)(2,1)S(1)} %slice_bitcast_fusion.12), channel_id=1, source_target_pairs={{0,2},{2,0},{1,3},{3,1},{4,6},{6,4},{5,7},{7,5},{8,10},{10,8},{9,1... | collective-permute-start | bytes 1966088 | tf_op jit(solution)/shard_map/ppermute | solution.py:67
  295.4 6.9 %collective-permute-start.76 = (bf16[64,1792]{1,0:T(8,128)(2,1)S(1)}, bf16[64,1792]{1,0:T(8,128)(2,1)S(1)}, u32[]{:S(2)}, u32[]{:S(2)}) collective-permute-start(bf16[64,1792]{1,0:T(8,128)(2,1)S(1)} %pad_maximum_fusion.11), channel_id=1, source_target_pairs={{0,8},{8,16},{16,24},{24,28},{28,20},{20,12},{12,4},{4,0},{1,9},{9... | collective-permute-start | bytes 688136 | tf_op jit(solution)/shard_map/ppermute | solution.py:67
  295.7 6.9 %collective-permute-start.77 = (bf16[64,1792]{1,0:T(8,128)(2,1)S(1)}, bf16[64,1792]{1,0:T(8,128)(2,1)S(1)}, u32[]{:S(2)}, u32[]{:S(2)}) collective-permute-start(bf16[64,1792]{1,0:T(8,128)(2,1)S(1)} %pad_maximum_fusion.12), channel_id=1, source_target_pairs={{8,0},{16,8},{24,16},{28,24},{20,28},{12,20},{4,12},{0,4},{9,1},{1... | collective-permute-start | bytes 688136 | tf_op jit(solution)/shard_map/ppermute | solution.py:67
  297.5 15.5 %collective-permute-start.83 = (bf16[128,2560]{1,0:T(8,128)(2,1)S(1)}, bf16[128,2560]{1,0:T(8,128)(2,1)S(1)}, u32[]{:S(2)}, u32[]{:S(2)}) collective-permute-start(bf16[128,2560]{1,0:T(8,128)(2,1)S(1)} %slice_bitcast_fusion.13), channel_id=1, source_target_pairs={{0,2},{2,0},{1,3},{3,1},{4,6},{6,4},{5,7},{7,5},{8,10},{10,8},{9,1... | collective-permute-start | bytes 1966088 | tf_op jit(solution)/shard_map/ppermute | solution.py:67
  313.7 14.5 %collective-permute-start.88 = (bf16[128,2560]{1,0:T(8,128)(2,1)S(1)}, bf16[128,2560]{1,0:T(8,128)(2,1)S(1)}, u32[]{:S(2)}, u32[]{:S(2)}) collective-permute-start(bf16[128,2560]{1,0:T(8,128)(2,1)S(1)} %fusion.32), channel_id=1, source_target_pairs={{0,2},{2,0},{1,3},{3,1},{4,6},{6,4},{5,7},{7,5},{8,10},{10,8},{9,1... | collective-permute-start | bytes 1966088 | tf_op jit(solution)/shard_map/ppermute | solution.py:67
  316.4 11.9 %collective-permute-start.87 = (bf16[128,2560]{1,0:T(8,128)(2,1)S(1)}, bf16[128,2560]{1,0:T(8,128)(2,1)S(1)}, u32[]{:S(2)}, u32[]{:S(2)}) collective-permute-start(bf16[128,2560]{1,0:T(8,128)(2,1)S(1)} %fusion.32), channel_id=1, source_target_pairs={{0,1},{1,0},{2,3},{3,2},{4,5},{5,4},{6,7},{7,6},{8,9},{9,8},{10,11... | collective-permute-start | bytes 1966088 | tf_op jit(solution)/shard_map/ppermute | solution.py:219
  344.4 6.5 %collective-permute-start.92 = (bf16[64,1792]{1,0:T(8,128)(2,1)S(1)}, bf16[64,1792]{1,0:T(8,128)(2,1)S(1)}, u32[]{:S(2)}, u32[]{:S(2)}) collective-permute-start(bf16[64,1792]{1,0:T(8,128)(2,1)S(1)} %pad_maximum_fusion.13), channel_id=1, source_target_pairs={{0,8},{8,16},{16,24},{24,28},{28,20},{20,12},{12,4},{4,0},{1,9},{9... | collective-permute-start | bytes 688136 | tf_op jit(solution)/shard_map/ppermute | solution.py:67
  344.8 6.5 %collective-permute-start.93 = (bf16[64,1792]{1,0:T(8,128)(2,1)S(1)}, bf16[64,1792]{1,0:T(8,128)(2,1)S(1)}, u32[]{:S(2)}, u32[]{:S(2)}) collective-permute-start(bf16[64,1792]{1,0:T(8,128)(2,1)S(1)} %pad_maximum_fusion.14), channel_id=1, source_target_pairs={{8,0},{16,8},{24,16},{28,24},{20,28},{12,20},{4,12},{0,4},{9,1},{1... | collective-permute-start | bytes 688136 | tf_op jit(solution)/shard_map/ppermute | solution.py:67
  (80 other events, 810.6 us)

commit v3 on v2

--- a/solution.py
+++ b/solution.py
@@ -402,12 +402,13 @@
             blocks.append(lax.ppermute(tie(blocks[-1], *after), "row", up))
         return blocks
 
-    def to_takers(blocks):
+    def to_takers(blocks, after):
         z = quotient(row_place, 2)
         here = [quotient(remainder(z - i + 4, 4), 2) == lane for i in range(2)]
         given = [jnp.where(here[i], blocks[i + 2], blocks[i]) for i in range(2)]
         kept = [jnp.where(here[i], blocks[i], blocks[i + 2]) for i in range(2)]
-        over = lax.ppermute(jnp.concatenate(given, axis=0), "col", [(i, i ^ 2) for i in range(cols)])
+        given = tie(jnp.concatenate(given, axis=0), *after)
+        over = lax.ppermute(given, "col", [(i, i ^ 2) for i in range(cols)])
         came = [over[:col_part], over[col_part:]]
         first = remainder(jnp.bitwise_xor(z, core), 2) == 0
         mine = [jnp.where(first, b[0], b[1]) for b in (kept, came)]
@@ -468,10 +469,10 @@
             total = total + jnp.sum(block * block, axis=1)
         total = total + lax.ppermute(total, "row", swap_x)
         scales.append(lax.rsqrt(total / model_width + EPSILON)[:, None])
-        own = to_takers(blocks)
-        other = lax.ppermute(own, "row", swap_x)
         stream_0 = join_cores(halves, ())
         gate_0, up_0, terms_0 = widen(stream_0)
+        own = to_takers(blocks, terms_0[:1])
+        other = lax.ppermute(own, "row", swap_x)
         stream_1 = join_x(own, tie(other, *terms_0))
     else:
         stream_1.step(second)
@@ -496,7 +497,7 @@
     gate_1, up_1, terms_1 = widen(tie(stream_1, *gate_0.got))
     hidden_0 = gated(gate_0.result(), up_0.result(), scales[0])
     everyone, far = gather_cols(hidden_0, terms_1)
-    gate_1, up_1 = lane_walk(tie(gate_1, far)), lane_walk(tie(up_1, far))
+    gate_1, up_1 = lane_walk(gate_1), lane_walk(tie(up_1, far))
     down_0 = down_walk(everyone)
     while down_0.done < down_0.steps - 1:
         down_0.step()

time: 376 us -> 376 us (level)
  starting transfers between devices: 94.1 us -> 98.1 us
  waiting for transfers between devices: 172 us -> 168 us
    ppermute x73, starting transfers between devices: 77.3 us -> 81.3 us  [send(): return lax.ppermute(block, self.axis, pairs)]
  transfers between devices with their start and end apart: 98 -> 98, of which waited for: 61 -> 61; matrix products, arithmetic and copies ran while one was open for 19% -> 16% of each run, Pallas kernels for 0% -> 0%
where the time goes in v3:
time: 376 us; the launch traced here: 369 us
  waiting for transfers between devices  168 us (45%)
  starting transfers between devices  98.1 us (26%)
  matrix products  59 us (16%)
  other arithmetic  21.9 us (6%)
  local copies, waits for them, and re-layouts  20.2 us (5%)
    ppermute x73, waiting for transfers between devices, send(): return lax.ppermute(block, self.axis, pairs)  124 us
    ppermute x73, starting transfers between devices, send(): return lax.ppermute(block, self.axis, pairs)  81.3 us
    dot_general x11, matrix products, dot32(): return jnp.dot(a, b, preferred_element_type=jnp.float32)  48.9 us
    ppermute x1, waiting for transfers between devices, per_device(): other = lax.ppermute(own, 'row', swap_x)  17.9 us
    ppermute x3, waiting for transfers between devices, along_z(): blocks.append(lax.ppermute(tie(blocks[-1], *after), 'row', up))  13.1 us
  transfers between devices with their start and end apart: 98, of which 61 were waited for; matrix products, arithmetic and copies ran while one was open for 16% of the time, Pallas kernels for 0%

profile of v3, /device:TPU:0, one launch (start us, length us, event | category | flops | bytes accessed | tf_op | source)
XLA Modules:
  0.0 369.2 jit_solution(10299460435001937946)
XLA Ops:
  0.6 3.0 collective-permute-start.1
  3.7 10.8 %collective-permute-done.1 = bf16[256,896]{1,0:T(8,128)(2,1)} collective-permute-done((bf16[256,896]{1,0:T(8,128)(2,1)}, bf16[256,896]{1,0:T(8,128)(2,1)}, u32[]{:S(2)}, u32[]{:S(2)}) %collective-permute-start.1) | collective-permute-done | bytes 458784 | tf_op jit(solution)/shard_map/ppermute | solution.py:67
  14.6 1.8 fusion.69
  16.5 1.9 fusion.3
  21.0 1.8 collective-permute-start.3
  23.0 1.7 collective-permute-start.11
  24.8 4.1 %convolution_convert_fusion.4 = bf16[1024,1792]{1,0:T(8,128)(2,1)S(1)} fusion(bf16[1024,896]{1,0:T(8,128)(2,1)S(1)} %get-tuple-element.107, bf16[896,1792]{1,0:T(8,128)(2,1)S(1)} %copy-done), kind=kOutput, calls=%fused_computation.10 | convolution fusion | flops 3290169344 | bytes 8716288 | tf_op jit(solution)/shard_map/dot_general | solution.py:191
  29.0 1.6 collective-permute-start.22
  34.0 1.6 collective-permute-start.12
  35.6 3.4 collective-permute-done.5
  42.5 2.6 collective-permute-start.13
  47.0 1.7 collective-permute-start.9
  49.2 1.7 collective-permute-start.24
  51.4 2.2 collective-permute-done.9
  53.5 1.6 collective-permute-done.10
  55.8 1.6 collective-permute-start.15
  57.9 7.0 %collective-permute-done.14 = bf16[128,512]{0,1:T(8,128)(2,1)S(1)} collective-permute-done((bf16[128,512]{0,1:T(8,128)(2,1)S(1)}, bf16[128,512]{0,1:T(8,128)(2,1)S(1)}, u32[]{:S(2)}, u32[]{:S(2)}) %collective-permute-start.14) | collective-permute-done | bytes 131104 | tf_op jit(solution)/shard_map/ppermute | solution.py:67
  65.4 1.6 collective-permute-start.17
  67.5 1.8 collective-permute-start.27
  69.4 2.0 collective-permute-done.16
  74.1 7.1 %collective-permute-done.18 = bf16[128,512]{0,1:T(8,128)(2,1)S(1)} collective-permute-done((bf16[128,512]{0,1:T(8,128)(2,1)S(1)}, bf16[128,512]{0,1:T(8,128)(2,1)S(1)}, u32[]{:S(2)}, u32[]{:S(2)}) %collective-permute-start.18) | collective-permute-done | bytes 131104 | tf_op jit(solution)/shard_map/ppermute | solution.py:67
  84.8 1.7 collective-permute-start.29
  87.7 2.5 concatenate.93
  90.3 2.7 collective-permute-done.28
  96.0 2.9 convert_reduce_fusion.1
  98.9 2.1 fusion.41
  103.5 2.9 convert_reduce_fusion
  106.4 2.1 fusion.40
  113.6 4.8 %collective-permute-done.32 = bf16[64,1792]{1,0:T(8,128)(2,1)S(1)} collective-permute-done((bf16[64,1792]{1,0:T(8,128)(2,1)}, bf16[64,1792]{1,0:T(8,128)(2,1)S(1)}, u32[]{:S(2)}, u32[]{:S(2)}) %collective-permute-start.32) | collective-permute-done | bytes 229408 | tf_op jit(solution)/shard_map/ppermute | solution.py:67
  122.5 3.1 collective-permute-done.57
  130.3 3.2 collective-permute-done.37
  134.5 2.1 convolution_convert_fusion.8
  138.8 5.9 %collective-permute-done.61 = bf16[64,1792]{1,0:T(8,128)(2,1)S(1)} collective-permute-done((bf16[64,1792]{1,0:T(8,128)(2,1)S(1)}, bf16[64,1792]{1,0:T(8,128)(2,1)S(1)}, u32[]{:S(2)}, u32[]{:S(2)}) %collective-permute-start.61) | collective-permute-done | bytes 229408 | tf_op jit(solution)/shard_map/ppermute | solution.py:67
  151.5 2.1 convolution_convert_fusion.7
  157.2 3.8 %collective-permute-done.40 = bf16[128,896]{1,0:T(8,128)(2,1)S(1)} collective-permute-done((bf16[128,896]{1,0:T(8,128)(2,1)S(1)}, bf16[128,896]{1,0:T(8,128)(2,1)S(1)}, u32[]{:S(2)}, u32[]{:S(2)}) %collective-permute-start.40) | collective-permute-done | bytes 229408 | tf_op jit(solution)/shard_map/ppermute | solution.py:67
  169.6 1.7 collective-permute-start.44
  173.6 2.7 collective-permute-done.44
  176.3 2.7 collective-permute-done.45
  181.2 2.8 collective-permute-done.47
  185.1 2.1 collective-permute-start.49
  189.0 6.2 %collective-permute-done.68 = bf16[128,896]{1,0:T(8,128)(2,1)S(1)} collective-permute-done((bf16[128,896]{1,0:T(8,128)(2,1)S(1)}, bf16[128,896]{1,0:T(8,128)(2,1)S(1)}, u32[]{:S(2)}, u32[]{:S(2)}) %collective-permute-start.68) | collective-permute-done | bytes 229408 | tf_op jit(solution)/shard_map/ppermute | solution.py:402
  195.2 5.0 %collective-permute-done.49 = bf16[128,3584]{1,0:T(8,128)(2,1)S(1)} collective-permute-done((bf16[128,3584]{1,0:T(8,128)(2,1)S(1)}, bf16[128,3584]{1,0:T(8,128)(2,1)S(1)}, u32[]{:S(2)}, u32[]{:S(2)}) %collective-permute-start.49) | collective-permute-done | bytes 917536 | tf_op jit(solution)/shard_map/ppermute | solution.py:387
  201.2 6.9 %collective-permute-done.69 = bf16[128,896]{1,0:T(8,128)(2,1)S(1)} collective-permute-done((bf16[128,896]{1,0:T(8,128)(2,1)S(1)}, bf16[128,896]{1,0:T(8,128)(2,1)S(1)}, u32[]{:S(2)}, u32[]{:S(2)}) %collective-permute-start.69) | collective-permute-done | bytes 229408 | tf_op jit(solution)/shard_map/ppermute | solution.py:402
  209.2 9.4 %convolution_convert_fusion.3 = bf16[512,2560]{1,0:T(8,128)(2,1)S(1)} fusion(bf16[512,1792]{1,0:T(8,128)(2,1)S(1)} %multiply_convert_fusion.1, bf16[1792,2560]{1,0:T(8,128)(2,1)} %param.21), kind=kOutput, calls=%fused_computation.9 | convolution fusion | flops 4698931200 | bytes 13631488 | tf_op jit(solution)/shard_map/dot_general | solution.py:191
  220.1 5.1 %convolution_convert_fusion.2 = bf16[512,2560]{1,0:T(8,128)(2,1)S(1)} fusion(bf16[512,1792]{1,0:T(8,128)(2,1)S(1)} %multiply_convert_fusion.1, bf16[1792,2560]{1,0:T(8,128)(2,1)S(1)} %bitcast.244), kind=kOutput, calls=%fused_computation.8 | convolution fusion | flops 4698931200 | bytes 13631488 | tf_op jit(solution)/shard_map/dot_general | solution.py:191
  225.4 1.7 collective-permute-done.70
  233.8 17.9 %collective-permute-done.72 = bf16[512,896]{1,0:T(8,128)(2,1)S(1)} collective-permute-done((bf16[512,896]{1,0:T(8,128)(2,1)S(1)}, bf16[512,896]{1,0:T(8,128)(2,1)S(1)}, u32[]{:S(2)}, u32[]{:S(2)}) %collective-permute-start.72) | collective-permute-done | bytes 917536 | tf_op jit(solution)/shard_map/ppermute | solution.py:475
  253.3 8.5 %collective-permute-done.54 = bf16[128,2560]{1,0:T(8,128)(2,1)S(1)} collective-permute-done((bf16[128,2560]{1,0:T(8,128)(2,1)S(1)}, bf16[128,2560]{1,0:T(8,128)(2,1)S(1)}, u32[]{:S(2)}, u32[]{:S(2)}) %collective-permute-start.54) | collective-permute-done | bytes 655392 | tf_op jit(solution)/shard_map/ppermute | solution.py:67
  264.3 5.1 %convolution_convert_fusion = bf16[512,2560]{1,0:T(8,128)(2,1)S(1)} fusion(bf16[512,1792]{1,0:T(8,128)(2,1)S(1)} %multiply_convert_fusion, bf16[1792,2560]{1,0:T(8,128)(2,1)S(1)} %bitcast.244), kind=kOutput, calls=%fused_computation.6 | convolution fusion | flops 4698931200 | bytes 13631488 | tf_op jit(solution)/shard_map/dot_general | solution.py:191
  270.1 5.3 %convolution_convert_fusion.1 = bf16[512,2560]{1,0:T(8,128)(2,1)S(1)} fusion(bf16[512,1792]{1,0:T(8,128)(2,1)S(1)} %multiply_convert_fusion, bf16[1792,2560]{1,0:T(8,128)(2,1)S(1)} %bitcast.246), kind=kOutput, calls=%fused_computation.7 | convolution fusion | flops 4698931200 | bytes 13631488 | tf_op jit(solution)/shard_map/dot_general | solution.py:191
  275.6 2.5 collective-permute-done.56
  280.6 9.4 %convolution_convert_fusion.6 = bf16[512,1792]{1,0:T(8,128)(2,1)S(1)} fusion(bf16[2560,1792]{1,0:T(8,128)(2,1)} %param.23, bf16[128,2560]{1,0:T(8,128)(2,1)S(1)} %collective-permute-done.73, bf16[128,2560]{1,0:T(8,128)(2,1)} %copy-done.33, bf16[128,2560]{1,0:T(8,128)(2,1)} %collective-permute-done.55, bf16[128,2560]{1,0:T(8,128)(2,1)S(1)} %fusion.36), kind=kOutput, calls=%fused_computation.23 | convolution fusion | flops 4709023744 | bytes 13631488 | tf_op jit(solution)/shard_map/dot_general | solution.py:191
  290.1 2.0 collective-permute-start.75
  292.4 2.8 collective-permute-done.74
  299.0 3.1 collective-permute-done.76
  306.1 2.6 collective-permute-done.84
  310.1 2.8 collective-permute-done.83
  317.4 4.0 %collective-permute-done.80 = bf16[64,1792]{1,0:T(8,128)(2,1)S(1)} collective-permute-done((bf16[64,1792]{1,0:T(8,128)(2,1)S(1)}, bf16[64,1792]{1,0:T(8,128)(2,1)S(1)}, u32[]{:S(2)}, u32[]{:S(2)}) %collective-permute-start.80) | collective-permute-done | bytes 229408 | tf_op jit(solution)/shard_map/ppermute | solution.py:67
  321.9 6.1 %collective-permute-done.88 = bf16[128,2560]{1,0:T(8,128)(2,1)S(1)} collective-permute-done((bf16[128,2560]{1,0:T(8,128)(2,1)S(1)}, bf16[128,2560]{1,0:T(8,128)(2,1)S(1)}, u32[]{:S(2)}, u32[]{:S(2)}) %collective-permute-start.88) | collective-permute-done | bytes 655392 | tf_op jit(solution)/shard_map/ppermute | solution.py:67
  328.1 2.0 collective-permute-done.89
  330.1 4.9 %convolution_convert_fusion.5 = bf16[512,1792]{1,0:T(8,128)(2,1)S(1)} fusion(bf16[2560,1792]{1,0:T(8,128)(2,1)S(1)} %bitcast.248, bf16[128,2560]{1,0:T(8,128)(2,1)S(1)} %collective-permute-done.89, bf16[128,2560]{1,0:T(8,128)(2,1)S(1)} %collective-permute-done.88, bf16[128,2560]{1,0:T(8,128)(2,1)S(1)} %collective-permute-done.87, ...), kind=kOutput, calls=%fused_computation.22 | convolution fusion | flops 4709023744 | bytes 13631488 | tf_op jit(solution)/shard_map/dot_general | solution.py:191
  346.7 3.8 %collective-permute-done.92 = bf16[64,1792]{1,0:T(8,128)(2,1)S(1)} collective-permute-done((bf16[64,1792]{1,0:T(8,128)(2,1)S(1)}, bf16[64,1792]{1,0:T(8,128)(2,1)S(1)}, u32[]{:S(2)}, u32[]{:S(2)}) %collective-permute-start.92) | collective-permute-done | bytes 229408 | tf_op jit(solution)/shard_map/ppermute | solution.py:67
  354.7 3.8 %collective-permute-done.94 = bf16[64,1792]{1,0:T(8,128)(2,1)S(1)} collective-permute-done((bf16[64,1792]{1,0:T(8,128)(2,1)S(1)}, bf16[64,1792]{1,0:T(8,128)(2,1)S(1)}, u32[]{:S(2)}, u32[]{:S(2)}) %collective-permute-start.94) | collective-permute-done | bytes 229408 | tf_op jit(solution)/shard_map/ppermute | solution.py:67
  363.7 2.8 collective-permute-done.96
  (394 shorter events, 126.6 us)
Async XLA Ops:
  0.6 13.9 %collective-permute-start.1 = (bf16[256,896]{1,0:T(8,128)(2,1)}, bf16[256,896]{1,0:T(8,128)(2,1)}, u32[]{:S(2)}, u32[]{:S(2)}) collective-permute-start(bf16[256,896]{1,0:T(8,128)(2,1)} %param.14), channel_id=1, source_target_pairs={{0,2},{2,0},{1,3},{3,1},{4,6},{6,4},{5,7},{7,5},{8,10},{10,8},{9,1... | collective-permute-start | bytes 1376264 | tf_op jit(solution)/shard_map/ppermute | solution.py:67
  3.7 12.7 %collective-permute-start = (bf16[256,896]{1,0:T(8,128)(2,1)}, bf16[256,896]{1,0:T(8,128)(2,1)}, u32[]{:S(2)}, u32[]{:S(2)}) collective-permute-start(bf16[256,896]{1,0:T(8,128)(2,1)} %param.14), channel_id=1, source_target_pairs={{0,1},{1,0},{2,3},{3,2},{4,5},{5,4},{6,7},{7,6},{8,9},{9,8},{10,11... | collective-permute-start | bytes 1376264 | tf_op jit(solution)/shard_map/ppermute | solution.py:219
  21.0 10.1 %collective-permute-start.3 = (bf16[64,512]{0,1:T(8,128)(2,1)S(1)}, bf16[64,512]{0,1:T(8,128)(2,1)S(1)}, u32[]{:S(2)}, u32[]{:S(2)}) collective-permute-start(bf16[64,512]{0,1:T(8,128)(2,1)S(1)} %get-tuple-element.87), channel_id=1, source_target_pairs={{0,8},{8,16},{16,24},{24,28},{28,20},{20,12},{12,4},{4,0},{1,9},{9... | collective-permute-start | bytes 196616 | tf_op jit(solution)/shard_map/ppermute | solution.py:67
  22.8 8.5 %collective-permute-start.4 = (bf16[64,512]{0,1:T(8,128)(2,1)S(1)}, bf16[64,512]{0,1:T(8,128)(2,1)S(1)}, u32[]{:S(2)}, u32[]{:S(2)}) collective-permute-start(bf16[64,512]{0,1:T(8,128)(2,1)S(1)} %get-tuple-element.88), channel_id=1, source_target_pairs={{8,0},{16,8},{24,16},{28,24},{20,28},{12,20},{4,12},{0,4},{9,1},{1... | collective-permute-start | bytes 196616 | tf_op jit(solution)/shard_map/ppermute | solution.py:67
  23.0 10.9 %collective-permute-start.11 = (f32[1024]{0:T(1024)S(1)}, f32[1024]{0:T(1024)S(1)}, u32[]{:S(2)}, u32[]{:S(2)}) collective-permute-start(f32[1024]{0:T(1024)S(1)} %get-tuple-element.95), channel_id=1, source_target_pairs={{0,4},{4,0},{8,12},{12,8},{16,20},{20,16},{24,28},{28,24},{1,5},{5... | collective-permute-start | bytes 12296 | tf_op jit(solution)/shard_map/ppermute | solution.py:314
  29.0 16.1 %collective-permute-start.22 = (bf16[64,1792]{1,0:T(8,128)(2,1)S(1)}, bf16[64,1792]{1,0:T(8,128)(2,1)S(1)}, u32[]{:S(2)}, u32[]{:S(2)}) collective-permute-start(bf16[64,1792]{1,0:T(8,128)(2,1)S(1)} %get-tuple-element.108), channel_id=1, source_target_pairs={{0,8},{8,16},{16,24},{24,28},{28,20},{20,12},{12,4},{4,0},{1,9},{9... | collective-permute-start | bytes 688136 | tf_op jit(solution)/shard_map/ppermute | solution.py:67
  30.6 14.4 %collective-permute-start.23 = (bf16[64,1792]{1,0:T(8,128)(2,1)S(1)}, bf16[64,1792]{1,0:T(8,128)(2,1)S(1)}, u32[]{:S(2)}, u32[]{:S(2)}) collective-permute-start(bf16[64,1792]{1,0:T(8,128)(2,1)S(1)} %get-tuple-element.109), channel_id=1, source_target_pairs={{8,0},{16,8},{24,16},{28,24},{20,28},{12,20},{4,12},{0,4},{9,1},{1... | collective-permute-start | bytes 688136 | tf_op jit(solution)/shard_map/ppermute | solution.py:67
  31.5 7.5 %collective-permute-start.5 = (bf16[128,512]{0,1:T(8,128)(2,1)S(1)}, bf16[128,512]{0,1:T(8,128)(2,1)S(1)}, u32[]{:S(2)}, u32[]{:S(2)}) collective-permute-start(bf16[128,512]{0,1:T(8,128)(2,1)S(1)} %pad_maximum_fusion.15), channel_id=1, source_target_pairs={{0,8},{8,16},{16,24},{24,28},{28,20},{20,12},{12,4},{4,0},{1,9},{9... | collective-permute-start | bytes 393224 | tf_op jit(solution)/shard_map/ppermute | solution.py:67
  33.1 7.2 %collective-permute-start.6 = (bf16[128,512]{0,1:T(8,128)(2,1)S(1)}, bf16[128,512]{0,1:T(8,128)(2,1)S(1)}, u32[]{:S(2)}, u32[]{:S(2)}) collective-permute-start(bf16[128,512]{0,1:T(8,128)(2,1)S(1)} %pad_maximum_fusion.16), channel_id=1, source_target_pairs={{8,0},{16,8},{24,16},{28,24},{20,28},{12,20},{4,12},{0,4},{9,1},{1... | collective-permute-start | bytes 393224 | tf_op jit(solution)/shard_map/ppermute | solution.py:67
  34.0 8.5 %collective-permute-start.12 = (f32[1024]{0:T(1024)S(1)}, f32[1024]{0:T(1024)S(1)}, u32[]{:S(2)}, u32[]{:S(2)}) collective-permute-start(f32[1024]{0:T(1024)S(1)} %add.389), channel_id=1, source_target_pairs={{0,8},{4,12},{8,0},{12,4},{16,24},{20,28},{24,16},{28,20},{1,9},{5... | collective-permute-start | bytes 12296 | tf_op jit(solution)/shard_map/ppermute | solution.py:314
  42.5 8.8 %collective-permute-start.13 = (f32[1024]{0:T(1024)S(1)}, f32[1024]{0:T(1024)S(1)}, u32[]{:S(2)}, u32[]{:S(2)}) collective-permute-start(f32[1024]{0:T(1024)S(1)} %add.390), channel_id=1, source_target_pairs={{0,16},{4,20},{8,24},{12,28},{16,0},{20,4},{24,8},{28,12},{1,17},{... | collective-permute-start | bytes 12296 | tf_op jit(solution)/shard_map/ppermute | solution.py:314
  47.0 6.5 %collective-permute-start.9 = (bf16[128,512]{0,1:T(8,128)(2,1)S(1)}, bf16[128,512]{0,1:T(8,128)(2,1)S(1)}, u32[]{:S(2)}, u32[]{:S(2)}) collective-permute-start(bf16[128,512]{0,1:T(8,128)(2,1)S(1)} %get-tuple-element.93), channel_id=1, source_target_pairs={{0,8},{8,16},{16,24},{24,28},{28,20},{20,12},{12,4},{4,0},{1,9},{9... | collective-permute-start | bytes 393224 | tf_op jit(solution)/shard_map/ppermute | solution.py:67
  48.7 6.4 %collective-permute-start.10 = (bf16[128,512]{0,1:T(8,128)(2,1)S(1)}, bf16[128,512]{0,1:T(8,128)(2,1)S(1)}, u32[]{:S(2)}, u32[]{:S(2)}) collective-permute-start(bf16[128,512]{0,1:T(8,128)(2,1)S(1)} %get-tuple-element.94), channel_id=1, source_target_pairs={{8,0},{16,8},{24,16},{28,24},{20,28},{12,20},{4,12},{0,4},{9,1},{1... | collective-permute-start | bytes 393224 | tf_op jit(solution)/shard_map/ppermute | solution.py:67
  49.2 17.9 %collective-permute-start.24 = (bf16[128,1792]{1,0:T(8,128)(2,1)S(1)}, bf16[128,1792]{1,0:T(8,128)(2,1)S(1)}, u32[]{:S(2)}, u32[]{:S(2)}) collective-permute-start(bf16[128,1792]{1,0:T(8,128)(2,1)S(1)} %get-tuple-element.110), channel_id=1, source_target_pairs={{0,8},{8,16},{16,24},{24,28},{28,20},{20,12},{12,4},{4,0},{1,9},{9... | collective-permute-start | bytes 1376264 | tf_op jit(solution)/shard_map/ppermute | solution.py:67
  50.9 16.2 %collective-permute-start.25 = (bf16[128,1792]{1,0:T(8,128)(2,1)S(1)}, bf16[128,1792]{1,0:T(8,128)(2,1)S(1)}, u32[]{:S(2)}, u32[]{:S(2)}) collective-permute-start(bf16[128,1792]{1,0:T(8,128)(2,1)S(1)} %get-tuple-element.111), channel_id=1, source_target_pairs={{8,0},{16,8},{24,16},{28,24},{20,28},{12,20},{4,12},{0,4},{9,1},{1... | collective-permute-start | bytes 1376264 | tf_op jit(solution)/shard_map/ppermute | solution.py:67
  55.3 9.7 %collective-permute-start.14 = (bf16[128,512]{0,1:T(8,128)(2,1)S(1)}, bf16[128,512]{0,1:T(8,128)(2,1)S(1)}, u32[]{:S(2)}, u32[]{:S(2)}) collective-permute-start(bf16[128,512]{0,1:T(8,128)(2,1)S(1)} %pad_maximum_fusion.17), channel_id=1, source_target_pairs={{8,0},{16,8},{24,16},{28,24},{20,28},{12,20},{4,12},{0,4},{9,1},{1... | collective-permute-start | bytes 393224 | tf_op jit(solution)/shard_map/ppermute | solution.py:67
  55.8 9.2 %collective-permute-start.15 = (bf16[128,512]{0,1:T(8,128)(2,1)S(1)}, bf16[128,512]{0,1:T(8,128)(2,1)S(1)}, u32[]{:S(2)}, u32[]{:S(2)}) collective-permute-start(bf16[128,512]{0,1:T(8,128)(2,1)S(1)} %pad_maximum_fusion.17), channel_id=1, source_target_pairs={{0,8},{8,16},{16,24},{24,28},{28,20},{20,12},{12,4},{4,0},{1,9},{9... | collective-permute-start | bytes 393224 | tf_op jit(solution)/shard_map/ppermute | solution.py:67
  65.0 6.5 %collective-permute-start.16 = (bf16[128,512]{0,1:T(8,128)(2,1)S(1)}, bf16[128,512]{0,1:T(8,128)(2,1)S(1)}, u32[]{:S(2)}, u32[]{:S(2)}) collective-permute-start(bf16[128,512]{0,1:T(8,128)(2,1)S(1)} %collective-permute-done.14), channel_id=1, source_target_pairs={{8,0},{16,8},{24,16},{28,24},{20,28},{12,20},{4,12},{0,4},{9,1},{1... | collective-permute-start | bytes 393224 | tf_op jit(solution)/shard_map/ppermute | solution.py:67
  65.4 6.4 %collective-permute-start.17 = (bf16[128,512]{0,1:T(8,128)(2,1)S(1)}, bf16[128,512]{0,1:T(8,128)(2,1)S(1)}, u32[]{:S(2)}, u32[]{:S(2)}) collective-permute-start(bf16[128,512]{0,1:T(8,128)(2,1)S(1)} %collective-permute-done.15), channel_id=1, source_target_pairs={{0,8},{8,16},{16,24},{24,28},{28,20},{20,12},{12,4},{4,0},{1,9},{9... | collective-permute-start | bytes 393224 | tf_op jit(solution)/shard_map/ppermute | solution.py:67
  67.3 16.1 %collective-permute-start.26 = (bf16[128,1792]{1,0:T(8,128)(2,1)S(1)}, bf16[128,1792]{1,0:T(8,128)(2,1)S(1)}, u32[]{:S(2)}, u32[]{:S(2)}) collective-permute-start(bf16[128,1792]{1,0:T(8,128)(2,1)S(1)} %get-tuple-element.112), channel_id=1, source_target_pairs={{0,8},{8,16},{16,24},{24,28},{28,20},{20,12},{12,4},{4,0},{1,9},{9... | collective-permute-start | bytes 1376264 | tf_op jit(solution)/shard_map/ppermute | solution.py:67
  67.5 15.8 %collective-permute-start.27 = (bf16[128,1792]{1,0:T(8,128)(2,1)S(1)}, bf16[128,1792]{1,0:T(8,128)(2,1)S(1)}, u32[]{:S(2)}, u32[]{:S(2)}) collective-permute-start(bf16[128,1792]{1,0:T(8,128)(2,1)S(1)} %get-tuple-element.113), channel_id=1, source_target_pairs={{8,0},{16,8},{24,16},{28,24},{20,28},{12,20},{4,12},{0,4},{9,1},{1... | collective-permute-start | bytes 1376264 | tf_op jit(solution)/shard_map/ppermute | solution.py:67
  71.9 9.3 %collective-permute-start.18 = (bf16[128,512]{0,1:T(8,128)(2,1)S(1)}, bf16[128,512]{0,1:T(8,128)(2,1)S(1)}, u32[]{:S(2)}, u32[]{:S(2)}) collective-permute-start(bf16[128,512]{0,1:T(8,128)(2,1)S(1)} %collective-permute-done.16), channel_id=1, source_target_pairs={{8,0},{16,8},{24,16},{28,24},{20,28},{12,20},{4,12},{0,4},{9,1},{1... | collective-permute-start | bytes 393224 | tf_op jit(solution)/shard_map/ppermute | solution.py:67
  72.4 8.8 %collective-permute-start.19 = (bf16[128,512]{0,1:T(8,128)(2,1)S(1)}, bf16[128,512]{0,1:T(8,128)(2,1)S(1)}, u32[]{:S(2)}, u32[]{:S(2)}) collective-permute-start(bf16[128,512]{0,1:T(8,128)(2,1)S(1)} %collective-permute-done.17), channel_id=1, source_target_pairs={{0,8},{8,16},{16,24},{24,28},{28,20},{20,12},{12,4},{4,0},{1,9},{9... | collective-permute-start | bytes 393224 | tf_op jit(solution)/shard_map/ppermute | solution.py:67
  84.4 8.7 %collective-permute-start.28 = (bf16[128,1792]{1,0:T(8,128)(2,1)}, bf16[128,1792]{1,0:T(8,128)(2,1)S(1)}, u32[]{:S(2)}, u32[]{:S(2)}) collective-permute-start(bf16[128,1792]{1,0:T(8,128)(2,1)} %get-tuple-element.114), channel_id=1, source_target_pairs={{0,8},{8,16},{16,24},{24,28},{28,20},{20,12},{12,4},{4,0},{1,9},{9... | collective-permute-start | bytes 1376264 | tf_op jit(solution)/shard_map/ppermute | solution.py:67
  84.8 9.0 %collective-permute-start.29 = (bf16[128,1792]{1,0:T(8,128)(2,1)S(1)}, bf16[128,1792]{1,0:T(8,128)(2,1)}, u32[]{:S(2)}, u32[]{:S(2)}) collective-permute-start(bf16[128,1792]{1,0:T(8,128)(2,1)S(1)} %get-tuple-element.115), channel_id=1, source_target_pairs={{8,0},{16,8},{24,16},{28,24},{20,28},{12,20},{4,12},{0,4},{9,1},{1... | collective-permute-start | bytes 1376264 | tf_op jit(solution)/shard_map/ppermute | solution.py:67
  101.4 7.9 %collective-permute-start.30 = (bf16[64,1792]{1,0:T(8,128)(2,1)S(1)}, bf16[64,1792]{1,0:T(8,128)(2,1)}, u32[]{:S(2)}, u32[]{:S(2)}) collective-permute-start(bf16[64,1792]{1,0:T(8,128)(2,1)S(1)} %convert_element_type.523), channel_id=1, source_target_pairs={{0,8},{8,16},{16,24},{24,28},{28,20},{20,12},{12,4},{4,0},{1,9},{9... | collective-permute-start | bytes 688136 | tf_op jit(solution)/shard_map/ppermute | solution.py:67
  102.0 7.7 %collective-permute-start.31 = (bf16[64,1792]{1,0:T(8,128)(2,1)S(1)}, bf16[64,1792]{1,0:T(8,128)(2,1)}, u32[]{:S(2)}, u32[]{:S(2)}) collective-permute-start(bf16[64,1792]{1,0:T(8,128)(2,1)S(1)} %convert_element_type.523), channel_id=1, source_target_pairs={{8,0},{16,8},{24,16},{28,24},{20,28},{12,20},{4,12},{0,4},{9,1},{1... | collective-permute-start | bytes 688136 | tf_op jit(solution)/shard_map/ppermute | solution.py:67
  109.6 8.8 %collective-permute-start.32 = (bf16[64,1792]{1,0:T(8,128)(2,1)}, bf16[64,1792]{1,0:T(8,128)(2,1)S(1)}, u32[]{:S(2)}, u32[]{:S(2)}) collective-permute-start(bf16[64,1792]{1,0:T(8,128)(2,1)} %collective-permute-done.30), channel_id=1, source_target_pairs={{0,8},{8,16},{16,24},{24,28},{28,20},{20,12},{12,4},{4,0},{1,9},{9... | collective-permute-start | bytes 688136 | tf_op jit(solution)/shard_map/ppermute | solution.py:67
  110.2 10.2 %collective-permute-start.33 = (bf16[64,1792]{1,0:T(8,128)(2,1)}, bf16[64,1792]{1,0:T(8,128)(2,1)S(1)}, u32[]{:S(2)}, u32[]{:S(2)}) collective-permute-start(bf16[64,1792]{1,0:T(8,128)(2,1)} %collective-permute-done.31), channel_id=1, source_target_pairs={{8,0},{16,8},{24,16},{28,24},{20,28},{12,20},{4,12},{0,4},{9,1},{1... | collective-permute-start | bytes 688136 | tf_op jit(solution)/shard_map/ppermute | solution.py:67
  118.4 7.2 %collective-permute-start.57 = (bf16[64,1792]{1,0:T(8,128)(2,1)S(1)}, bf16[64,1792]{1,0:T(8,128)(2,1)S(1)}, u32[]{:S(2)}, u32[]{:S(2)}) collective-permute-start(bf16[64,1792]{1,0:T(8,128)(2,1)S(1)} %convert_element_type.527), channel_id=1, source_target_pairs={{0,8},{8,16},{16,24},{24,28},{28,20},{20,12},{12,4},{4,0},{1,9},{9... | collective-permute-start | bytes 688136 | tf_op jit(solution)/shard_map/ppermute | solution.py:67
  119.0 6.6 %collective-permute-start.58 = (bf16[64,1792]{1,0:T(8,128)(2,1)S(1)}, bf16[64,1792]{1,0:T(8,128)(2,1)S(1)}, u32[]{:S(2)}, u32[]{:S(2)}) collective-permute-start(bf16[64,1792]{1,0:T(8,128)(2,1)S(1)} %convert_element_type.527), channel_id=1, source_target_pairs={{8,0},{16,8},{24,16},{28,24},{20,28},{12,20},{4,12},{0,4},{9,1},{1... | collective-permute-start | bytes 688136 | tf_op jit(solution)/shard_map/ppermute | solution.py:67
  120.4 7.7 %collective-permute-start.34 = (bf16[64,1792]{1,0:T(8,128)(2,1)S(1)}, bf16[64,1792]{1,0:T(8,128)(2,1)S(1)}, u32[]{:S(2)}, u32[]{:S(2)}) collective-permute-start(bf16[64,1792]{1,0:T(8,128)(2,1)S(1)} %collective-permute-done.32), channel_id=1, source_target_pairs={{0,8},{8,16},{16,24},{24,28},{28,20},{20,12},{12,4},{4,0},{1,9},{9... | collective-permute-start | bytes 688136 | tf_op jit(solution)/shard_map/ppermute | solution.py:67
  121.0 7.1 %collective-permute-start.35 = (bf16[64,1792]{1,0:T(8,128)(2,1)S(1)}, bf16[64,1792]{1,0:T(8,128)(2,1)S(1)}, u32[]{:S(2)}, u32[]{:S(2)}) collective-permute-start(bf16[64,1792]{1,0:T(8,128)(2,1)S(1)} %collective-permute-done.33), channel_id=1, source_target_pairs={{8,0},{16,8},{24,16},{28,24},{20,28},{12,20},{4,12},{0,4},{9,1},{1... | collective-permute-start | bytes 688136 | tf_op jit(solution)/shard_map/ppermute | solution.py:67
  125.6 11.0 %collective-permute-start.59 = (bf16[64,1792]{1,0:T(8,128)(2,1)S(1)}, bf16[64,1792]{1,0:T(8,128)(2,1)S(1)}, u32[]{:S(2)}, u32[]{:S(2)}) collective-permute-start(bf16[64,1792]{1,0:T(8,128)(2,1)S(1)} %collective-permute-done.57), channel_id=1, source_target_pairs={{0,8},{8,16},{16,24},{24,28},{28,20},{20,12},{12,4},{4,0},{1,9},{9... | collective-permute-start | bytes 688136 | tf_op jit(solution)/shard_map/ppermute | solution.py:67
  126.3 10.4 %collective-permute-start.60 = (bf16[64,1792]{1,0:T(8,128)(2,1)S(1)}, bf16[64,1792]{1,0:T(8,128)(2,1)S(1)}, u32[]{:S(2)}, u32[]{:S(2)}) collective-permute-start(bf16[64,1792]{1,0:T(8,128)(2,1)S(1)} %collective-permute-done.58), channel_id=1, source_target_pairs={{8,0},{16,8},{24,16},{28,24},{20,28},{12,20},{4,12},{0,4},{9,1},{1... | collective-permute-start | bytes 688136 | tf_op jit(solution)/shard_map/ppermute | solution.py:67
  136.6 8.4 %collective-permute-start.38 = (bf16[2,128,896]{2,1,0:T(8,128)(2,1)S(1)}, bf16[2,128,896]{2,1,0:T(8,128)(2,1)S(1)}, u32[]{:S(2)}, u32[]{:S(2)}) collective-permute-start(bf16[2,128,896]{2,1,0:T(8,128)(2,1)S(1)} %slice_bitcast_fusion.17), channel_id=1, source_target_pairs={{0,1},{1,0},{2,3},{3,2},{4,5},{5,4},{6,7},{7,6},{8,9},{9,8},{10,11... | collective-permute-start | bytes 1376264 | tf_op jit(solution)/shard_map/ppermute | solution.py:219
  136.7 8.0 %collective-permute-start.61 = (bf16[64,1792]{1,0:T(8,128)(2,1)S(1)}, bf16[64,1792]{1,0:T(8,128)(2,1)S(1)}, u32[]{:S(2)}, u32[]{:S(2)}) collective-permute-start(bf16[64,1792]{1,0:T(8,128)(2,1)S(1)} %collective-permute-done.59), channel_id=1, source_target_pairs={{0,8},{8,16},{16,24},{24,28},{28,20},{20,12},{12,4},{4,0},{1,9},{9... | collective-permute-start | bytes 688136 | tf_op jit(solution)/shard_map/ppermute | solution.py:67
  137.3 7.7 %collective-permute-start.62 = (bf16[64,1792]{1,0:T(8,128)(2,1)S(1)}, bf16[64,1792]{1,0:T(8,128)(2,1)S(1)}, u32[]{:S(2)}, u32[]{:S(2)}) collective-permute-start(bf16[64,1792]{1,0:T(8,128)(2,1)S(1)} %collective-permute-done.60), channel_id=1, source_target_pairs={{8,0},{16,8},{24,16},{28,24},{20,28},{12,20},{4,12},{0,4},{9,1},{1... | collective-permute-start | bytes 688136 | tf_op jit(solution)/shard_map/ppermute | solution.py:67
  157.0 8.1 %collective-permute-start.65 = (bf16[2,128,896]{2,1,0:T(8,128)(2,1)S(1)}, bf16[2,128,896]{2,1,0:T(8,128)(2,1)S(1)}, u32[]{:S(2)}, u32[]{:S(2)}) collective-permute-start(bf16[2,128,896]{2,1,0:T(8,128)(2,1)S(1)} %slice_bitcast_fusion.15), channel_id=1, source_target_pairs={{0,1},{1,0},{2,3},{3,2},{4,5},{5,4},{6,7},{7,6},{8,9},{9,8},{10,11... | collective-permute-start | bytes 1376264 | tf_op jit(solution)/shard_map/ppermute | solution.py:219
  161.7 7.4 %collective-permute-start.42 = (bf16[128,896]{1,0:T(8,128)(2,1)S(1)}, bf16[128,896]{1,0:T(8,128)(2,1)S(1)}, u32[]{:S(2)}, u32[]{:S(2)}) collective-permute-start(bf16[128,896]{1,0:T(8,128)(2,1)S(1)} %collective-permute-done.40), channel_id=1, source_target_pairs={{0,8},{8,16},{16,24},{24,28},{28,20},{20,12},{12,4},{4,0},{1,9},{9... | collective-permute-start | bytes 688136 | tf_op jit(solution)/shard_map/ppermute | solution.py:67
  162.7 6.9 %collective-permute-start.43 = (bf16[128,896]{1,0:T(8,128)(2,1)}, bf16[128,896]{1,0:T(8,128)(2,1)S(1)}, u32[]{:S(2)}, u32[]{:S(2)}) collective-permute-start(bf16[128,896]{1,0:T(8,128)(2,1)} %collective-permute-done.41), channel_id=1, source_target_pairs={{8,0},{16,8},{24,16},{28,24},{20,28},{12,20},{4,12},{0,4},{9,1},{1... | collective-permute-start | bytes 688136 | tf_op jit(solution)/shard_map/ppermute | solution.py:67
  169.6 6.7 %collective-permute-start.44 = (bf16[128,896]{1,0:T(8,128)(2,1)S(1)}, bf16[128,896]{1,0:T(8,128)(2,1)S(1)}, u32[]{:S(2)}, u32[]{:S(2)}) collective-permute-start(bf16[128,896]{1,0:T(8,128)(2,1)S(1)} %collective-permute-done.42), channel_id=1, source_target_pairs={{0,8},{8,16},{16,24},{24,28},{28,20},{20,12},{12,4},{4,0},{1,9},{9... | collective-permute-start | bytes 688136 | tf_op jit(solution)/shard_map/ppermute | solution.py:67
  171.3 7.7 %collective-permute-start.45 = (bf16[128,896]{1,0:T(8,128)(2,1)S(1)}, bf16[128,896]{1,0:T(8,128)(2,1)S(1)}, u32[]{:S(2)}, u32[]{:S(2)}) collective-permute-start(bf16[128,896]{1,0:T(8,128)(2,1)S(1)} %collective-permute-done.43), channel_id=1, source_target_pairs={{8,0},{16,8},{24,16},{28,24},{20,28},{12,20},{4,12},{0,4},{9,1},{1... | collective-permute-start | bytes 688136 | tf_op jit(solution)/shard_map/ppermute | solution.py:67
  172.5 14.8 %collective-permute-start.67 = (bf16[128,896]{1,0:T(8,128)(2,1)S(1)}, bf16[128,896]{1,0:T(8,128)(2,1)S(1)}, u32[]{:S(2)}, u32[]{:S(2)}) collective-permute-start(bf16[128,896]{1,0:T(8,128)(2,1)S(1)} %fusion.45), channel_id=1, source_target_pairs={{0,8},{4,12},{8,16},{12,20},{16,24},{20,28},{24,0},{28,4},{1,9},{5... | collective-permute-start | bytes 688136 | tf_op jit(solution)/shard_map/ppermute | solution.py:402
  185.1 15.2 %collective-permute-start.49 = (bf16[128,3584]{1,0:T(8,128)(2,1)S(1)}, bf16[128,3584]{1,0:T(8,128)(2,1)S(1)}, u32[]{:S(2)}, u32[]{:S(2)}) collective-permute-start(bf16[128,3584]{1,0:T(8,128)(2,1)S(1)} %constant_dynamic-slice_fusion.8), channel_id=1, source_target_pairs={{0,2},{1,3},{2,0},{3,1},{4,6},{5,7},{6,4},{7,5},{8,10},{9,11},{10,... | collective-permute-start | bytes 2752520 | tf_op jit(solution)/shard_map/ppermute | solution.py:387
  187.3 7.9 %collective-permute-start.68 = (bf16[128,896]{1,0:T(8,128)(2,1)S(1)}, bf16[128,896]{1,0:T(8,128)(2,1)S(1)}, u32[]{:S(2)}, u32[]{:S(2)}) collective-permute-start(bf16[128,896]{1,0:T(8,128)(2,1)S(1)} %collective-permute-done.67), channel_id=1, source_target_pairs={{0,8},{4,12},{8,16},{12,20},{16,24},{20,28},{24,0},{28,4},{1,9},{5... | collective-permute-start | bytes 688136 | tf_op jit(solution)/shard_map/ppermute | solution.py:402
  188.9 19.3 %collective-permute-start.48 = (bf16[128,1792]{1,0:T(8,128)(2,1)S(1)}, bf16[128,1792]{1,0:T(8,128)(2,1)S(1)}, u32[]{:S(2)}, u32[]{:S(2)}) collective-permute-start(bf16[128,1792]{1,0:T(8,128)(2,1)S(1)} %get-tuple-element.201), channel_id=1, source_target_pairs={{0,1},{1,0},{2,3},{3,2},{4,5},{5,4},{6,7},{7,6},{8,9},{9,8},{10,11... | collective-permute-start | bytes 1376264 | tf_op jit(solution)/shard_map/ppermute | solution.py:219
  200.2 7.8 %collective-permute-start.69 = (bf16[128,896]{1,0:T(8,128)(2,1)S(1)}, bf16[128,896]{1,0:T(8,128)(2,1)S(1)}, u32[]{:S(2)}, u32[]{:S(2)}) collective-permute-start(bf16[128,896]{1,0:T(8,128)(2,1)S(1)} %collective-permute-done.68), channel_id=1, source_target_pairs={{0,8},{4,12},{8,16},{12,20},{16,24},{20,28},{24,0},{28,4},{1,9},{5... | collective-permute-start | bytes 688136 | tf_op jit(solution)/shard_map/ppermute | solution.py:402
  201.0 7.3 %collective-permute-start.50 = (bf16[128,1792]{1,0:T(8,128)(2,1)S(1)}, bf16[128,1792]{1,0:T(8,128)(2,1)S(1)}, u32[]{:S(2)}, u32[]{:S(2)}) collective-permute-start(bf16[128,1792]{1,0:T(8,128)(2,1)S(1)} %get-tuple-element.218), channel_id=1, source_target_pairs={{0,1},{1,0},{2,3},{3,2},{4,5},{5,4},{6,7},{7,6},{8,9},{9,8},{10,11... | collective-permute-start | bytes 1376264 | tf_op jit(solution)/shard_map/ppermute | solution.py:219
  218.5 8.5 %collective-permute-start.70 = (bf16[256,896]{1,0:T(8,128)(2,1)S(1)}, bf16[256,896]{1,0:T(8,128)(2,1)S(1)}, u32[]{:S(2)}, u32[]{:S(2)}) collective-permute-start(bf16[256,896]{1,0:T(8,128)(2,1)S(1)} %pad_maximum_fusion.8), channel_id=1, source_target_pairs={{0,2},{1,3},{2,0},{3,1},{4,6},{5,7},{6,4},{7,5},{8,10},{9,11},{10,... | collective-permute-start | bytes 1376264 | tf_op jit(solution)/shard_map/ppermute | solution.py:411
  229.2 22.5 %collective-permute-start.72 = (bf16[512,896]{1,0:T(8,128)(2,1)S(1)}, bf16[512,896]{1,0:T(8,128)(2,1)S(1)}, u32[]{:S(2)}, u32[]{:S(2)}) collective-permute-start(bf16[512,896]{1,0:T(8,128)(2,1)S(1)} %pad_maximum_fusion.4), channel_id=1, source_target_pairs={{0,4},{4,0},{8,12},{12,8},{16,20},{20,16},{24,28},{28,24},{1,5},{5... | collective-permute-start | bytes 2752520 | tf_op jit(solution)/shard_map/ppermute | solution.py:475
  231.2 22.1 %collective-permute-start.52 = (bf16[128,2560]{1,0:T(8,128)(2,1)S(1)}, bf16[128,2560]{1,0:T(8,128)(2,1)S(1)}, u32[]{:S(2)}, u32[]{:S(2)}) collective-permute-start(bf16[128,2560]{1,0:T(8,128)(2,1)S(1)} %slice_bitcast_fusion.12), channel_id=1, source_target_pairs={{0,2},{2,0},{1,3},{3,1},{4,6},{6,4},{5,7},{7,5},{8,10},{10,8},{9,1... | collective-permute-start | bytes 1966088 | tf_op jit(solution)/shard_map/ppermute | solution.py:67
  233.1 28.7 %collective-permute-start.54 = (bf16[128,2560]{1,0:T(8,128)(2,1)S(1)}, bf16[128,2560]{1,0:T(8,128)(2,1)S(1)}, u32[]{:S(2)}, u32[]{:S(2)}) collective-permute-start(bf16[128,2560]{1,0:T(8,128)(2,1)S(1)} %slice_bitcast_fusion.10), channel_id=1, source_target_pairs={{0,2},{2,0},{1,3},{3,1},{4,6},{6,4},{5,7},{7,5},{8,10},{10,8},{9,1... | collective-permute-start | bytes 1966088 | tf_op jit(solution)/shard_map/ppermute | solution.py:67
  262.4 15.7 %collective-permute-start.56 = (bf16[128,2560]{1,0:T(8,128)(2,1)S(1)}, bf16[128,2560]{1,0:T(8,128)(2,1)S(1)}, u32[]{:S(2)}, u32[]{:S(2)}) collective-permute-start(bf16[128,2560]{1,0:T(8,128)(2,1)S(1)} %fusion.36), channel_id=1, source_target_pairs={{0,2},{2,0},{1,3},{3,1},{4,6},{6,4},{5,7},{7,5},{8,10},{10,8},{9,1... | collective-permute-start | bytes 1966088 | tf_op jit(solution)/shard_map/ppermute | solution.py:67
  264.0 16.6 %collective-permute-start.55 = (bf16[128,2560]{1,0:T(8,128)(2,1)S(1)}, bf16[128,2560]{1,0:T(8,128)(2,1)}, u32[]{:S(2)}, u32[]{:S(2)}) collective-permute-start(bf16[128,2560]{1,0:T(8,128)(2,1)S(1)} %fusion.36), channel_id=1, source_target_pairs={{0,1},{1,0},{2,3},{3,2},{4,5},{5,4},{6,7},{7,6},{8,9},{9,8},{10,11... | collective-permute-start | bytes 1966088 | tf_op jit(solution)/shard_map/ppermute | solution.py:219
  269.5 8.6 %collective-permute-start.85 = (bf16[2,128,2560]{2,1,0:T(8,128)(2,1)S(1)}, bf16[2,128,2560]{2,1,0:T(8,128)(2,1)S(1)}, u32[]{:S(2)}, u32[]{:S(2)}) collective-permute-start(bf16[2,128,2560]{2,1,0:T(8,128)(2,1)S(1)} %slice_bitcast_fusion), channel_id=1, source_target_pairs={{0,1},{1,0},{2,3},{3,2},{4,5},{5,4},{6,7},{7,6},{8,9},{9,8},{10,11... | collective-permute-start | bytes 3932168 | tf_op jit(solution)/shard_map/ppermute | solution.py:219
  275.5 16.6 %collective-permute-start.82 = (bf16[2,128,2560]{2,1,0:T(8,128)(2,1)S(1)}, bf16[2,128,2560]{2,1,0:T(8,128)(2,1)S(1)}, u32[]{:S(2)}, u32[]{:S(2)}) collective-permute-start(bf16[2,128,2560]{2,1,0:T(8,128)(2,1)S(1)} %slice_bitcast_fusion.2), channel_id=1, source_target_pairs={{0,1},{1,0},{2,3},{3,2},{4,5},{5,4},{6,7},{7,6},{8,9},{9,8},{10,11... | collective-permute-start | bytes 3932168 | tf_op jit(solution)/shard_map/ppermute | solution.py:219
  279.0 31.0 %collective-permute-start.86 = (bf16[128,2560]{1,0:T(8,128)(2,1)S(1)}, bf16[128,2560]{1,0:T(8,128)(2,1)S(1)}, u32[]{:S(2)}, u32[]{:S(2)}) collective-permute-start(bf16[128,2560]{1,0:T(8,128)(2,1)S(1)} %slice_bitcast_fusion.14), channel_id=1, source_target_pairs={{0,2},{2,0},{1,3},{3,1},{4,6},{6,4},{5,7},{7,5},{8,10},{10,8},{9,1... | collective-permute-start | bytes 1966088 | tf_op jit(solution)/shard_map/ppermute | solution.py:67
  295.4 6.8 %collective-permute-start.76 = (bf16[64,1792]{1,0:T(8,128)(2,1)S(1)}, bf16[64,1792]{1,0:T(8,128)(2,1)S(1)}, u32[]{:S(2)}, u32[]{:S(2)}) collective-permute-start(bf16[64,1792]{1,0:T(8,128)(2,1)S(1)} %pad_maximum_fusion.11), channel_id=1, source_target_pairs={{0,8},{8,16},{16,24},{24,28},{28,20},{20,12},{12,4},{4,0},{1,9},{9... | collective-permute-start | bytes 688136 | tf_op jit(solution)/shard_map/ppermute | solution.py:67
  296.0 6.4 %collective-permute-start.77 = (bf16[64,1792]{1,0:T(8,128)(2,1)S(1)}, bf16[64,1792]{1,0:T(8,128)(2,1)S(1)}, u32[]{:S(2)}, u32[]{:S(2)}) collective-permute-start(bf16[64,1792]{1,0:T(8,128)(2,1)S(1)} %pad_maximum_fusion.12), channel_id=1, source_target_pairs={{8,0},{16,8},{24,16},{28,24},{20,28},{12,20},{4,12},{0,4},{9,1},{1... | collective-permute-start | bytes 688136 | tf_op jit(solution)/shard_map/ppermute | solution.py:67
  297.5 15.4 %collective-permute-start.83 = (bf16[128,2560]{1,0:T(8,128)(2,1)S(1)}, bf16[128,2560]{1,0:T(8,128)(2,1)S(1)}, u32[]{:S(2)}, u32[]{:S(2)}) collective-permute-start(bf16[128,2560]{1,0:T(8,128)(2,1)S(1)} %slice_bitcast_fusion.8), channel_id=1, source_target_pairs={{0,2},{2,0},{1,3},{3,1},{4,6},{6,4},{5,7},{7,5},{8,10},{10,8},{9,1... | collective-permute-start | bytes 1966088 | tf_op jit(solution)/shard_map/ppermute | solution.py:67
  313.5 14.5 %collective-permute-start.88 = (bf16[128,2560]{1,0:T(8,128)(2,1)S(1)}, bf16[128,2560]{1,0:T(8,128)(2,1)S(1)}, u32[]{:S(2)}, u32[]{:S(2)}) collective-permute-start(bf16[128,2560]{1,0:T(8,128)(2,1)S(1)} %fusion.32), channel_id=1, source_target_pairs={{0,2},{2,0},{1,3},{3,1},{4,6},{6,4},{5,7},{7,5},{8,10},{10,8},{9,1... | collective-permute-start | bytes 1966088 | tf_op jit(solution)/shard_map/ppermute | solution.py:67
  317.4 10.7 %collective-permute-start.87 = (bf16[128,2560]{1,0:T(8,128)(2,1)S(1)}, bf16[128,2560]{1,0:T(8,128)(2,1)S(1)}, u32[]{:S(2)}, u32[]{:S(2)}) collective-permute-start(bf16[128,2560]{1,0:T(8,128)(2,1)S(1)} %fusion.32), channel_id=1, source_target_pairs={{0,1},{1,0},{2,3},{3,2},{4,5},{5,4},{6,7},{7,6},{8,9},{9,8},{10,11... | collective-permute-start | bytes 1966088 | tf_op jit(solution)/shard_map/ppermute | solution.py:219
  343.9 6.6 %collective-permute-start.92 = (bf16[64,1792]{1,0:T(8,128)(2,1)S(1)}, bf16[64,1792]{1,0:T(8,128)(2,1)S(1)}, u32[]{:S(2)}, u32[]{:S(2)}) collective-permute-start(bf16[64,1792]{1,0:T(8,128)(2,1)S(1)} %pad_maximum_fusion.13), channel_id=1, source_target_pairs={{0,8},{8,16},{16,24},{24,28},{28,20},{20,12},{12,4},{4,0},{1,9},{9... | collective-permute-start | bytes 688136 | tf_op jit(solution)/shard_map/ppermute | solution.py:67
  (80 other events, 752.6 us)
